TPU v7x, 32 devices: a whole 2x2x4 slice. The times are simulated.
32 devices in a mesh: chan: 8 (over z, x), row: 4 (over y, core).
Axes of the slice: x: 2, y: 2, z: 4, core: 2. Of those that a mesh axis runs over, the one named last changes fastest.
Arguments:
- amplitudes: bfloat16 [2048, 8, 640], P('row', 'chan'), may hold values from -6 to 6
- block_rows: int32 [8], P('chan'), may hold values from 256 to 2048, as said below
- recoupling: bfloat16 [8, 8], replicated, may hold values from -1 to 2
- interaction: bfloat16 [2048, 8, 2048], P(None, 'chan', 'row'), may hold values from -0.125 to 0.125
Outputs:
- residual: bfloat16 [2048, 8, 640], P('row', 'chan')
Inputs may be any that keep to these rules, and one draw needn't show every extreme that they name: `block_rows`: each entry is at least 256 and at most 2048; some channel has exactly 2048 live rows.
All inputs are finite; a program needn't handle non-finite values.
Results may differ from a plain program's by a relative error of at most 0.015.
Values may be sent and summed in bfloat16 or wider, within the bound.
No kernel may reach another device: no remote copies, remote signals or barrier semaphores. Data moves between devices by JAX's collectives and lax.ppermute only.
A program may use at most 64 MiB of HBM per device.

v0:
```python
import jax
import jax.numpy as jnp
from jax import lax
from jax.sharding import PartitionSpec as P


def on_device(amplitudes, block_rows, recoupling, interaction):
    rows_here = amplitudes.shape[0]
    offset = lax.axis_index("row") * rows_here
    local_rows = offset + lax.iota(jnp.int32, rows_here)
    row_valid_mask = (local_rows[:, None] < block_rows[None, :])[:, :, None]
    zero = jnp.zeros((), jnp.bfloat16)
    masked = jnp.where(row_valid_mask, amplitudes, zero)
    spread = lax.all_to_all(masked, "chan", split_axis=0, concat_axis=1, tiled=True)
    mixed_rows = jnp.einsum(
        "kj,rjq->rkq", recoupling, spread, preferred_element_type=jnp.float32
    ).astype(jnp.bfloat16)
    crossing_row_set = lax.all_to_all(mixed_rows, "chan", split_axis=1, concat_axis=0, tiled=True)
    partials = jnp.einsum(
        "zmo,omu->zmu", interaction, crossing_row_set, preferred_element_type=jnp.float32
    )
    full_terms = partials.astype(jnp.bfloat16).astype(jnp.float32)
    reduced_total = lax.psum(full_terms.astype(jnp.bfloat16), "row").astype(jnp.float32)
    own_rows = lax.dynamic_slice_in_dim(reduced_total, offset, rows_here, 0)
    summed_rows = own_rows.astype(jnp.bfloat16)
    back_spread = lax.all_to_all(summed_rows, "chan", split_axis=0, concat_axis=1, tiled=True)
    unmixed = jnp.einsum(
        "jk,rjq->rkq", recoupling, back_spread, preferred_element_type=jnp.float32
    ).astype(jnp.bfloat16)
    back_rows = lax.all_to_all(unmixed, "chan", split_axis=1, concat_axis=0, tiled=True)
    return jnp.where(row_valid_mask, back_rows, zero)


def solution(mesh):
    return jax.shard_map(
        on_device,
        mesh=mesh,
        in_specs=(P("row", "chan", None), P("chan"), P(), P(None, "chan", "row")),
        out_specs=P("row", "chan", None),
        check_vma=False,
    )
```

profile of v0, /device:TPU:0, one launch (start us, length us, event | category | flops | bytes accessed | tf_op | source)
XLA Modules:
  0.0 177.9 jit_solution(16956620607784500751)
XLA Ops:
  6.5 0.0 copy-start
  6.5 0.0 all-reduce.2.cloned.1.call-start
  7.4 1.2 broadcast_select_fusion
  8.6 0.5 broadcast.37
  9.1 1.1 reduce
  10.2 0.2 reshape.56
  10.4 24.9 %all_to_all.69 = bf16[8,2,20480]{2,1,0:T(2,128)(2,1)} all-to-all(bf16[8,2,20480]{2,1,0:T(2,128)(2,1)S(1)} %reshape.56), channel_id=1, replica_groups=mesh['chan'=8,'row'=4] {'chan'}, dimensions={0} | all-to-all | bytes 1310720 | tf_op jit(solution)/shard_map/all_to_all | solution.py:14
  35.3 0.0 copy-start.1
  35.3 2.3 %reshape.57 = bf16[512,1,640]{2,1,0:T(2,128)(2,1)S(1)} reshape(bf16[8,2,20480]{2,1,0:T(2,128)(2,1)} %all_to_all.69) | data formatting | bytes 1310720
  37.6 0.1 copy.22
  37.7 0.0 copy-done.1
  37.7 0.5 fusion.2
  38.2 0.1 copy.15
  38.3 20.6 %all_to_all.70 = bf16[64,8,640]{2,0,1:T(8,128)(2,1)S(1)} all-to-all(bf16[64,8,640]{2,0,1:T(8,128)(2,1)S(1)} %copy.15), channel_id=1, replica_groups=mesh['chan'=8,'row'=4] {'chan'}, dimensions={1} | all-to-all | bytes 1310720 | tf_op jit(solution)/shard_map/all_to_all | solution.py:18
  58.9 0.0 copy-done
  58.9 3.1 %fusion = bf16[2048,1,640]{0,2,1:T(8,128)(2,1)} fusion(bf16[512,640]{1,0:T(8,128)(2,1)S(1)} %bitcast.47, bf16[2048,1,512]{2,0,1:T(8,128)(2,1)S(1)} %copy-done), kind=kOutput, calls=%fused_computation.1 | convolution fusion | flops 1343488000 | bytes 5373952 | tf_op jit(solution)/shard_map/zmo,omu->zmu/dot_general | solution.py:19
  62.0 0.0 all-reduce.2.cloned.1.call-update
  62.0 58.7 %all-reduce.2.cloned.1.call-done = bf16[2048,1,640]{0,2,1:T(8,128)(2,1)} async-done(((bf16[2048,1,640]{0,2,1:T(8,128)(2,1)}), bf16[2048,1,640]{0,2,1:T(8,128)(2,1)}) %all-reduce.2.cloned.1.call-update) | async-done | bytes 2621456 | tf_op jit(solution)/shard_map/psum | solution.py:23
  120.8 1.1 convert_convert_fusion
  121.9 1.1 reduce.1
  123.0 0.3 copy.33
  123.3 0.2 reshape.58
  123.5 23.0 %all_to_all.71 = bf16[8,2,20480]{2,1,0:T(2,128)(2,1)} all-to-all(bf16[8,2,20480]{2,1,0:T(2,128)(2,1)S(1)} %reshape.58), channel_id=1, replica_groups=mesh['chan'=8,'row'=4] {'chan'}, dimensions={0} | all-to-all | bytes 1310720 | tf_op jit(solution)/shard_map/all_to_all | solution.py:26
  146.5 2.3 %reshape.59 = bf16[512,1,640]{2,1,0:T(2,128)(2,1)S(1)} reshape(bf16[8,2,20480]{2,1,0:T(2,128)(2,1)} %all_to_all.71) | data formatting | bytes 1310720
  148.9 0.1 copy.23
  149.0 0.5 fusion.3
  149.5 0.1 copy.19
  149.6 20.5 %all_to_all.72 = bf16[64,8,640]{2,0,1:T(8,128)(2,1)S(1)} all-to-all(bf16[64,8,640]{2,0,1:T(8,128)(2,1)S(1)} %copy.19), channel_id=1, replica_groups=mesh['chan'=8,'row'=4] {'chan'}, dimensions={1} | all-to-all | bytes 1310720 | tf_op jit(solution)/shard_map/all_to_all | solution.py:30
  170.1 1.0 bitcast_select_fusion
  (1 shorter events, 0.0 us)
Async XLA Ops:
  6.5 52.3 %copy-start = (bf16[2048,1,512]{2,0,1:T(8,128)(2,1)S(1)}, bf16[2048,1,512]{2,0,1:T(8,128)(2,1)}, u32[]{:S(2)}) copy-start(bf16[2048,1,512]{2,0,1:T(8,128)(2,1)} %param.7) | copy-start | bytes 6291460
  6.5 114.2 %all-reduce.2.cloned.1.call-start = ((), (), s32[]{:S(2)}) async-start(), calls=%async_computation.4 | async-start | bytes 5242880 | tf_op jit(solution)/shard_map/psum | solution.py:23
  35.3 2.5 %copy-start.1 = (bf16[8,8]{1,0:T(8,128)(2,1)S(1)}, bf16[8,8]{1,0:T(8,128)(2,1)}, u32[]{:S(2)}) copy-start(bf16[8,8]{1,0:T(8,128)(2,1)} %param.6) | copy-start | bytes 388
Sparse Core Ops, SparseCore 0:
  62.1 58.5 all-reduce.1
where the time goes:
time: 178 us
  blocking collectives  88.9 us (50%)
  waiting for transfers between devices  58.8 us (33%)
  between operations  14.3 us (8%)
  local copies, waits for them, and re-layouts  6.14 us (3%)
  other arithmetic  5.63 us (3%)
  matrix products  4.12 us (2%)
    psum x1, waiting for transfers between devices, on_device(): lax.psum(full_terms.astype(jnp.bfloat16), 'row').astype(jnp.float32)  58.7 us
    all_to_all x1, blocking collectives, on_device(): lax.all_to_all(masked, 'chan', split_axis=0, concat_axis=1, tiled=True)  24.9 us
    all_to_all x1, blocking collectives, on_device(): lax.all_to_all(summed_rows, 'chan', split_axis=0, concat_axis=1, tiled=True)  23 us
    all_to_all x1, blocking collectives, on_device(): lax.all_to_all(mixed_rows, 'chan', split_axis=1, concat_axis=0, tiled=True)  20.6 us
    all_to_all x1, blocking collectives, on_device(): lax.all_to_all(unmixed, 'chan', split_axis=1, concat_axis=0, tiled=True)  20.5 us
    unnamed x11, local copies, waits for them, and re-layouts  5.48 us
  transfers between devices with their start and end apart: 1, of which 1 were waited for; matrix products, arithmetic and copies ran while one was open for 0% of the time, Pallas kernels for 0%

commit v1 on v0

v1 whole, which is shorter than its diff:
```python
import jax
import jax.numpy as jnp
from jax import lax
from jax.sharding import PartitionSpec as P

F32 = jnp.float32
BF16 = jnp.bfloat16


def chunk_bounds(columns, pieces):
    unit = 128 if columns % 128 == 0 else 1
    units = columns // unit
    pieces = min(pieces, units)
    marks = [units * i // pieces * unit for i in range(pieces + 1)]
    return list(zip(marks[:-1], marks[1:]))


def solution(mesh):
    n_chan, n_row = mesh.shape["chan"], mesh.shape["row"]
    chan_bits = [1 << b for b in range(n_chan.bit_length() - 1)]
    row_bits = [1 << b for b in range(n_row.bit_length() - 1)]
    gather_bits = [chan_bits[-1], chan_bits[0]]
    reduce_bits = [b for b in chan_bits if b not in gather_bits]

    def swap(x, axis, size, bit):
        return lax.ppermute(x, axis, [(i, i ^ bit) for i in range(size)])

    def on_device(amplitudes, block_rows, recoupling, interaction):
        rows_here, _, columns = amplitudes.shape
        c = lax.axis_index("chan")
        g = lax.axis_index("row")
        local_rows = g * rows_here + lax.iota(jnp.int32, rows_here)
        live = (local_rows < block_rows[0])[:, None]
        zero = jnp.zeros((), BF16)
        index = lax.iota(jnp.int32, n_chan)
        pick = ((c ^ index)[:, None] == index[None, :]).astype(BF16)
        coef = jnp.dot(
            jnp.dot(pick, recoupling, preferred_element_type=F32).astype(BF16),
            pick.T, preferred_element_type=F32)

        own = amplitudes.reshape(rows_here, columns)
        weights = interaction.reshape(interaction.shape[0], interaction.shape[2])

        def gather(block):
            held = {0: block}
            for bit in gather_bits:
                held.update({m ^ bit: swap(v, "chan", n_chan, bit) for m, v in list(held.items())})
            return held

        def mix(held, t, matrix):
            return sum(matrix[t, m] * v.astype(F32) for m, v in held.items())

        def spread_targets(bits):
            out = [0]
            for bit in bits:
                out += [t ^ bit for t in out]
            return out

        def recouple_in(block):
            held = gather(block)
            part = {t: mix(held, t, coef) for t in spread_targets(reduce_bits)}
            for bit in reversed(reduce_bits):
                keep = [t for t in part if not t & bit]
                part = {t: part[t] + swap(part[t ^ bit].astype(BF16), "chan", n_chan, bit).astype(F32) for t in keep}
            return part[0].astype(BF16)

        def recouple_out(block):
            held = {0: block}
            for bit in reduce_bits:
                held.update({m ^ bit: swap(v, "chan", n_chan, bit) for m, v in list(held.items())})
            part = {t: mix(held, t, coef.T) for t in spread_targets(gather_bits)}
            for bit in reversed(gather_bits):
                keep = [t for t in part if not t & bit]
                part = {t: part[t] + swap(part[t ^ bit].astype(BF16), "chan", n_chan, bit).astype(F32) for t in keep}
            return part[0].astype(BF16)

        def sum_rows(partial):
            part = partial.reshape(n_row, -1, partial.shape[-1])
            for bit in row_bits:
                pairs = part.reshape(part.shape[0] // 2, 2, *part.shape[1:])
                mine = (g & bit) // bit
                kept = lax.dynamic_index_in_dim(pairs, mine, 1, keepdims=False)
                sent = lax.dynamic_index_in_dim(pairs, 1 - mine, 1, keepdims=False)
                part = (kept.astype(F32) + swap(sent, "row", n_row, bit).astype(F32)).astype(BF16)
            return part[0]

        outs = []
        for lo, hi in chunk_bounds(columns, 5):
            block = jnp.where(live, own[:, lo:hi], zero)
            cross = recouple_in(block)
            partial = jnp.dot(weights, cross, preferred_element_type=F32).astype(BF16)
            outs.append(jnp.where(live, recouple_out(sum_rows(partial)), zero))
        return jnp.concatenate(outs, axis=1).reshape(amplitudes.shape)

    return jax.shard_map(
        on_device,
        mesh=mesh,
        in_specs=(P("row", "chan", None), P("chan"), P(), P(None, "chan", "row")),
        out_specs=P("row", "chan", None),
        check_vma=False,
    )
```

time: 178 us -> 178 us (level)
  blocking collectives: 88.9 us -> 0 us
  starting transfers between devices: 0.01 us -> 52.2 us
  other arithmetic: 5.63 us -> 47.8 us
  waiting for transfers between devices: 58.8 us -> 18 us
  local copies, waits for them, and re-layouts: 6.14 us -> 31.8 us
  matrix products: 4.12 us -> 25.1 us
  between operations: 14.3 us -> 1.38 us
    all_to_all x4 -> x0, blocking collectives: 88.9 us -> none  [the longest x1 24.9 us: on_device(): lax.all_to_all(masked, 'chan', split_axis=0, concat_axis=1, tiled=True)]
    psum x1 -> x0, waiting for transfers between devices: 58.7 us -> none  [on_device(): lax.psum(full_terms.astype(jnp.bfloat16), 'row').astype(jnp.float32)]
    ppermute x0 -> x50, starting transfers between devices: none -> 52.2 us  [swap(): return lax.ppermute(x, axis, [(i, i ^ bit) for i in range(size)])]
    convert_element_type x2 -> x20, other arithmetic: 2.27 us -> 39.3 us  [the longest x10 18.8 us: recouple_out(): part[t ^ bit].astype(BF16)]
    dot_general x3 -> x6, matrix products: 4.12 us -> 25.1 us  [the longest x5 24.1 us: on_device(): partial = jnp.dot(weights, cross, preferred_element_type=F32).astype(BF16)]
    dynamic_slice x0 -> x8, local copies, waits for them, and re-layouts: none -> 18.1 us  [the longest x5 9.6 us: sum_rows(): sent = lax.dynamic_index_in_dim(pairs, 1 - mine, 1, keepdims=False)]
    ppermute x0 -> x50, waiting for transfers between devices: none -> 18 us  [swap(): return lax.ppermute(x, axis, [(i, i ^ bit) for i in range(size)])]
    unnamed x0 -> x4, other arithmetic: none -> 5.57 us
  transfers between devices with their start and end apart: 1 -> 50, of which waited for: 1 -> 8; matrix products, arithmetic and copies ran while one was open for 0% -> 57% of each run, Pallas kernels for 0% -> 0%
where the time goes in v1:
time: 178 us; the launch traced here: 176 us
  starting transfers between devices  52.2 us (29%)
  other arithmetic  47.8 us (27%)
  local copies, waits for them, and re-layouts  31.8 us (18%)
  matrix products  25.1 us (14%)
  waiting for transfers between devices  18 us (10%)
    ppermute x50, starting transfers between devices, swap(): return lax.ppermute(x, axis, [(i, i ^ bit) for i in range(size)])  52.2 us
    dot_general x5, matrix products, on_device(): partial = jnp.dot(weights, cross, preferred_element_type=F32).astype(BF16)  24.1 us
    convert_element_type x10, other arithmetic, recouple_out(): part[t ^ bit].astype(BF16)  18.8 us
    ppermute x50, waiting for transfers between devices, swap(): return lax.ppermute(x, axis, [(i, i ^ bit) for i in range(size)])  18 us
    convert_element_type x5, other arithmetic, recouple_in(): part[t ^ bit].astype(BF16)  15.3 us
    dynamic_slice x5, local copies, waits for them, and re-layouts, sum_rows(): sent = lax.dynamic_index_in_dim(pairs, 1 - mine, 1, keepdims=False)  9.6 us
    dynamic_slice x3, local copies, waits for them, and re-layouts, sum_rows(): kept = lax.dynamic_index_in_dim(pairs, mine, 1, keepdims=False)  8.54 us
    unnamed x61, local copies, waits for them, and re-layouts  7.25 us
  transfers between devices with their start and end apart: 50, of which 8 were waited for; matrix products, arithmetic and copies ran while one was open for 57% of the time, Pallas kernels for 0%

profile of v1, /device:TPU:0, one launch (start us, length us, event | category | flops | bytes accessed | tf_op | source)
XLA Modules:
  0.0 176.3 jit_solution(17031530649484309771)
XLA Ops:
  0.8 1.3 slice_select_fusion
  2.2 4.1 %collective-permute-start = (bf16[512,128]{1,0:T(8,128)(2,1)S(1)}, bf16[512,128]{1,0:T(8,128)(2,1)S(1)}, u32[]{:S(2)}, u32[]{:S(2)}) collective-permute-start(bf16[512,128]{1,0:T(8,128)(2,1)S(1)} %get-tuple-element.9), channel_id=1, source_target_pairs={{0,16},{4,20},{8,24},{12,28},{16,0},{20,4},{24,8},{28,12},{1,17},{... | collective-permute-start | bytes 393224 | tf_op jit(solution)/shard_map/ppermute | solution.py:26
  6.3 1.5 collective-permute-start.1
  8.4 2.8 %collective-permute-start.10 = (bf16[512,128]{1,0:T(8,128)(2,1)S(1)}, bf16[512,128]{1,0:T(8,128)(2,1)S(1)}, u32[]{:S(2)}, u32[]{:S(2)}) collective-permute-start(bf16[512,128]{1,0:T(8,128)(2,1)S(1)} %get-tuple-element.8), channel_id=1, source_target_pairs={{0,16},{4,20},{8,24},{12,28},{16,0},{20,4},{24,8},{28,12},{1,17},{... | collective-permute-start | bytes 393224 | tf_op jit(solution)/shard_map/ppermute | solution.py:26
  12.2 6.8 %collective-permute-done = bf16[512,128]{1,0:T(8,128)(2,1)S(1)} collective-permute-done((bf16[512,128]{1,0:T(8,128)(2,1)S(1)}, bf16[512,128]{1,0:T(8,128)(2,1)S(1)}, u32[]{:S(2)}, u32[]{:S(2)}) %collective-permute-start) | collective-permute-done | bytes 131104 | tf_op jit(solution)/shard_map/ppermute | solution.py:26
  19.0 1.8 %collective-permute-start.2 = (bf16[512,128]{1,0:T(8,128)(2,1)S(1)}, bf16[512,128]{1,0:T(8,128)(2,1)S(1)}, u32[]{:S(2)}, u32[]{:S(2)}) collective-permute-start(bf16[512,128]{1,0:T(8,128)(2,1)S(1)} %collective-permute-done), channel_id=1, source_target_pairs={{0,4},{4,0},{8,12},{12,8},{16,20},{20,16},{24,28},{28,24},{1,5},{5... | collective-permute-start | bytes 393224 | tf_op jit(solution)/shard_map/ppermute | solution.py:26
  22.5 2.9 %collective-permute-done.2 = bf16[512,128]{1,0:T(8,128)(2,1)S(1)} collective-permute-done((bf16[512,128]{1,0:T(8,128)(2,1)S(1)}, bf16[512,128]{1,0:T(8,128)(2,1)S(1)}, u32[]{:S(2)}, u32[]{:S(2)}) %collective-permute-start.2) | collective-permute-done | bytes 131104 | tf_op jit(solution)/shard_map/ppermute | solution.py:26
  25.4 1.3 collective-permute-start.22
  26.6 2.5 %fusion.24 = bf16[512,128]{1,0:T(8,128)(2,1)S(1)} fusion(bf16[512,128]{1,0:T(8,128)(2,1)S(1)} %get-tuple-element.9, bf16[512,128]{1,0:T(8,128)(2,1)S(1)} %collective-permute-done, bf16[512,128]{1,0:T(8,128)(2,1)S(1)} %collective-permute-done.1, bf16[512,128]{1,0:T(8,128)(2,1)S(1)} %collective-permute-done.2, f32[]{:T(128)} %bitcast.11, f32[]{:T(128)} %bitcast.10, ...), kind=kLoop, calls=%fused_computation.115 | loop fusion | flops 786432 | bytes 655376 | tf_op jit(solution)/shard_map/convert_element_type | solution.py:64
  30.1 1.5 collective-permute-done.22
  32.4 3.2 %fusion.42 = bf16[512,128]{1,0:T(8,128)(2,1)} fusion(bf16[512,128]{1,0:T(8,128)(2,1)S(1)} %get-tuple-element.7, bf16[512,128]{1,0:T(8,128)(2,1)S(1)} %collective-permute-done.20, bf16[512,128]{1,0:T(8,128)(2,1)S(1)} %collective-permute-done.21, bf16[512,128]{1,0:T(8,128)(2,1)S(1)} %collective-permute-done.22, f32[]{:T(128)} %bitcast.11, f32[]{:T(128)} %bitcast.10, ...), kind=kLoop, calls=%fused_computation.133 | loop fusion | flops 786432 | bytes 655376 | tf_op jit(solution)/shard_map/convert_element_type | solution.py:64
  35.6 1.3 collective-permute-start.31
  38.9 1.4 collective-permute-start.3
  40.3 3.2 %fusion.33 = bf16[512,128]{1,0:T(8,128)(2,1)} fusion(bf16[512,128]{1,0:T(8,128)(2,1)S(1)} %get-tuple-element.8, bf16[512,128]{1,0:T(8,128)(2,1)S(1)} %collective-permute-done.10, bf16[512,128]{1,0:T(8,128)(2,1)S(1)} %collective-permute-done.11, bf16[512,128]{1,0:T(8,128)(2,1)S(1)} %collective-permute-done.12, f32[]{:T(128)} %bitcast.11, f32[]{:T(128)} %bitcast.10, ...), kind=kLoop, calls=%fused_computation.124 | loop fusion | flops 786432 | bytes 655376 | tf_op jit(solution)/shard_map/convert_element_type | solution.py:64
  44.1 1.4 collective-permute-start.13
  45.5 3.2 %fusion.60 = bf16[512,128]{1,0:T(8,128)(2,1)} fusion(bf16[512,128]{1,0:T(8,128)(2,1)S(1)} %get-tuple-element.5, bf16[512,128]{1,0:T(8,128)(2,1)S(1)} %collective-permute-done.40, bf16[512,128]{1,0:T(8,128)(2,1)S(1)} %collective-permute-done.41, bf16[512,128]{1,0:T(8,128)(2,1)S(1)} %collective-permute-done.42, f32[]{:T(128)} %bitcast.11, f32[]{:T(128)} %bitcast.10, ...), kind=kLoop, calls=%fused_computation.151 | loop fusion | flops 786432 | bytes 655376 | tf_op jit(solution)/shard_map/convert_element_type | solution.py:64
  49.3 3.2 %fusion.51 = bf16[512,128]{1,0:T(8,128)(2,1)} fusion(bf16[512,128]{1,0:T(8,128)(2,1)S(1)} %get-tuple-element.6, bf16[512,128]{1,0:T(8,128)(2,1)S(1)} %collective-permute-done.30, bf16[512,128]{1,0:T(8,128)(2,1)S(1)} %collective-permute-done.31, bf16[512,128]{1,0:T(8,128)(2,1)S(1)} %collective-permute-done.32, f32[]{:T(128)} %bitcast.11, f32[]{:T(128)} %bitcast.10, ...), kind=kLoop, calls=%fused_computation.142 | loop fusion | flops 786432 | bytes 655376 | tf_op jit(solution)/shard_map/convert_element_type | solution.py:64
  52.5 1.4 collective-permute-start.33
  54.1 4.3 %fusion = bf16[2048,128]{0,1:T(8,128)(2,1)S(1)} fusion(bf16[2048,1,512]{2,0,1:T(8,128)(2,1)S(1)} %copy-done, bf16[512,128]{1,0:T(8,128)(2,1)S(1)} %get-tuple-element.9, bf16[512,128]{1,0:T(8,128)(2,1)} %copy-done.11, bf16[512,128]{1,0:T(8,128)(2,1)} %copy-done.12, bf16[512,128]{1,0:T(8,128)(2,1)} %copy-done.13, ...), kind=kOutput, calls=%fused_computation.5 | convolution fusion | flops 269615104 | bytes 3276816 | tf_op jit(solution)/shard_map/dot_general | solution.py:91
  58.8 1.9 %constant_dynamic-slice_fusion.14 = (bf16[2,1,512,128]{2,1,0,3:T(2,128)(2,1)S(1)}, bf16[2,1,512,128]{2,1,0,3:T(2,128)(2,1)}) fusion(bf16[2,2,512,128]{2,1,0,3:T(2,128)(2,1)S(1)} %reshape_reshape.15, s32[]{:T(128)S(6)} %select_n.76, s32[]{:T(128)S(6)} %select_n.77), kind=kLoop, calls=%fused_computation.266 | loop fusion | bytes 1048584 | tf_op jit(solution)/shard_map/jit(dynamic_index_in_dim)/dynamic_slice | solution.py:82
  60.7 1.9 %copy.6 = bf16[2,1,512,128]{3,2,0,1:T(8,128)(2,1)} copy(bf16[2,1,512,128]{2,1,0,3:T(2,128)(2,1)} %get-tuple-element.19) | data formatting | bytes 524288 | tf_op jit(solution)/shard_map/jit(dynamic_index_in_dim)/dynamic_slice | solution.py:83
  62.6 5.2 %fusion.2 = bf16[2048,128]{0,1:T(8,128)(2,1)} fusion(bf16[2048,1,512]{2,0,1:T(8,128)(2,1)S(1)} %copy-done, bf16[512,128]{1,0:T(8,128)(2,1)} %copy-done.3, bf16[512,128]{1,0:T(8,128)(2,1)} %copy-done.9, bf16[512,128]{1,0:T(8,128)(2,1)} %copy-done.10, bf16[512,128]{1,0:T(8,128)(2,1)} %copy-done.25, bf16[512,128]{1,0:T(8,128)(2,1)} %collective-permute-done.23, ...), kind=kOutput, calls=%fused_computation.7 | convolution fusion | flops 269615104 | bytes 3276816 | tf_op jit(solution)/shard_map/dot_general | solution.py:91
  68.9 1.4 reshape_reshape.17
  70.3 5.2 %fusion.1 = bf16[2048,128]{0,1:T(8,128)(2,1)} fusion(bf16[2048,1,512]{2,0,1:T(8,128)(2,1)S(1)} %copy-done, bf16[512,128]{1,0:T(8,128)(2,1)S(1)} %get-tuple-element.8, bf16[512,128]{1,0:T(8,128)(2,1)} %copy-done.8, bf16[512,128]{1,0:T(8,128)(2,1)} %copy-done.21, bf16[512,128]{1,0:T(8,128)(2,1)} %copy-done.26, bf16[512,128]{1,0:T(8,128)(2,1)} %collective-permute-done.13, ...), kind=kOutput, calls=%fused_computation.6 | convolution fusion | flops 269615104 | bytes 3276816 | tf_op jit(solution)/shard_map/dot_general | solution.py:91
  75.5 1.4 reshape_reshape.16
  76.9 3.4 %constant_dynamic-slice_fusion.8 = (bf16[2,1,512,128]{2,1,0,3:T(2,128)(2,1)}, bf16[2,1,512,128]{2,1,0,3:T(2,128)(2,1)}, bf16[2,1,512,128]{2,1,0,3:T(2,128)(2,1)}, bf16[2,1,512,128]{2,1,0,3:T(2,128)(2,1)}) fusion(bf16[2,2,512,128]{2,1,0,3:T(2,128)(2,1)S(1)} %reshape_reshape.17, s32[]{:T(128)S(6)} %select_n.76, s32[]{:T(128)S(6)} %select_n.77, ...), kind=kLoop, calls=%fused_computation.260 | loop fusion | bytes 2097160 | tf_op jit(solution)/shard_map/jit(dynamic_index_in_dim)/dynamic_slice | solution.py:82
  80.3 1.9 %copy.8 = bf16[2,1,512,128]{3,2,0,1:T(8,128)(2,1)} copy(bf16[2,1,512,128]{2,1,0,3:T(2,128)(2,1)} %get-tuple-element.48) | data formatting | bytes 524288 | tf_op jit(solution)/shard_map/jit(dynamic_index_in_dim)/dynamic_slice | solution.py:83
  82.7 1.9 %copy.16 = bf16[2,1,512,128]{3,2,0,1:T(8,128)(2,1)} copy(bf16[2,1,512,128]{2,1,0,3:T(2,128)(2,1)} %get-tuple-element.49) | data formatting | bytes 524288
  84.6 1.9 %copy.10 = bf16[2,1,512,128]{3,2,0,1:T(8,128)(2,1)} copy(bf16[2,1,512,128]{2,1,0,3:T(2,128)(2,1)} %get-tuple-element.15) | data formatting | bytes 524288 | tf_op jit(solution)/shard_map/jit(dynamic_index_in_dim)/dynamic_slice | solution.py:83
  86.6 4.2 %fusion.4 = bf16[2048,128]{0,1:T(8,128)(2,1)S(1)} fusion(bf16[2048,1,512]{2,0,1:T(8,128)(2,1)S(1)} %copy-done, bf16[512,128]{1,0:T(8,128)(2,1)S(1)} %get-tuple-element.5, bf16[512,128]{1,0:T(8,128)(2,1)S(1)} %copy-done.15, bf16[512,128]{1,0:T(8,128)(2,1)S(1)} %copy-done.19, bf16[512,128]{1,0:T(8,128)(2,1)S(1)} %copy-done.24, ...), kind=kOutput, calls=%fused_computation.9 | convolution fusion | flops 269615104 | bytes 3276816 | tf_op jit(solution)/shard_map/dot_general | solution.py:91
  90.8 5.2 %fusion.3 = bf16[2048,128]{0,1:T(8,128)(2,1)} fusion(bf16[2048,1,512]{2,0,1:T(8,128)(2,1)S(1)} %copy-done, bf16[512,128]{1,0:T(8,128)(2,1)S(1)} %get-tuple-element.6, bf16[512,128]{1,0:T(8,128)(2,1)S(1)} %copy-done.17, bf16[512,128]{1,0:T(8,128)(2,1)} %copy-done.20, bf16[512,128]{1,0:T(8,128)(2,1)} %copy-done.22, ...), kind=kOutput, calls=%fused_computation.8 | convolution fusion | flops 269615104 | bytes 3276816 | tf_op jit(solution)/shard_map/dot_general | solution.py:91
  96.8 1.4 reshape_reshape.18
  98.3 3.3 %constant_dynamic-slice_fusion.2 = (bf16[2,1,512,128]{2,1,0,3:T(2,128)(2,1)}, bf16[2,1,512,128]{2,1,0,3:T(2,128)(2,1)}, bf16[2,1,512,128]{2,1,0,3:T(2,128)(2,1)}, bf16[2,1,512,128]{2,1,0,3:T(2,128)(2,1)}) fusion(bf16[2,2,512,128]{2,1,0,3:T(2,128)(2,1)S(1)} %reshape_reshape.19, s32[]{:T(128)S(6)} %select_n.76, s32[]{:T(128)S(6)} %select_n.77, ...), kind=kLoop, calls=%fused_computation.254 | loop fusion | bytes 2097160 | tf_op jit(solution)/shard_map/jit(dynamic_index_in_dim)/dynamic_slice | solution.py:82
  101.6 2.0 %copy.12 = bf16[2,1,512,128]{3,2,0,1:T(8,128)(2,1)} copy(bf16[2,1,512,128]{2,1,0,3:T(2,128)(2,1)} %get-tuple-element.46) | data formatting | bytes 524288 | tf_op jit(solution)/shard_map/jit(dynamic_index_in_dim)/dynamic_slice | solution.py:83
  104.0 1.9 %copy.18 = bf16[2,1,512,128]{3,2,0,1:T(8,128)(2,1)} copy(bf16[2,1,512,128]{2,1,0,3:T(2,128)(2,1)} %get-tuple-element.47) | data formatting | bytes 524288
  105.9 1.9 %copy.14 = bf16[2,1,512,128]{3,2,0,1:T(8,128)(2,1)} copy(bf16[2,1,512,128]{2,1,0,3:T(2,128)(2,1)} %get-tuple-element.11) | data formatting | bytes 524288 | tf_op jit(solution)/shard_map/jit(dynamic_index_in_dim)/dynamic_slice | solution.py:83
  110.0 1.6 collective-permute-start.5
  114.3 1.6 collective-permute-start.25
  118.5 1.6 collective-permute-start.45
  120.9 1.4 collective-permute-start.16
  123.1 1.6 collective-permute-done.35
  125.5 1.7 collective-permute-done.45
  127.9 1.3 fusion.71
  129.2 1.4 collective-permute-start.8
  130.7 1.3 fusion.82
  132.8 1.3 fusion.93
  134.1 1.5 collective-permute-start.28
  135.6 1.3 fusion.104
  137.9 1.3 fusion.115
  140.3 2.5 %fusion.66 = (bf16[512,128]{1,0:T(8,128)(2,1)S(1)}, bf16[512,128]{1,0:T(8,128)(2,1)S(1)}) fusion(bf16[512,128]{1,0:T(8,128)(2,1)S(1)} %fusion.116, bf16[512,128]{1,0:T(8,128)(2,1)S(1)} %collective-permute-done.6, f32[]{:T(128)} %bitcast.19, f32[]{:T(128)} %bitcast.18, bf16[512,128]{1,0:T(8,128)(2,1)S(1)} %collective-permute-done.8, f32[]{:T(128)} %bitcast.21, ...), kind=kLoop, calls=%fused_computation.157 | loop fusion | flops 786432 | bytes 655376 | tf_op jit(solution)/shard_map/convert_element_type | solution.py:74
  142.8 1.8 %collective-permute-start.9 = (bf16[512,128]{1,0:T(8,128)(2,1)S(1)}, bf16[512,128]{1,0:T(8,128)(2,1)S(1)}, u32[]{:S(2)}, u32[]{:S(2)}) collective-permute-start(bf16[512,128]{1,0:T(8,128)(2,1)S(1)} %get-tuple-element.29), channel_id=1, source_target_pairs={{0,16},{4,20},{8,24},{12,28},{16,0},{20,4},{24,8},{28,12},{1,17},{... | collective-permute-start | bytes 393224 | tf_op jit(solution)/shard_map/ppermute | solution.py:26
  145.5 2.5 %fusion.77 = (bf16[512,128]{1,0:T(8,128)(2,1)S(1)}, bf16[512,128]{1,0:T(8,128)(2,1)S(1)}) fusion(bf16[512,128]{1,0:T(8,128)(2,1)S(1)} %fusion.117, bf16[512,128]{1,0:T(8,128)(2,1)S(1)} %collective-permute-done.16, f32[]{:T(128)} %bitcast.19, f32[]{:T(128)} %bitcast.18, bf16[512,128]{1,0:T(8,128)(2,1)S(1)} %collective-permute-done.18, f32[]{:T(128)} %bitcast.21, ...), kind=kLoop, calls=%fused_computation.168 | loop fusion | flops 786432 | bytes 655376 | tf_op jit(solution)/shard_map/convert_element_type | solution.py:74
  148.0 1.3 collective-permute-start.19
  149.3 2.5 %fusion.88 = (bf16[512,128]{1,0:T(8,128)(2,1)S(1)}, bf16[512,128]{1,0:T(8,128)(2,1)S(1)}) fusion(bf16[512,128]{1,0:T(8,128)(2,1)S(1)} %fusion.118, bf16[512,128]{1,0:T(8,128)(2,1)S(1)} %collective-permute-done.26, f32[]{:T(128)} %bitcast.19, f32[]{:T(128)} %bitcast.18, bf16[512,128]{1,0:T(8,128)(2,1)S(1)} %collective-permute-done.28, f32[]{:T(128)} %bitcast.21, ...), kind=kLoop, calls=%fused_computation.179 | loop fusion | flops 786432 | bytes 655376 | tf_op jit(solution)/shard_map/convert_element_type | solution.py:74
  153.0 2.5 %fusion.99 = (bf16[512,128]{1,0:T(8,128)(2,1)S(1)}, bf16[512,128]{1,0:T(8,128)(2,1)S(1)}) fusion(bf16[512,128]{1,0:T(8,128)(2,1)S(1)} %fusion.119, bf16[512,128]{1,0:T(8,128)(2,1)S(1)} %collective-permute-done.36, f32[]{:T(128)} %bitcast.19, f32[]{:T(128)} %bitcast.18, bf16[512,128]{1,0:T(8,128)(2,1)S(1)} %collective-permute-done.38, f32[]{:T(128)} %bitcast.21, ...), kind=kLoop, calls=%fused_computation.190 | loop fusion | flops 786432 | bytes 655376 | tf_op jit(solution)/shard_map/convert_element_type | solution.py:74
  155.5 1.8 %collective-permute-start.29 = (bf16[512,128]{1,0:T(8,128)(2,1)S(1)}, bf16[512,128]{1,0:T(8,128)(2,1)S(1)}, u32[]{:S(2)}, u32[]{:S(2)}) collective-permute-start(bf16[512,128]{1,0:T(8,128)(2,1)S(1)} %get-tuple-element.25), channel_id=1, source_target_pairs={{0,16},{4,20},{8,24},{12,28},{16,0},{20,4},{24,8},{28,12},{1,17},{... | collective-permute-start | bytes 393224 | tf_op jit(solution)/shard_map/ppermute | solution.py:26
  157.2 2.5 %fusion.110 = (bf16[512,128]{1,0:T(8,128)(2,1)S(1)}, bf16[512,128]{1,0:T(8,128)(2,1)S(1)}) fusion(bf16[512,128]{1,0:T(8,128)(2,1)S(1)} %fusion.120, bf16[512,128]{1,0:T(8,128)(2,1)S(1)} %collective-permute-done.46, f32[]{:T(128)} %bitcast.19, f32[]{:T(128)} %bitcast.18, bf16[512,128]{1,0:T(8,128)(2,1)S(1)} %collective-permute-done.48, f32[]{:T(128)} %bitcast.21, ...), kind=kLoop, calls=%fused_computation.201 | loop fusion | flops 786432 | bytes 655376 | tf_op jit(solution)/shard_map/convert_element_type | solution.py:74
  161.9 1.4 fusion.130
  164.5 1.7 collective-permute-start.49
  166.2 1.4 fusion.128
  168.6 1.4 fusion.126
  170.0 2.5 %collective-permute-done.39 = bf16[512,128]{1,0:T(8,128)(2,1)S(1)} collective-permute-done((bf16[512,128]{1,0:T(8,128)(2,1)S(1)}, bf16[512,128]{1,0:T(8,128)(2,1)S(1)}, u32[]{:S(2)}, u32[]{:S(2)}) %collective-permute-start.39) | collective-permute-done | bytes 131104 | tf_op jit(solution)/shard_map/ppermute | solution.py:26
  172.5 1.4 fusion.124
  174.0 1.4 fusion.122
  (156 shorter events, 32.5 us)
Async XLA Ops:
  0.0 54.1 %copy-start = (bf16[2048,1,512]{2,0,1:T(8,128)(2,1)S(1)}, bf16[2048,1,512]{2,0,1:T(8,128)(2,1)}, u32[]{:S(2)}) copy-start(bf16[2048,1,512]{2,0,1:T(8,128)(2,1)} %param.7) | copy-start | bytes 6291460
  2.1 51.9 %copy-start.3 = (bf16[512,128]{1,0:T(8,128)(2,1)}, bf16[512,128]{1,0:T(8,128)(2,1)S(1)}, u32[]{:S(2)}) copy-start(bf16[512,128]{1,0:T(8,128)(2,1)S(1)} %get-tuple-element.7) | copy-start | bytes 393220
  2.2 16.9 %collective-permute-start = (bf16[512,128]{1,0:T(8,128)(2,1)S(1)}, bf16[512,128]{1,0:T(8,128)(2,1)S(1)}, u32[]{:S(2)}, u32[]{:S(2)}) collective-permute-start(bf16[512,128]{1,0:T(8,128)(2,1)S(1)} %get-tuple-element.9), channel_id=1, source_target_pairs={{0,16},{4,20},{8,24},{12,28},{16,0},{20,4},{24,8},{28,12},{1,17},{... | collective-permute-start | bytes 393224 | tf_op jit(solution)/shard_map/ppermute | solution.py:26
  6.3 15.9 %collective-permute-start.1 = (bf16[512,128]{1,0:T(8,128)(2,1)S(1)}, bf16[512,128]{1,0:T(8,128)(2,1)S(1)}, u32[]{:S(2)}, u32[]{:S(2)}) collective-permute-start(bf16[512,128]{1,0:T(8,128)(2,1)S(1)} %get-tuple-element.9), channel_id=1, source_target_pairs={{0,4},{4,0},{8,12},{12,8},{16,20},{20,16},{24,28},{28,24},{1,5},{5... | collective-permute-start | bytes 393224 | tf_op jit(solution)/shard_map/ppermute | solution.py:26
  7.8 14.7 %collective-permute-start.20 = (bf16[512,128]{1,0:T(8,128)(2,1)S(1)}, bf16[512,128]{1,0:T(8,128)(2,1)S(1)}, u32[]{:S(2)}, u32[]{:S(2)}) collective-permute-start(bf16[512,128]{1,0:T(8,128)(2,1)S(1)} %get-tuple-element.7), channel_id=1, source_target_pairs={{0,16},{4,20},{8,24},{12,28},{16,0},{20,4},{24,8},{28,12},{1,17},{... | collective-permute-start | bytes 393224 | tf_op jit(solution)/shard_map/ppermute | solution.py:26
  8.1 21.1 %collective-permute-start.21 = (bf16[512,128]{1,0:T(8,128)(2,1)S(1)}, bf16[512,128]{1,0:T(8,128)(2,1)S(1)}, u32[]{:S(2)}, u32[]{:S(2)}) collective-permute-start(bf16[512,128]{1,0:T(8,128)(2,1)S(1)} %get-tuple-element.7), channel_id=1, source_target_pairs={{0,4},{4,0},{8,12},{12,8},{16,20},{20,16},{24,28},{28,24},{1,5},{5... | collective-permute-start | bytes 393224 | tf_op jit(solution)/shard_map/ppermute | solution.py:26
  8.4 21.7 %collective-permute-start.10 = (bf16[512,128]{1,0:T(8,128)(2,1)S(1)}, bf16[512,128]{1,0:T(8,128)(2,1)S(1)}, u32[]{:S(2)}, u32[]{:S(2)}) collective-permute-start(bf16[512,128]{1,0:T(8,128)(2,1)S(1)} %get-tuple-element.8), channel_id=1, source_target_pairs={{0,16},{4,20},{8,24},{12,28},{16,0},{20,4},{24,8},{28,12},{1,17},{... | collective-permute-start | bytes 393224 | tf_op jit(solution)/shard_map/ppermute | solution.py:26
  19.0 34.9 %copy-start.11 = (bf16[512,128]{1,0:T(8,128)(2,1)}, bf16[512,128]{1,0:T(8,128)(2,1)S(1)}, u32[]{:S(2)}) copy-start(bf16[512,128]{1,0:T(8,128)(2,1)S(1)} %collective-permute-done) | copy-start | bytes 393220
  19.0 6.4 %collective-permute-start.2 = (bf16[512,128]{1,0:T(8,128)(2,1)S(1)}, bf16[512,128]{1,0:T(8,128)(2,1)S(1)}, u32[]{:S(2)}, u32[]{:S(2)}) collective-permute-start(bf16[512,128]{1,0:T(8,128)(2,1)S(1)} %collective-permute-done), channel_id=1, source_target_pairs={{0,4},{4,0},{8,12},{12,8},{16,20},{20,16},{24,28},{28,24},{1,5},{5... | collective-permute-start | bytes 393224 | tf_op jit(solution)/shard_map/ppermute | solution.py:26
  22.2 31.7 %copy-start.12 = (bf16[512,128]{1,0:T(8,128)(2,1)}, bf16[512,128]{1,0:T(8,128)(2,1)S(1)}, u32[]{:S(2)}) copy-start(bf16[512,128]{1,0:T(8,128)(2,1)S(1)} %collective-permute-done.1) | copy-start | bytes 393220
  22.2 13.4 %collective-permute-start.11 = (bf16[512,128]{1,0:T(8,128)(2,1)S(1)}, bf16[512,128]{1,0:T(8,128)(2,1)S(1)}, u32[]{:S(2)}, u32[]{:S(2)}) collective-permute-start(bf16[512,128]{1,0:T(8,128)(2,1)S(1)} %get-tuple-element.8), channel_id=1, source_target_pairs={{0,4},{4,0},{8,12},{12,8},{16,20},{20,16},{24,28},{28,24},{1,5},{5... | collective-permute-start | bytes 393224 | tf_op jit(solution)/shard_map/ppermute | solution.py:26
  22.5 31.6 %copy-start.9 = (bf16[512,128]{1,0:T(8,128)(2,1)}, bf16[512,128]{1,0:T(8,128)(2,1)S(1)}, u32[]{:S(2)}) copy-start(bf16[512,128]{1,0:T(8,128)(2,1)S(1)} %collective-permute-done.20) | copy-start | bytes 393220
  22.5 14.4 %collective-permute-start.40 = (bf16[512,128]{1,0:T(8,128)(2,1)S(1)}, bf16[512,128]{1,0:T(8,128)(2,1)S(1)}, u32[]{:S(2)}, u32[]{:S(2)}) collective-permute-start(bf16[512,128]{1,0:T(8,128)(2,1)S(1)} %get-tuple-element.5), channel_id=1, source_target_pairs={{0,16},{4,20},{8,24},{12,28},{16,0},{20,4},{24,8},{28,12},{1,17},{... | collective-permute-start | bytes 393224 | tf_op jit(solution)/shard_map/ppermute | solution.py:26
  25.4 28.6 %copy-start.13 = (bf16[512,128]{1,0:T(8,128)(2,1)}, bf16[512,128]{1,0:T(8,128)(2,1)S(1)}, u32[]{:S(2)}) copy-start(bf16[512,128]{1,0:T(8,128)(2,1)S(1)} %collective-permute-done.2) | copy-start | bytes 393220
  25.4 6.2 %collective-permute-start.22 = (bf16[512,128]{1,0:T(8,128)(2,1)S(1)}, bf16[512,128]{1,0:T(8,128)(2,1)S(1)}, u32[]{:S(2)}, u32[]{:S(2)}) collective-permute-start(bf16[512,128]{1,0:T(8,128)(2,1)S(1)} %collective-permute-done.20), channel_id=1, source_target_pairs={{0,4},{4,0},{8,12},{12,8},{16,20},{20,16},{24,28},{28,24},{1,5},{5... | collective-permute-start | bytes 393224 | tf_op jit(solution)/shard_map/ppermute | solution.py:26
  29.2 24.8 %copy-start.10 = (bf16[512,128]{1,0:T(8,128)(2,1)}, bf16[512,128]{1,0:T(8,128)(2,1)S(1)}, u32[]{:S(2)}) copy-start(bf16[512,128]{1,0:T(8,128)(2,1)S(1)} %collective-permute-done.21) | copy-start | bytes 393220
  29.2 14.3 %collective-permute-start.41 = (bf16[512,128]{1,0:T(8,128)(2,1)S(1)}, bf16[512,128]{1,0:T(8,128)(2,1)S(1)}, u32[]{:S(2)}, u32[]{:S(2)}) collective-permute-start(bf16[512,128]{1,0:T(8,128)(2,1)S(1)} %get-tuple-element.5), channel_id=1, source_target_pairs={{0,4},{4,0},{8,12},{12,8},{16,20},{20,16},{24,28},{28,24},{1,5},{5... | collective-permute-start | bytes 393224 | tf_op jit(solution)/shard_map/ppermute | solution.py:26
  30.0 24.0 %copy-start.8 = (bf16[512,128]{1,0:T(8,128)(2,1)}, bf16[512,128]{1,0:T(8,128)(2,1)S(1)}, u32[]{:S(2)}) copy-start(bf16[512,128]{1,0:T(8,128)(2,1)S(1)} %collective-permute-done.10) | copy-start | bytes 393220
  30.0 7.6 %collective-permute-start.30 = (bf16[512,128]{1,0:T(8,128)(2,1)S(1)}, bf16[512,128]{1,0:T(8,128)(2,1)S(1)}, u32[]{:S(2)}, u32[]{:S(2)}) collective-permute-start(bf16[512,128]{1,0:T(8,128)(2,1)S(1)} %get-tuple-element.6), channel_id=1, source_target_pairs={{0,16},{4,20},{8,24},{12,28},{16,0},{20,4},{24,8},{28,12},{1,17},{... | collective-permute-start | bytes 393224 | tf_op jit(solution)/shard_map/ppermute | solution.py:26
  31.6 7.3 %collective-permute-start.12 = (bf16[512,128]{1,0:T(8,128)(2,1)S(1)}, bf16[512,128]{1,0:T(8,128)(2,1)S(1)}, u32[]{:S(2)}, u32[]{:S(2)}) collective-permute-start(bf16[512,128]{1,0:T(8,128)(2,1)S(1)} %collective-permute-done.10), channel_id=1, source_target_pairs={{0,4},{4,0},{8,12},{12,8},{16,20},{20,16},{24,28},{28,24},{1,5},{5... | collective-permute-start | bytes 393224 | tf_op jit(solution)/shard_map/ppermute | solution.py:26
  35.6 18.4 %copy-start.21 = (bf16[512,128]{1,0:T(8,128)(2,1)}, bf16[512,128]{1,0:T(8,128)(2,1)S(1)}, u32[]{:S(2)}) copy-start(bf16[512,128]{1,0:T(8,128)(2,1)S(1)} %collective-permute-done.11) | copy-start | bytes 393220
  35.6 13.1 %collective-permute-start.31 = (bf16[512,128]{1,0:T(8,128)(2,1)S(1)}, bf16[512,128]{1,0:T(8,128)(2,1)S(1)}, u32[]{:S(2)}, u32[]{:S(2)}) collective-permute-start(bf16[512,128]{1,0:T(8,128)(2,1)S(1)} %get-tuple-element.6), channel_id=1, source_target_pairs={{0,4},{4,0},{8,12},{12,8},{16,20},{20,16},{24,28},{28,24},{1,5},{5... | collective-permute-start | bytes 393224 | tf_op jit(solution)/shard_map/ppermute | solution.py:26
  36.9 17.1 %copy-start.14 = (bf16[512,128]{1,0:T(8,128)(2,1)}, bf16[512,128]{1,0:T(8,128)(2,1)S(1)}, u32[]{:S(2)}) copy-start(bf16[512,128]{1,0:T(8,128)(2,1)S(1)} %collective-permute-done.40) | copy-start | bytes 393220
  36.9 7.3 %collective-permute-start.42 = (bf16[512,128]{1,0:T(8,128)(2,1)S(1)}, bf16[512,128]{1,0:T(8,128)(2,1)S(1)}, u32[]{:S(2)}, u32[]{:S(2)}) collective-permute-start(bf16[512,128]{1,0:T(8,128)(2,1)S(1)} %collective-permute-done.40), channel_id=1, source_target_pairs={{0,4},{4,0},{8,12},{12,8},{16,20},{20,16},{24,28},{28,24},{1,5},{5... | collective-permute-start | bytes 393224 | tf_op jit(solution)/shard_map/ppermute | solution.py:26
  37.7 16.3 %copy-start.16 = (bf16[512,128]{1,0:T(8,128)(2,1)}, bf16[512,128]{1,0:T(8,128)(2,1)S(1)}, u32[]{:S(2)}) copy-start(bf16[512,128]{1,0:T(8,128)(2,1)S(1)} %collective-permute-done.30) | copy-start | bytes 393220
  37.7 11.7 %collective-permute-start.32 = (bf16[512,128]{1,0:T(8,128)(2,1)S(1)}, bf16[512,128]{1,0:T(8,128)(2,1)S(1)}, u32[]{:S(2)}, u32[]{:S(2)}) collective-permute-start(bf16[512,128]{1,0:T(8,128)(2,1)S(1)} %collective-permute-done.30), channel_id=1, source_target_pairs={{0,4},{4,0},{8,12},{12,8},{16,20},{20,16},{24,28},{28,24},{1,5},{5... | collective-permute-start | bytes 393224 | tf_op jit(solution)/shard_map/ppermute | solution.py:26
  38.9 15.1 %copy-start.26 = (bf16[512,128]{1,0:T(8,128)(2,1)}, bf16[512,128]{1,0:T(8,128)(2,1)S(1)}, u32[]{:S(2)}) copy-start(bf16[512,128]{1,0:T(8,128)(2,1)S(1)} %collective-permute-done.12) | copy-start | bytes 393220
  38.9 15.0 %collective-permute-start.3 = (bf16[512,128]{1,0:T(8,128)(2,1)S(1)}, bf16[512,128]{1,0:T(8,128)(2,1)S(1)}, u32[]{:S(2)}, u32[]{:S(2)}) collective-permute-start(bf16[512,128]{1,0:T(8,128)(2,1)S(1)} %fusion.24), channel_id=1, source_target_pairs={{0,8},{4,12},{8,0},{12,4},{16,24},{20,28},{24,16},{28,20},{1,9},{5... | collective-permute-start | bytes 393224 | tf_op jit(solution)/shard_map/ppermute | solution.py:26
  43.5 10.5 %copy-start.18 = (bf16[512,128]{1,0:T(8,128)(2,1)}, bf16[512,128]{1,0:T(8,128)(2,1)S(1)}, u32[]{:S(2)}) copy-start(bf16[512,128]{1,0:T(8,128)(2,1)S(1)} %collective-permute-done.41) | copy-start | bytes 393220
  43.5 19.1 %collective-permute-start.23 = (bf16[512,128]{1,0:T(8,128)(2,1)}, bf16[512,128]{1,0:T(8,128)(2,1)}, u32[]{:S(2)}, u32[]{:S(2)}) collective-permute-start(bf16[512,128]{1,0:T(8,128)(2,1)} %fusion.42), channel_id=1, source_target_pairs={{0,8},{4,12},{8,0},{12,4},{16,24},{20,28},{24,16},{28,20},{1,9},{5... | collective-permute-start | bytes 393224 | tf_op jit(solution)/shard_map/ppermute | solution.py:26
  44.1 26.2 %collective-permute-start.13 = (bf16[512,128]{1,0:T(8,128)(2,1)}, bf16[512,128]{1,0:T(8,128)(2,1)}, u32[]{:S(2)}, u32[]{:S(2)}) collective-permute-start(bf16[512,128]{1,0:T(8,128)(2,1)} %fusion.33), channel_id=1, source_target_pairs={{0,8},{4,12},{8,0},{12,4},{16,24},{20,28},{24,16},{28,20},{1,9},{5... | collective-permute-start | bytes 393224 | tf_op jit(solution)/shard_map/ppermute | solution.py:26
  48.7 37.8 %collective-permute-start.43 = (bf16[512,128]{1,0:T(8,128)(2,1)}, bf16[512,128]{1,0:T(8,128)(2,1)}, u32[]{:S(2)}, u32[]{:S(2)}) collective-permute-start(bf16[512,128]{1,0:T(8,128)(2,1)} %fusion.60), channel_id=1, source_target_pairs={{0,8},{4,12},{8,0},{12,4},{16,24},{20,28},{24,16},{28,20},{1,9},{5... | collective-permute-start | bytes 393224 | tf_op jit(solution)/shard_map/ppermute | solution.py:26
  52.5 38.3 %collective-permute-start.33 = (bf16[512,128]{1,0:T(8,128)(2,1)}, bf16[512,128]{1,0:T(8,128)(2,1)}, u32[]{:S(2)}, u32[]{:S(2)}) collective-permute-start(bf16[512,128]{1,0:T(8,128)(2,1)} %fusion.51), channel_id=1, source_target_pairs={{0,8},{4,12},{8,0},{12,4},{16,24},{20,28},{24,16},{28,20},{1,9},{5... | collective-permute-start | bytes 393224 | tf_op jit(solution)/shard_map/ppermute | solution.py:26
  62.6 46.3 %collective-permute-start.4 = (bf16[2,512,128]{2,1,0:T(8,128)(2,1)}, bf16[2,512,128]{2,1,0:T(8,128)(2,1)}, u32[]{:S(2)}, u32[]{:S(2)}) collective-permute-start(bf16[2,512,128]{2,1,0:T(8,128)(2,1)} %bitcast.15), channel_id=1, source_target_pairs={{0,1},{1,0},{2,3},{3,2},{4,5},{5,4},{6,7},{7,6},{8,9},{9,8},{10,11... | collective-permute-start | bytes 786440 | tf_op jit(solution)/shard_map/ppermute | solution.py:26
  82.2 29.4 %collective-permute-start.14 = (bf16[2,512,128]{2,1,0:T(8,128)(2,1)}, bf16[2,512,128]{2,1,0:T(8,128)(2,1)}, u32[]{:S(2)}, u32[]{:S(2)}) collective-permute-start(bf16[2,512,128]{2,1,0:T(8,128)(2,1)} %bitcast.26), channel_id=1, source_target_pairs={{0,1},{1,0},{2,3},{3,2},{4,5},{5,4},{6,7},{7,6},{8,9},{9,8},{10,11... | collective-permute-start | bytes 786440 | tf_op jit(solution)/shard_map/ppermute | solution.py:26
  86.5 26.7 %collective-permute-start.24 = (bf16[2,512,128]{2,1,0:T(8,128)(2,1)}, bf16[2,512,128]{2,1,0:T(8,128)(2,1)}, u32[]{:S(2)}, u32[]{:S(2)}) collective-permute-start(bf16[2,512,128]{2,1,0:T(8,128)(2,1)} %bitcast.30), channel_id=1, source_target_pairs={{0,1},{1,0},{2,3},{3,2},{4,5},{5,4},{6,7},{7,6},{8,9},{9,8},{10,11... | collective-permute-start | bytes 786440 | tf_op jit(solution)/shard_map/ppermute | solution.py:26
  101.6 10.0 %copy-start.5 = (bf16[2,1,512,128]{3,2,0,1:T(8,128)(2,1)S(1)}, bf16[2,1,512,128]{3,2,0,1:T(8,128)(2,1)}, u32[]{:S(2)}) copy-start(bf16[2,1,512,128]{3,2,0,1:T(8,128)(2,1)} %copy.16) | copy-start | bytes 786436
  103.5 12.3 %collective-permute-start.34 = (bf16[2,512,128]{2,1,0:T(8,128)(2,1)}, bf16[2,512,128]{2,1,0:T(8,128)(2,1)}, u32[]{:S(2)}, u32[]{:S(2)}) collective-permute-start(bf16[2,512,128]{2,1,0:T(8,128)(2,1)} %bitcast.85), channel_id=1, source_target_pairs={{0,1},{1,0},{2,3},{3,2},{4,5},{5,4},{6,7},{7,6},{8,9},{9,8},{10,11... | collective-permute-start | bytes 786440 | tf_op jit(solution)/shard_map/ppermute | solution.py:26
  107.8 9.7 %collective-permute-start.44 = (bf16[2,512,128]{2,1,0:T(8,128)(2,1)}, bf16[2,512,128]{2,1,0:T(8,128)(2,1)}, u32[]{:S(2)}, u32[]{:S(2)}) collective-permute-start(bf16[2,512,128]{2,1,0:T(8,128)(2,1)} %bitcast.84), channel_id=1, source_target_pairs={{0,1},{1,0},{2,3},{3,2},{4,5},{5,4},{6,7},{7,6},{8,9},{9,8},{10,11... | collective-permute-start | bytes 786440 | tf_op jit(solution)/shard_map/ppermute | solution.py:26
  110.0 10.1 %collective-permute-start.5 = (bf16[1,512,128]{2,1,0:T(8,128)(2,1)S(1)}, bf16[1,512,128]{2,1,0:T(8,128)(2,1)S(1)}, u32[]{:S(2)}, u32[]{:S(2)}) collective-permute-start(bf16[1,512,128]{2,1,0:T(8,128)(2,1)S(1)} %constant_dynamic-slice_fusion.12), channel_id=1, source_target_pairs={{0,2},{1,3},{2,0},{3,1},{4,6},{5,7},{6,4},{7,5},{8,10},{9,11},{10,... | collective-permute-start | bytes 393224 | tf_op jit(solution)/shard_map/ppermute | solution.py:26
  112.6 8.3 %collective-permute-start.15 = (bf16[1,512,128]{2,1,0:T(8,128)(2,1)S(1)}, bf16[1,512,128]{2,1,0:T(8,128)(2,1)S(1)}, u32[]{:S(2)}, u32[]{:S(2)}) collective-permute-start(bf16[1,512,128]{2,1,0:T(8,128)(2,1)S(1)} %constant_dynamic-slice_fusion.9), channel_id=1, source_target_pairs={{0,2},{1,3},{2,0},{3,1},{4,6},{5,7},{6,4},{7,5},{8,10},{9,11},{10,... | collective-permute-start | bytes 393224 | tf_op jit(solution)/shard_map/ppermute | solution.py:26
  114.3 8.1 %collective-permute-start.25 = (bf16[1,512,128]{2,1,0:T(8,128)(2,1)S(1)}, bf16[1,512,128]{2,1,0:T(8,128)(2,1)S(1)}, u32[]{:S(2)}, u32[]{:S(2)}) collective-permute-start(bf16[1,512,128]{2,1,0:T(8,128)(2,1)S(1)} %constant_dynamic-slice_fusion.6), channel_id=1, source_target_pairs={{0,2},{1,3},{2,0},{3,1},{4,6},{5,7},{6,4},{7,5},{8,10},{9,11},{10,... | collective-permute-start | bytes 393224 | tf_op jit(solution)/shard_map/ppermute | solution.py:26
  116.9 7.9 %collective-permute-start.35 = (bf16[1,512,128]{2,1,0:T(8,128)(2,1)S(1)}, bf16[1,512,128]{2,1,0:T(8,128)(2,1)S(1)}, u32[]{:S(2)}, u32[]{:S(2)}) collective-permute-start(bf16[1,512,128]{2,1,0:T(8,128)(2,1)S(1)} %constant_dynamic-slice_fusion.3), channel_id=1, source_target_pairs={{0,2},{1,3},{2,0},{3,1},{4,6},{5,7},{6,4},{7,5},{8,10},{9,11},{10,... | collective-permute-start | bytes 393224 | tf_op jit(solution)/shard_map/ppermute | solution.py:26
  118.5 8.7 %collective-permute-start.45 = (bf16[1,512,128]{2,1,0:T(8,128)(2,1)S(1)}, bf16[1,512,128]{2,1,0:T(8,128)(2,1)S(1)}, u32[]{:S(2)}, u32[]{:S(2)}) collective-permute-start(bf16[1,512,128]{2,1,0:T(8,128)(2,1)S(1)} %constant_dynamic-slice_fusion), channel_id=1, source_target_pairs={{0,2},{1,3},{2,0},{3,1},{4,6},{5,7},{6,4},{7,5},{8,10},{9,11},{10,... | collective-permute-start | bytes 393224 | tf_op jit(solution)/shard_map/ppermute | solution.py:26
  120.2 7.8 %collective-permute-start.6 = (bf16[512,128]{1,0:T(8,128)(2,1)S(1)}, bf16[512,128]{1,0:T(8,128)(2,1)S(1)}, u32[]{:S(2)}, u32[]{:S(2)}) collective-permute-start(bf16[512,128]{1,0:T(8,128)(2,1)S(1)} %fusion.116), channel_id=1, source_target_pairs={{0,8},{4,12},{8,0},{12,4},{16,24},{20,28},{24,16},{28,20},{1,9},{5... | collective-permute-start | bytes 393224 | tf_op jit(solution)/shard_map/ppermute | solution.py:26
  120.9 9.7 %collective-permute-start.16 = (bf16[512,128]{1,0:T(8,128)(2,1)S(1)}, bf16[512,128]{1,0:T(8,128)(2,1)S(1)}, u32[]{:S(2)}, u32[]{:S(2)}) collective-permute-start(bf16[512,128]{1,0:T(8,128)(2,1)S(1)} %fusion.117), channel_id=1, source_target_pairs={{0,8},{4,12},{8,0},{12,4},{16,24},{20,28},{24,16},{28,20},{1,9},{5... | collective-permute-start | bytes 393224 | tf_op jit(solution)/shard_map/ppermute | solution.py:26
  122.4 10.4 %collective-permute-start.26 = (bf16[512,128]{1,0:T(8,128)(2,1)S(1)}, bf16[512,128]{1,0:T(8,128)(2,1)S(1)}, u32[]{:S(2)}, u32[]{:S(2)}) collective-permute-start(bf16[512,128]{1,0:T(8,128)(2,1)S(1)} %fusion.118), channel_id=1, source_target_pairs={{0,8},{4,12},{8,0},{12,4},{16,24},{20,28},{24,16},{28,20},{1,9},{5... | collective-permute-start | bytes 393224 | tf_op jit(solution)/shard_map/ppermute | solution.py:26
  124.8 10.8 %collective-permute-start.36 = (bf16[512,128]{1,0:T(8,128)(2,1)S(1)}, bf16[512,128]{1,0:T(8,128)(2,1)S(1)}, u32[]{:S(2)}, u32[]{:S(2)}) collective-permute-start(bf16[512,128]{1,0:T(8,128)(2,1)S(1)} %fusion.119), channel_id=1, source_target_pairs={{0,8},{4,12},{8,0},{12,4},{16,24},{20,28},{24,16},{28,20},{1,9},{5... | collective-permute-start | bytes 393224 | tf_op jit(solution)/shard_map/ppermute | solution.py:26
  127.2 10.6 %collective-permute-start.46 = (bf16[512,128]{1,0:T(8,128)(2,1)S(1)}, bf16[512,128]{1,0:T(8,128)(2,1)S(1)}, u32[]{:S(2)}, u32[]{:S(2)}) collective-permute-start(bf16[512,128]{1,0:T(8,128)(2,1)S(1)} %fusion.120), channel_id=1, source_target_pairs={{0,8},{4,12},{8,0},{12,4},{16,24},{20,28},{24,16},{28,20},{1,9},{5... | collective-permute-start | bytes 393224 | tf_op jit(solution)/shard_map/ppermute | solution.py:26
  129.2 11.1 %collective-permute-start.8 = (bf16[512,128]{1,0:T(8,128)(2,1)S(1)}, bf16[512,128]{1,0:T(8,128)(2,1)S(1)}, u32[]{:S(2)}, u32[]{:S(2)}) collective-permute-start(bf16[512,128]{1,0:T(8,128)(2,1)S(1)} %fusion.71), channel_id=1, source_target_pairs={{0,4},{4,0},{8,12},{12,8},{16,20},{20,16},{24,28},{28,24},{1,5},{5... | collective-permute-start | bytes 393224 | tf_op jit(solution)/shard_map/ppermute | solution.py:26
  132.0 12.6 %collective-permute-start.18 = (bf16[512,128]{1,0:T(8,128)(2,1)S(1)}, bf16[512,128]{1,0:T(8,128)(2,1)S(1)}, u32[]{:S(2)}, u32[]{:S(2)}) collective-permute-start(bf16[512,128]{1,0:T(8,128)(2,1)S(1)} %fusion.82), channel_id=1, source_target_pairs={{0,4},{4,0},{8,12},{12,8},{16,20},{20,16},{24,28},{28,24},{1,5},{5... | collective-permute-start | bytes 393224 | tf_op jit(solution)/shard_map/ppermute | solution.py:26
  134.1 13.9 %collective-permute-start.28 = (bf16[512,128]{1,0:T(8,128)(2,1)S(1)}, bf16[512,128]{1,0:T(8,128)(2,1)S(1)}, u32[]{:S(2)}, u32[]{:S(2)}) collective-permute-start(bf16[512,128]{1,0:T(8,128)(2,1)S(1)} %fusion.93), channel_id=1, source_target_pairs={{0,4},{4,0},{8,12},{12,8},{16,20},{20,16},{24,28},{28,24},{1,5},{5... | collective-permute-start | bytes 393224 | tf_op jit(solution)/shard_map/ppermute | solution.py:26
  136.9 14.9 %collective-permute-start.38 = (bf16[512,128]{1,0:T(8,128)(2,1)S(1)}, bf16[512,128]{1,0:T(8,128)(2,1)S(1)}, u32[]{:S(2)}, u32[]{:S(2)}) collective-permute-start(bf16[512,128]{1,0:T(8,128)(2,1)S(1)} %fusion.104), channel_id=1, source_target_pairs={{0,4},{4,0},{8,12},{12,8},{16,20},{20,16},{24,28},{28,24},{1,5},{5... | collective-permute-start | bytes 393224 | tf_op jit(solution)/shard_map/ppermute | solution.py:26
  139.2 16.3 %collective-permute-start.48 = (bf16[512,128]{1,0:T(8,128)(2,1)S(1)}, bf16[512,128]{1,0:T(8,128)(2,1)S(1)}, u32[]{:S(2)}, u32[]{:S(2)}) collective-permute-start(bf16[512,128]{1,0:T(8,128)(2,1)S(1)} %fusion.115), channel_id=1, source_target_pairs={{0,4},{4,0},{8,12},{12,8},{16,20},{20,16},{24,28},{28,24},{1,5},{5... | collective-permute-start | bytes 393224 | tf_op jit(solution)/shard_map/ppermute | solution.py:26
  142.8 16.9 %collective-permute-start.9 = (bf16[512,128]{1,0:T(8,128)(2,1)S(1)}, bf16[512,128]{1,0:T(8,128)(2,1)S(1)}, u32[]{:S(2)}, u32[]{:S(2)}) collective-permute-start(bf16[512,128]{1,0:T(8,128)(2,1)S(1)} %get-tuple-element.29), channel_id=1, source_target_pairs={{0,16},{4,20},{8,24},{12,28},{16,0},{20,4},{24,8},{28,12},{1,17},{... | collective-permute-start | bytes 393224 | tf_op jit(solution)/shard_map/ppermute | solution.py:26
  144.6 16.1 %collective-permute-start.7 = (bf16[512,128]{1,0:T(8,128)(2,1)S(1)}, bf16[512,128]{1,0:T(8,128)(2,1)S(1)}, u32[]{:S(2)}, u32[]{:S(2)}) collective-permute-start(bf16[512,128]{1,0:T(8,128)(2,1)S(1)} %get-tuple-element.28), channel_id=1, source_target_pairs={{0,4},{4,0},{8,12},{12,8},{16,20},{20,16},{24,28},{28,24},{1,5},{5... | collective-permute-start | bytes 393224 | tf_op jit(solution)/shard_map/ppermute | solution.py:26
  148.0 15.3 %collective-permute-start.19 = (bf16[512,128]{1,0:T(8,128)(2,1)S(1)}, bf16[512,128]{1,0:T(8,128)(2,1)S(1)}, u32[]{:S(2)}, u32[]{:S(2)}) collective-permute-start(bf16[512,128]{1,0:T(8,128)(2,1)S(1)} %get-tuple-element.27), channel_id=1, source_target_pairs={{0,16},{4,20},{8,24},{12,28},{16,0},{20,4},{24,8},{28,12},{1,17},{... | collective-permute-start | bytes 393224 | tf_op jit(solution)/shard_map/ppermute | solution.py:26
  151.8 12.7 %collective-permute-start.17 = (bf16[512,128]{1,0:T(8,128)(2,1)S(1)}, bf16[512,128]{1,0:T(8,128)(2,1)S(1)}, u32[]{:S(2)}, u32[]{:S(2)}) collective-permute-start(bf16[512,128]{1,0:T(8,128)(2,1)S(1)} %get-tuple-element.26), channel_id=1, source_target_pairs={{0,4},{4,0},{8,12},{12,8},{16,20},{20,16},{24,28},{28,24},{1,5},{5... | collective-permute-start | bytes 393224 | tf_op jit(solution)/shard_map/ppermute | solution.py:26
  155.5 12.8 %collective-permute-start.29 = (bf16[512,128]{1,0:T(8,128)(2,1)S(1)}, bf16[512,128]{1,0:T(8,128)(2,1)S(1)}, u32[]{:S(2)}, u32[]{:S(2)}) collective-permute-start(bf16[512,128]{1,0:T(8,128)(2,1)S(1)} %get-tuple-element.25), channel_id=1, source_target_pairs={{0,16},{4,20},{8,24},{12,28},{16,0},{20,4},{24,8},{28,12},{1,17},{... | collective-permute-start | bytes 393224 | tf_op jit(solution)/shard_map/ppermute | solution.py:26
  159.7 8.9 %collective-permute-start.27 = (bf16[512,128]{1,0:T(8,128)(2,1)S(1)}, bf16[512,128]{1,0:T(8,128)(2,1)S(1)}, u32[]{:S(2)}, u32[]{:S(2)}) collective-permute-start(bf16[512,128]{1,0:T(8,128)(2,1)S(1)} %get-tuple-element.24), channel_id=1, source_target_pairs={{0,4},{4,0},{8,12},{12,8},{16,20},{20,16},{24,28},{28,24},{1,5},{5... | collective-permute-start | bytes 393224 | tf_op jit(solution)/shard_map/ppermute | solution.py:26
  160.7 11.8 %collective-permute-start.39 = (bf16[512,128]{1,0:T(8,128)(2,1)S(1)}, bf16[512,128]{1,0:T(8,128)(2,1)S(1)}, u32[]{:S(2)}, u32[]{:S(2)}) collective-permute-start(bf16[512,128]{1,0:T(8,128)(2,1)S(1)} %get-tuple-element.23), channel_id=1, source_target_pairs={{0,16},{4,20},{8,24},{12,28},{16,0},{20,4},{24,8},{28,12},{1,17},{... | collective-permute-start | bytes 393224 | tf_op jit(solution)/shard_map/ppermute | solution.py:26
  163.3 9.2 %collective-permute-start.37 = (bf16[512,128]{1,0:T(8,128)(2,1)S(1)}, bf16[512,128]{1,0:T(8,128)(2,1)S(1)}, u32[]{:S(2)}, u32[]{:S(2)}) collective-permute-start(bf16[512,128]{1,0:T(8,128)(2,1)S(1)} %get-tuple-element.22), channel_id=1, source_target_pairs={{0,4},{4,0},{8,12},{12,8},{16,20},{20,16},{24,28},{28,24},{1,5},{5... | collective-permute-start | bytes 393224 | tf_op jit(solution)/shard_map/ppermute | solution.py:26
  164.5 9.5 %collective-permute-start.49 = (bf16[512,128]{1,0:T(8,128)(2,1)S(1)}, bf16[512,128]{1,0:T(8,128)(2,1)S(1)}, u32[]{:S(2)}, u32[]{:S(2)}) collective-permute-start(bf16[512,128]{1,0:T(8,128)(2,1)S(1)} %get-tuple-element.21), channel_id=1, source_target_pairs={{0,16},{4,20},{8,24},{12,28},{16,0},{20,4},{24,8},{28,12},{1,17},{... | collective-permute-start | bytes 393224 | tf_op jit(solution)/shard_map/ppermute | solution.py:26
  168.3 5.7 %collective-permute-start.47 = (bf16[512,128]{1,0:T(8,128)(2,1)S(1)}, bf16[512,128]{1,0:T(8,128)(2,1)S(1)}, u32[]{:S(2)}, u32[]{:S(2)}) collective-permute-start(bf16[512,128]{1,0:T(8,128)(2,1)S(1)} %get-tuple-element.20), channel_id=1, source_target_pairs={{0,4},{4,0},{8,12},{12,8},{16,20},{20,16},{24,28},{28,24},{1,5},{5... | collective-permute-start | bytes 393224 | tf_op jit(solution)/shard_map/ppermute | solution.py:26
  (14 other events, 84.1 us)

commit v2 on v0

v2 whole, which is shorter than its diff:
```python
import functools
import heapq

import jax
import jax.numpy as jnp
from jax import lax
from jax.experimental import pallas as pl
from jax.experimental.pallas import tpu as pltpu
from jax.sharding import PartitionSpec as P

F32 = jnp.float32
BF16 = jnp.bfloat16
SLAB = 64
MATMUL_ROWS = 256
VMEM_LIMIT = 16 * 1024 * 1024
PERIOD = 5.2
EARLY = 3.5
AFTER_FAR = 6.5
AFTER_CORNER = 5.5
AFTER_PARTIAL = 5.2
AFTER_CORE = 2.0
AFTER_ROW = 4.0
AFTER_LAST = 4.2

smem = pl.BlockSpec(memory_space=pltpu.SMEM)
vmem = pl.BlockSpec(memory_space=pltpu.VMEM)
unread = pl.BlockSpec(memory_space=pl.ANY)


def chunk_bounds(columns):
    width = 128 if columns % 128 == 0 else columns
    return [(lo, width) for lo in range(0, columns, width)]


class Chain:
    def __init__(self):
        self.token = []

    def call(self, kernel, name, out_shape, scalars, arrays, scratch=(), out_specs=None, whole=(), aliases=None):
        count = len(scalars) + len(arrays) + len(whole)
        tokens = len(self.token)

        def body(*refs):
            kernel(*refs[:count], *refs[count + tokens:count + tokens + len(out_shape)], *refs[count + tokens + len(out_shape) + 1:])

        *outs, token = pl.pallas_call(
            body, name=name, out_shape=[*out_shape, jax.ShapeDtypeStruct((8, 128), F32)],
            in_specs=[smem] * len(scalars) + [vmem] * len(arrays) + [unread] * (len(whole) + tokens),
            out_specs=[*(out_specs or [vmem] * len(out_shape)), unread],
            scratch_shapes=list(scratch),
            input_output_aliases=aliases or {},
            compiler_params=pltpu.CompilerParams(vmem_limit_bytes=VMEM_LIMIT),
            cost_estimate=pl.CostEstimate(flops=0, transcendentals=0, bytes_accessed=0),
        )(*scalars, *arrays, *whole, *self.token)
        self.token = [token]
        return outs

    def pin(self, *arrays):
        return self.call(
            lambda *refs: None, "pin", [like(a) for a in arrays], [], [], out_specs=[unread] * len(arrays), whole=arrays,
            aliases={i: i for i in range(len(arrays))})


def like(array):
    return jax.ShapeDtypeStruct(array.shape, array.dtype)


def slabs(rows, body, step=SLAB):
    step = step if rows % step == 0 else rows

    @pl.loop(0, rows // step)
    def _(i):
        body(pl.ds(pl.multiple_of(i * step, step), step))


def masked(total, at, left):
    row = lax.broadcasted_iota(jnp.int32, total.shape, 0) + at.start
    return jnp.where(row < left, total, 0.0).astype(BF16)


def mask_chunk(chain, place, block_rows, own, lo, width):
    rows = own.shape[0]

    def kernel(place_ref, length_ref, own_ref, out_ref):
        left = length_ref[0] - place_ref[1] * rows

        def body(at):
            out_ref[at, :] = masked(own_ref[at, lo:lo + width].astype(F32), at, left)

        slabs(rows, body)

    return chain.call(kernel, "mask_chunk", [jax.ShapeDtypeStruct((rows, width), BF16)], [place, block_rows], [own])[0]


def mixed(matrix_ref, c, held, at, target, transposed):
    total = None
    for source, ref in held:
        t, m = c ^ target, c ^ source
        weight = matrix_ref[m, t] if transposed else matrix_ref[t, m]
        term = ref[at, :].astype(F32) * weight
        total = term if total is None else total + term
    return total


def stacked(count, rows, width):
    return jax.ShapeDtypeStruct((count, rows, width), BF16)


def mix(chain, place, matrix, held, targets, received, transposed):
    rows, width = held[0][1].shape

    def kernel(place_ref, matrix_ref, *refs):
        held_refs = [(m, ref) for (m, _), ref in zip(held, refs)]
        received_refs = refs[len(held):-1]
        out_ref = refs[-1]

        def body(at):
            for i, t in enumerate(targets):
                total = mixed(matrix_ref, place_ref[0], held_refs, at, t, transposed)
                for (_, names), ref in zip(received, received_refs):
                    if t in names:
                        total = total + ref[names.index(t), at, :].astype(F32)
                out_ref[i, at, :] = total.astype(BF16)

        slabs(rows, body)

    arrays = [b for _, b in held] + [r for r, _ in received]
    return chain.call(kernel, "mix", [stacked(len(targets), rows, width)], [place, matrix], arrays)[0]


def mix_multiply(chain, place, matrix, held, received, weights, sent, kept):
    rows, width = held[0][1].shape
    group = weights.shape[0] // (len(sent) + len(kept))

    def kernel(place_ref, matrix_ref, *refs):
        held_refs = [(m, ref) for (m, _), ref in zip(held, refs)]
        received_refs = refs[len(held):len(held) + len(received)]
        weights_ref, sent_ref, kept_ref, cross_ref = refs[len(held) + len(received):]

        def body(at):
            total = mixed(matrix_ref, place_ref[0], held_refs, at, 0, False)
            for ref in received_refs:
                total = total + ref[0, at, :].astype(F32)
            cross_ref[at, :] = total.astype(BF16)

        slabs(rows, body)
        for names, out_ref in ((sent, sent_ref), (kept, kept_ref)):
            for i, d in enumerate(names):
                base = (place_ref[1] ^ d) * group

                def rows_of(at):
                    from_row = pl.ds(pl.multiple_of(base + at.start, at.size), at.size)
                    out_ref[i, at, :] = jnp.dot(
                        weights_ref[from_row, :], cross_ref[...], preferred_element_type=F32).astype(BF16)

                slabs(group, rows_of, MATMUL_ROWS)

    arrays = [b for _, b in held] + received + [weights]
    outs = [stacked(len(sent), group, width), stacked(len(kept), group, width)]
    return chain.call(kernel, "mix_multiply", outs, [place, matrix], arrays, scratch=[pltpu.VMEM((rows, width), BF16)])


def add_up(chain, stacks, targets):
    _, rows, width = stacks[0][0].shape

    def kernel(*refs):
        def body(at):
            for i, t in enumerate(targets):
                terms = [ref[names.index(t), at, :].astype(F32) for (_, names), ref in zip(stacks, refs) if t in names]
                refs[-1][i, at, :] = functools.reduce(lambda a, b: a + b, terms).astype(BF16)

        slabs(rows, body)

    return chain.call(kernel, "add_up", [stacked(len(targets), rows, width)], [], [s for s, _ in stacks])[0]


def finish(chain, place, matrix, block_rows, held, received, lo, columns, result):
    rows, width = held[0][1].shape

    def kernel(place_ref, matrix_ref, length_ref, *refs):
        left = length_ref[0] - place_ref[1] * rows
        held_refs = [(m, ref) for (m, _), ref in zip(held, refs)]
        received_refs = refs[len(held):len(held) + len(received)]
        out_ref, chunk_ref, done = refs[-3:]

        def body(at):
            total = mixed(matrix_ref, place_ref[0], held_refs, at, 0, True)
            for ref in received_refs:
                total = total + ref[0, at, :].astype(F32)
            chunk_ref[at, :] = masked(total, at, left)

        slabs(rows, body)
        copy = pltpu.make_async_copy(chunk_ref, out_ref.at[:, lo:lo + width], done)
        copy.start()
        copy.wait()

    arrays = [b for _, b in held] + received
    whole = [] if result is None else [result]
    return chain.call(
        kernel, "finish", [jax.ShapeDtypeStruct((rows, columns), BF16)], [place, matrix, block_rows], arrays,
        scratch=[pltpu.VMEM((rows, width), BF16), pltpu.SemaphoreType.DMA(())], out_specs=[unread],
        whole=whole, aliases={3 + len(arrays): 0} if whole else {})[0]


def solution(mesh):
    n_chan, n_row = mesh.shape["chan"], mesh.shape["row"]
    chan_bits = [1 << b for b in range(n_chan.bit_length() - 1)]
    row_bits = [1 << b for b in range(n_row.bit_length() - 1)]
    far, near = chan_bits[-1], chan_bits[0]
    reduce_bits = [b for b in reversed(chan_bits) if b not in (far, near)]

    def swap(x, axis, size, bit):
        return lax.ppermute(x, axis, [(i, i ^ bit) for i in range(size)])

    def on_device(amplitudes, block_rows, recoupling, interaction):
        rows, _, columns = amplitudes.shape
        place = jnp.stack([lax.axis_index("chan"), lax.axis_index("row")]).astype(jnp.int32)
        matrix = recoupling.astype(F32)
        own = amplitudes.reshape(rows, columns)
        weights = interaction.reshape(interaction.shape[0], interaction.shape[2])
        chain = Chain()
        result = None

        def recouple(block, transposed, last, after_partial):
            other = swap(block, "chan", n_chan, far)
            beside = swap(block, "chan", n_chan, near)
            yield AFTER_FAR
            other, beside = chain.pin(other, beside)
            corner = swap(other, "chan", n_chan, near)
            held = [(0, block), (far, other), (near, beside), (far ^ near, corner)]
            targets = [0]
            for bit in reduce_bits:
                targets = targets + [t ^ bit for t in targets]
            received = []
            yield AFTER_CORNER
            for bit in reduce_bits:
                sent = [t for t in targets if t & bit]
                targets = [t for t in targets if not t & bit]
                part = mix(chain, place, matrix, held, sent, received, transposed)
                received.append((swap(part, "chan", n_chan, bit), [t ^ bit for t in sent]))
                yield after_partial
            return last(held, [r for r, _ in received])

        def one_chunk(lo, width):
            block = mask_chunk(chain, place, block_rows, own, lo, width)
            bit = row_bits[0]
            sent = [d for d in range(n_row) if d & bit]
            targets = [d for d in range(n_row) if not d & bit]
            parts, kept = yield from recouple(
                block, False,
                lambda held, received: mix_multiply(chain, place, matrix, held, received, weights, sent, targets),
                AFTER_PARTIAL)
            stacks = [(kept, targets), (swap(parts, "row", n_row, bit), targets)]
            yield AFTER_CORE
            for bit in row_bits[1:]:
                sent = [d for d in targets if d & bit]
                targets = [d for d in targets if not d & bit]
                stacks.append((swap(add_up(chain, stacks, sent), "row", n_row, bit), targets))
                yield AFTER_ROW
            block = add_up(chain, stacks, targets)[0]

            def last(held, received):
                nonlocal result
                result = finish(chain, place, matrix, block_rows, held, received, lo, columns, result)

            yield from recouple(block, True, last, AFTER_LAST)

        queue = [(i * PERIOD - (EARLY if i else 0), i, one_chunk(lo, width)) for i, (lo, width) in enumerate(chunk_bounds(columns))]
        while queue:
            time, i, work = heapq.heappop(queue)
            wait = next(work, None)
            if wait is not None:
                heapq.heappush(queue, (max(time, i * PERIOD) + wait, i, work))
        return result.reshape(amplitudes.shape)

    return jax.shard_map(
        on_device,
        mesh=mesh,
        in_specs=(P("row", "chan", None), P("chan"), P(), P(None, "chan", "row")),
        out_specs=P("row", "chan", None),
        check_vma=False,
    )
```

time: 178 us -> 143 us (0.80)
  blocking collectives: 88.9 us -> 0 us
  starting transfers between devices: 0.01 us -> 43.6 us
  Pallas kernels: 0 us -> 31.7 us
  between operations: 14.3 us -> 1.26 us
  other arithmetic: 5.63 us -> 0.76 us
  matrix products: 4.12 us -> 0 us
  waiting for transfers between devices: 58.8 us -> 61.9 us
  local copies, waits for them, and re-layouts: 6.14 us -> 3.27 us
    all_to_all x4 -> x0, blocking collectives: 88.9 us -> none  [the longest x1 24.9 us: on_device(): lax.all_to_all(masked, 'chan', split_axis=0, concat_axis=1, tiled=True)]
    ppermute x0 -> x50, waiting for transfers between devices: none -> 61.9 us  [swap(): return lax.ppermute(x, axis, [(i, i ^ bit) for i in range(size)])]
    psum x1 -> x0, waiting for transfers between devices: 58.7 us -> none  [on_device(): lax.psum(full_terms.astype(jnp.bfloat16), 'row').astype(jnp.float32)]
    ppermute x0 -> x50, starting transfers between devices: none -> 43.6 us  [swap(): return lax.ppermute(x, axis, [(i, i ^ bit) for i in range(size)])]
    pallas_call x0 -> x45, Pallas kernels: none -> 31.7 us  [call(): pl.pallas_call(body, name=name, out_shape=[*out_shape, jax.ShapeDtypeStru...]
    dot_general x3 -> x0, matrix products: 4.12 us -> none  [the longest x1 3.13 us: on_device(): jnp.einsum('zmo,omu->zmu', interaction, crossing_row_set, preferred_eleme...]
    select_n x3 -> x0, other arithmetic: 3.36 us -> none  [the longest x2 2.36 us: on_device(): masked = jnp.where(row_valid_mask, amplitudes, zero)]
    unnamed x11 -> x10, local copies, waits for them, and re-layouts: 5.48 us -> 3.27 us
  transfers between devices with their start and end apart: 1 -> 50, of which waited for: 1 -> 28; matrix products, arithmetic and copies ran while one was open for 0% -> 0% of each run, Pallas kernels for 0% -> 10%
where the time goes in v2:
time: 143 us; the launch traced here: 142 us
  waiting for transfers between devices  61.9 us (43%)
  starting transfers between devices  43.6 us (30%)
  Pallas kernels  31.7 us (22%)
  local copies, waits for them, and re-layouts  3.27 us (2%)
    ppermute x50, waiting for transfers between devices, swap(): return lax.ppermute(x, axis, [(i, i ^ bit) for i in range(size)])  61.9 us
    ppermute x50, starting transfers between devices, swap(): return lax.ppermute(x, axis, [(i, i ^ bit) for i in range(size)])  43.6 us
    pallas_call x45, Pallas kernels, call(): pl.pallas_call(body, name=name, out_shape=[*out_shape, jax.ShapeDtypeStru...  31.7 us
    unnamed x10, local copies, waits for them, and re-layouts  3.27 us
  transfers between devices with their start and end apart: 50, of which 28 were waited for; matrix products, arithmetic and copies ran while one was open for 0% of the time, Pallas kernels for 10%

profile of v2, /device:TPU:0, one launch (start us, length us, event | category | flops | bytes accessed | tf_op | source)
XLA Modules:
  0.0 142.5 jit_solution(3959209208651351463)
XLA Ops:
  0.9 1.1 copy-done.1
  2.6 4.1 %collective-permute-start.2 = (bf16[512,128]{1,0:T(8,128)(2,1)S(1)}, bf16[512,128]{1,0:T(8,128)(2,1)S(1)}, u32[]{:S(2)}, u32[]{:S(2)}) collective-permute-start(bf16[512,128]{1,0:T(8,128)(2,1)S(1)} %get-tuple-element.111.refs_2_), channel_id=1, source_target_pairs={{0,16},{4,20},{8,24},{12,28},{16,0},{20,4},{24,8},{28,12},{1,17},{... | collective-permute-start | bytes 393224 | tf_op jit(solution)/shard_map/ppermute | solution.py:213
  6.7 1.5 %collective-permute-start.3 = (bf16[512,128]{1,0:T(8,128)(2,1)S(1)}, bf16[512,128]{1,0:T(8,128)(2,1)S(1)}, u32[]{:S(2)}, u32[]{:S(2)}) collective-permute-start(bf16[512,128]{1,0:T(8,128)(2,1)S(1)} %get-tuple-element.111.refs_2_), channel_id=1, source_target_pairs={{0,4},{4,0},{8,12},{12,8},{16,20},{20,16},{24,28},{28,24},{1,5},{5... | collective-permute-start | bytes 393224 | tf_op jit(solution)/shard_map/ppermute | solution.py:213
  9.5 7.1 %collective-permute-done.2.refs_0_ = bf16[512,128]{1,0:T(8,128)(2,1)S(1)} collective-permute-done((bf16[512,128]{1,0:T(8,128)(2,1)S(1)}, bf16[512,128]{1,0:T(8,128)(2,1)S(1)}, u32[]{:S(2)}, u32[]{:S(2)}) %collective-permute-start.2) | collective-permute-done | bytes 131104 | tf_op jit(solution)/shard_map/ppermute | solution.py:213
  16.6 1.8 %collective-permute-start.5 = (bf16[512,128]{1,0:T(8,128)(2,1)S(1)}, bf16[512,128]{1,0:T(8,128)(2,1)S(1)}, u32[]{:S(2)}, u32[]{:S(2)}) collective-permute-start(bf16[512,128]{1,0:T(8,128)(2,1)S(1)} %get-tuple-element.117.refs_3_), channel_id=1, source_target_pairs={{0,4},{4,0},{8,12},{12,8},{16,20},{20,16},{24,28},{28,24},{1,5},{5... | collective-permute-start | bytes 393224 | tf_op jit(solution)/shard_map/ppermute | solution.py:213
  19.2 1.1 copy-done.2
  21.2 1.4 collective-permute-done.5.refs_5_
  23.4 2.0 %collective-permute-start.6 = (bf16[1,512,128]{2,1,0:T(8,128)(2,1)S(1)}, bf16[1,512,128]{2,1,0:T(8,128)(2,1)S(1)}, u32[]{:S(2)}, u32[]{:S(2)}) collective-permute-start(bf16[1,512,128]{2,1,0:T(8,128)(2,1)S(1)} %get-tuple-element.120), channel_id=1, source_target_pairs={{0,8},{4,12},{8,0},{12,4},{16,24},{20,28},{24,16},{28,20},{1,9},{5... | collective-permute-start | bytes 393224 | tf_op jit(solution)/shard_map/ppermute | solution.py:213
  25.4 1.1 copy-done.3
  27.1 1.1 collective-permute-done.7.refs_0_
  28.2 1.3 collective-permute-done.6.refs_6_
  29.5 2.5 %mix_multiply.5 = (bf16[2,512,128]{2,1,0:T(8,128)(2,1)S(1)}, bf16[2,512,128]{2,1,0:T(8,128)(2,1)S(1)}, f32[8,128]{1,0:T(8,128)S(1)}) custom-call(s32[2]{0:T(128)S(1)} %pad_add_fusion.refs_0_, f32[8,8]{1,0:T(8,128)S(1)} %convert_element_type.3.refs_1_, bf16[512,128]{1,0:T(8,128)(2,1)S(1)} %get-tuple-element.111.refs_2_, ...), custom_call_target="tpu_custom_call" | custom-call | tf_op jit(solution)/shard_map/mix_multiply/pallas_call | solution.py:46
  32.2 1.5 %collective-permute-start.4 = (bf16[512,128]{1,0:T(8,128)(2,1)S(1)}, bf16[512,128]{1,0:T(8,128)(2,1)S(1)}, u32[]{:S(2)}, u32[]{:S(2)}) collective-permute-start(bf16[512,128]{1,0:T(8,128)(2,1)S(1)} %get-tuple-element.115.refs_3_), channel_id=1, source_target_pairs={{0,4},{4,0},{8,12},{12,8},{16,20},{20,16},{24,28},{28,24},{1,5},{5... | collective-permute-start | bytes 393224 | tf_op jit(solution)/shard_map/ppermute | solution.py:213
  33.6 0.8 collective-permute-start.12
  34.4 1.2 collective-permute-start.13
  35.6 2.9 %collective-permute-done.4.refs_5_ = bf16[512,128]{1,0:T(8,128)(2,1)S(1)} collective-permute-done((bf16[512,128]{1,0:T(8,128)(2,1)S(1)}, bf16[512,128]{1,0:T(8,128)(2,1)S(1)}, u32[]{:S(2)}, u32[]{:S(2)}) %collective-permute-start.4) | collective-permute-done | bytes 131104 | tf_op jit(solution)/shard_map/ppermute | solution.py:213
  40.5 2.5 %collective-permute-done.12.refs_0_ = bf16[512,128]{1,0:T(8,128)(2,1)S(1)} collective-permute-done((bf16[512,128]{1,0:T(8,128)(2,1)S(1)}, bf16[512,128]{1,0:T(8,128)(2,1)S(1)}, u32[]{:S(2)}, u32[]{:S(2)}) %collective-permute-start.12) | collective-permute-done | bytes 131104 | tf_op jit(solution)/shard_map/ppermute | solution.py:213
  43.0 2.7 %collective-permute-done.11.refs_6_ = bf16[1,512,128]{2,1,0:T(8,128)(2,1)S(1)} collective-permute-done((bf16[1,512,128]{2,1,0:T(8,128)(2,1)S(1)}, bf16[1,512,128]{2,1,0:T(8,128)(2,1)S(1)}, u32[]{:S(2)}, u32[]{:S(2)}) %collective-permute-start.11) | collective-permute-done | bytes 131104 | tf_op jit(solution)/shard_map/ppermute | solution.py:213
  45.7 2.5 %mix_multiply.6 = (bf16[2,512,128]{2,1,0:T(8,128)(2,1)S(1)}, bf16[2,512,128]{2,1,0:T(8,128)(2,1)S(1)}, f32[8,128]{1,0:T(8,128)S(1)}) custom-call(s32[2]{0:T(128)S(1)} %pad_add_fusion.refs_0_, f32[8,8]{1,0:T(8,128)S(1)} %convert_element_type.3.refs_1_, bf16[512,128]{1,0:T(8,128)(2,1)S(1)} %get-tuple-element.110.refs_2_, ...), custom_call_target="tpu_custom_call" | custom-call | tf_op jit(solution)/shard_map/mix_multiply/pallas_call | solution.py:46
  49.0 1.5 %collective-permute-start.16 = (bf16[1,512,128]{2,1,0:T(8,128)(2,1)S(1)}, bf16[1,512,128]{2,1,0:T(8,128)(2,1)S(1)}, u32[]{:S(2)}, u32[]{:S(2)}) collective-permute-start(bf16[1,512,128]{2,1,0:T(8,128)(2,1)S(1)} %get-tuple-element.137), channel_id=1, source_target_pairs={{0,2},{1,3},{2,0},{3,1},{4,6},{5,7},{6,4},{7,5},{8,10},{9,11},{10,... | collective-permute-start | bytes 393224 | tf_op jit(solution)/shard_map/ppermute | solution.py:213
  50.5 1.4 collective-permute-start.10
  52.4 2.3 %collective-permute-done.17.refs_5_ = bf16[512,128]{1,0:T(8,128)(2,1)S(1)} collective-permute-done((bf16[512,128]{1,0:T(8,128)(2,1)S(1)}, bf16[512,128]{1,0:T(8,128)(2,1)S(1)}, u32[]{:S(2)}, u32[]{:S(2)}) %collective-permute-start.17) | collective-permute-done | bytes 131104 | tf_op jit(solution)/shard_map/ppermute | solution.py:213
  55.7 1.3 collective-permute-done.10.refs_1_
  57.0 3.1 %collective-permute-done.9.refs_0_ = bf16[512,128]{1,0:T(8,128)(2,1)S(1)} collective-permute-done((bf16[512,128]{1,0:T(8,128)(2,1)S(1)}, bf16[512,128]{1,0:T(8,128)(2,1)S(1)}, u32[]{:S(2)}, u32[]{:S(2)}) %collective-permute-start.9) | collective-permute-done | bytes 131104 | tf_op jit(solution)/shard_map/ppermute | solution.py:213
  60.1 2.7 %collective-permute-done.21.refs_6_ = bf16[1,512,128]{2,1,0:T(8,128)(2,1)S(1)} collective-permute-done((bf16[1,512,128]{2,1,0:T(8,128)(2,1)S(1)}, bf16[1,512,128]{2,1,0:T(8,128)(2,1)S(1)}, u32[]{:S(2)}, u32[]{:S(2)}) %collective-permute-start.21) | collective-permute-done | bytes 131104 | tf_op jit(solution)/shard_map/ppermute | solution.py:213
  62.8 2.5 %mix_multiply.7 = (bf16[2,512,128]{2,1,0:T(8,128)(2,1)S(1)}, bf16[2,512,128]{2,1,0:T(8,128)(2,1)S(1)}, f32[8,128]{1,0:T(8,128)S(1)}) custom-call(s32[2]{0:T(128)S(1)} %pad_add_fusion.refs_0_, f32[8,8]{1,0:T(8,128)S(1)} %convert_element_type.3.refs_1_, bf16[512,128]{1,0:T(8,128)(2,1)S(1)} %get-tuple-element.121.refs_2_, ...), custom_call_target="tpu_custom_call" | custom-call | tf_op jit(solution)/shard_map/mix_multiply/pallas_call | solution.py:46
  66.1 0.8 collective-permute-start.23
  66.9 1.2 collective-permute-start.20
  68.1 3.6 %collective-permute-done.24.refs_5_ = bf16[512,128]{1,0:T(8,128)(2,1)S(1)} collective-permute-done((bf16[512,128]{1,0:T(8,128)(2,1)S(1)}, bf16[512,128]{1,0:T(8,128)(2,1)S(1)}, u32[]{:S(2)}, u32[]{:S(2)}) %collective-permute-start.24) | collective-permute-done | bytes 131104 | tf_op jit(solution)/shard_map/ppermute | solution.py:213
  73.5 1.8 %collective-permute-done.19.refs_0_ = bf16[512,128]{1,0:T(8,128)(2,1)S(1)} collective-permute-done((bf16[512,128]{1,0:T(8,128)(2,1)S(1)}, bf16[512,128]{1,0:T(8,128)(2,1)S(1)}, u32[]{:S(2)}, u32[]{:S(2)}) %collective-permute-start.19) | collective-permute-done | bytes 131104 | tf_op jit(solution)/shard_map/ppermute | solution.py:213
  75.3 1.7 %collective-permute-done.18.refs_5_ = bf16[512,128]{1,0:T(8,128)(2,1)S(1)} collective-permute-done((bf16[512,128]{1,0:T(8,128)(2,1)S(1)}, bf16[512,128]{1,0:T(8,128)(2,1)S(1)}, u32[]{:S(2)}, u32[]{:S(2)}) %collective-permute-start.18) | collective-permute-done | bytes 131104 | tf_op jit(solution)/shard_map/ppermute | solution.py:213
  78.3 2.5 %mix_multiply.8 = (bf16[2,512,128]{2,1,0:T(8,128)(2,1)S(1)}, bf16[2,512,128]{2,1,0:T(8,128)(2,1)S(1)}, f32[8,128]{1,0:T(8,128)S(1)}) custom-call(s32[2]{0:T(128)S(1)} %pad_add_fusion.refs_0_, f32[8,8]{1,0:T(8,128)S(1)} %convert_element_type.3.refs_1_, bf16[512,128]{1,0:T(8,128)(2,1)S(1)} %get-tuple-element.129.refs_2_, ...), custom_call_target="tpu_custom_call" | custom-call | tf_op jit(solution)/shard_map/mix_multiply/pallas_call | solution.py:46
  80.9 1.4 %collective-permute-start.31 = (bf16[1,512,128]{2,1,0:T(8,128)(2,1)S(1)}, bf16[1,512,128]{2,1,0:T(8,128)(2,1)S(1)}, u32[]{:S(2)}, u32[]{:S(2)}) collective-permute-start(bf16[1,512,128]{2,1,0:T(8,128)(2,1)S(1)} %get-tuple-element.167), channel_id=1, source_target_pairs={{0,2},{1,3},{2,0},{3,1},{4,6},{5,7},{6,4},{7,5},{8,10},{9,11},{10,... | collective-permute-start | bytes 393224 | tf_op jit(solution)/shard_map/ppermute | solution.py:213
  82.4 1.4 collective-permute-start.28
  84.4 2.4 %collective-permute-done.31.refs_2_ = bf16[1,512,128]{2,1,0:T(8,128)(2,1)S(1)} collective-permute-done((bf16[1,512,128]{2,1,0:T(8,128)(2,1)S(1)}, bf16[1,512,128]{2,1,0:T(8,128)(2,1)S(1)}, u32[]{:S(2)}, u32[]{:S(2)}) %collective-permute-start.31) | collective-permute-done | bytes 131104 | tf_op jit(solution)/shard_map/ppermute | solution.py:213
  87.0 4.1 %collective-permute-done.27.refs_0_ = bf16[512,128]{1,0:T(8,128)(2,1)S(1)} collective-permute-done((bf16[512,128]{1,0:T(8,128)(2,1)S(1)}, bf16[512,128]{1,0:T(8,128)(2,1)S(1)}, u32[]{:S(2)}, u32[]{:S(2)}) %collective-permute-start.27) | collective-permute-done | bytes 131104 | tf_op jit(solution)/shard_map/ppermute | solution.py:213
  91.1 0.8 mix.15
  91.9 1.9 %collective-permute-done.25.refs_6_ = bf16[1,512,128]{2,1,0:T(8,128)(2,1)S(1)} collective-permute-done((bf16[1,512,128]{2,1,0:T(8,128)(2,1)S(1)}, bf16[1,512,128]{2,1,0:T(8,128)(2,1)S(1)}, u32[]{:S(2)}, u32[]{:S(2)}) %collective-permute-start.25) | collective-permute-done | bytes 131104 | tf_op jit(solution)/shard_map/ppermute | solution.py:213
  93.8 2.5 %mix_multiply.9 = (bf16[2,512,128]{2,1,0:T(8,128)(2,1)S(1)}, bf16[2,512,128]{2,1,0:T(8,128)(2,1)S(1)}, f32[8,128]{1,0:T(8,128)S(1)}) custom-call(s32[2]{0:T(128)S(1)} %pad_add_fusion.refs_0_, f32[8,8]{1,0:T(8,128)S(1)} %convert_element_type.3.refs_1_, bf16[512,128]{1,0:T(8,128)(2,1)S(1)} %get-tuple-element.127.refs_2_, ...), custom_call_target="tpu_custom_call" | custom-call | tf_op jit(solution)/shard_map/mix_multiply/pallas_call | solution.py:46
  96.4 0.9 collective-permute-start.34
  97.4 2.6 %collective-permute-start.37 = (bf16[512,128]{1,0:T(8,128)(2,1)S(1)}, bf16[512,128]{1,0:T(8,128)(2,1)S(1)}, u32[]{:S(2)}, u32[]{:S(2)}) collective-permute-start(bf16[512,128]{1,0:T(8,128)(2,1)S(1)} %bitcast.24), channel_id=1, source_target_pairs={{0,16},{4,20},{8,24},{12,28},{16,0},{20,4},{24,8},{28,12},{1,17},{... | collective-permute-start | bytes 393224 | tf_op jit(solution)/shard_map/ppermute | solution.py:213
  100.1 1.0 collective-permute-start.38
  101.1 1.3 collective-permute-done.34.refs_2_
  102.4 1.0 collective-permute-start.36
  103.4 1.8 %collective-permute-done.33.refs_7_ = bf16[1,512,128]{2,1,0:T(8,128)(2,1)S(1)} collective-permute-done((bf16[1,512,128]{2,1,0:T(8,128)(2,1)S(1)}, bf16[1,512,128]{2,1,0:T(8,128)(2,1)S(1)}, u32[]{:S(2)}, u32[]{:S(2)}) %collective-permute-start.33) | collective-permute-done | bytes 131104 | tf_op jit(solution)/shard_map/ppermute | solution.py:213
  105.3 1.5 %finish.5 = (bf16[512,640]{1,0:T(8,128)(2,1)}, f32[8,128]{1,0:T(8,128)S(1)}) custom-call(s32[2]{0:T(128)S(1)} %pad_add_fusion.refs_0_, f32[8,8]{1,0:T(8,128)S(1)} %convert_element_type.3.refs_1_, s32[1]{0:T(128)S(6)} %copy.53.refs_1_.refs_2_, bf16[512,128]{1,0:T(8,128)(2,1)S(1)} %bitcast.39, bf16[512,128]{1,0:T(8,128)(2,1)S(1)} %get-tuple-element.160.refs_3_.refs_4_, ...), custom_call_target="tpu_custom_call" | custom-call | tf_op jit(solution)/shard_map/finish/pallas_call | solution.py:46
  106.9 0.9 collective-permute-start.35
  109.0 2.2 %collective-permute-start.42 = (bf16[512,128]{1,0:T(8,128)(2,1)S(1)}, bf16[512,128]{1,0:T(8,128)(2,1)S(1)}, u32[]{:S(2)}, u32[]{:S(2)}) collective-permute-start(bf16[512,128]{1,0:T(8,128)(2,1)S(1)} %bitcast.28), channel_id=1, source_target_pairs={{0,16},{4,20},{8,24},{12,28},{16,0},{20,4},{24,8},{28,12},{1,17},{... | collective-permute-start | bytes 393224 | tf_op jit(solution)/shard_map/ppermute | solution.py:213
  111.2 1.0 collective-permute-start.43
  112.2 1.0 collective-permute-start.41
  113.3 2.1 %collective-permute-done.44.refs_7_ = bf16[1,512,128]{2,1,0:T(8,128)(2,1)S(1)} collective-permute-done((bf16[1,512,128]{2,1,0:T(8,128)(2,1)S(1)}, bf16[1,512,128]{2,1,0:T(8,128)(2,1)S(1)}, u32[]{:S(2)}, u32[]{:S(2)}) %collective-permute-start.44) | collective-permute-done | bytes 131104 | tf_op jit(solution)/shard_map/ppermute | solution.py:213
  115.4 1.5 %finish.6 = (bf16[512,640]{1,0:T(8,128)(2,1)}, f32[8,128]{1,0:T(8,128)S(1)}) custom-call(s32[2]{0:T(128)S(1)} %pad_add_fusion.refs_0_, f32[8,8]{1,0:T(8,128)S(1)} %convert_element_type.3.refs_1_, s32[1]{0:T(128)S(6)} %copy.53.refs_1_.refs_2_, bf16[512,128]{1,0:T(8,128)(2,1)S(1)} %bitcast.23, ...), custom_call_target="tpu_custom_call", output_to_operand_aliasing={{0}: (8, {})} | custom-call | tf_op jit(solution)/shard_map/finish/pallas_call | solution.py:46
  119.2 2.2 %collective-permute-start.39 = (bf16[512,128]{1,0:T(8,128)(2,1)S(1)}, bf16[512,128]{1,0:T(8,128)(2,1)S(1)}, u32[]{:S(2)}, u32[]{:S(2)}) collective-permute-start(bf16[512,128]{1,0:T(8,128)(2,1)S(1)} %bitcast.32), channel_id=1, source_target_pairs={{0,16},{4,20},{8,24},{12,28},{16,0},{20,4},{24,8},{28,12},{1,17},{... | collective-permute-start | bytes 393224 | tf_op jit(solution)/shard_map/ppermute | solution.py:213
  121.4 1.0 collective-permute-start.40
  122.4 1.0 collective-permute-start.47
  123.4 2.0 %collective-permute-done.45.refs_7_ = bf16[1,512,128]{2,1,0:T(8,128)(2,1)S(1)} collective-permute-done((bf16[1,512,128]{2,1,0:T(8,128)(2,1)S(1)}, bf16[1,512,128]{2,1,0:T(8,128)(2,1)S(1)}, u32[]{:S(2)}, u32[]{:S(2)}) %collective-permute-start.45) | collective-permute-done | bytes 131104 | tf_op jit(solution)/shard_map/ppermute | solution.py:213
  125.5 1.5 %finish.7 = (bf16[512,640]{1,0:T(8,128)(2,1)}, f32[8,128]{1,0:T(8,128)S(1)}) custom-call(s32[2]{0:T(128)S(1)} %pad_add_fusion.refs_0_, f32[8,8]{1,0:T(8,128)S(1)} %convert_element_type.3.refs_1_, s32[1]{0:T(128)S(6)} %copy.53.refs_1_.refs_2_, bf16[512,128]{1,0:T(8,128)(2,1)S(1)} %bitcast.27, ...), custom_call_target="tpu_custom_call", output_to_operand_aliasing={{0}: (8, {})} | custom-call | tf_op jit(solution)/shard_map/finish/pallas_call | solution.py:46
  127.0 0.9 collective-permute-done.47.refs_5_.refs_6_
  129.0 1.0 collective-permute-start.46
  130.0 3.7 %collective-permute-done.48.refs_7_ = bf16[1,512,128]{2,1,0:T(8,128)(2,1)S(1)} collective-permute-done((bf16[1,512,128]{2,1,0:T(8,128)(2,1)S(1)}, bf16[1,512,128]{2,1,0:T(8,128)(2,1)S(1)}, u32[]{:S(2)}, u32[]{:S(2)}) %collective-permute-start.48) | collective-permute-done | bytes 131104 | tf_op jit(solution)/shard_map/ppermute | solution.py:213
  133.7 1.5 %finish.8 = (bf16[512,640]{1,0:T(8,128)(2,1)}, f32[8,128]{1,0:T(8,128)S(1)}) custom-call(s32[2]{0:T(128)S(1)} %pad_add_fusion.refs_0_, f32[8,8]{1,0:T(8,128)S(1)} %convert_element_type.3.refs_1_, s32[1]{0:T(128)S(6)} %copy.53.refs_1_.refs_2_, bf16[512,128]{1,0:T(8,128)(2,1)S(1)} %bitcast.31, ...), custom_call_target="tpu_custom_call", output_to_operand_aliasing={{0}: (8, {})} | custom-call | tf_op jit(solution)/shard_map/finish/pallas_call | solution.py:46
  135.2 0.8 mix.19
  136.6 4.4 %collective-permute-done.49.refs_7_ = bf16[1,512,128]{2,1,0:T(8,128)(2,1)S(1)} collective-permute-done((bf16[1,512,128]{2,1,0:T(8,128)(2,1)S(1)}, bf16[1,512,128]{2,1,0:T(8,128)(2,1)S(1)}, u32[]{:S(2)}, u32[]{:S(2)}) %collective-permute-start.49) | collective-permute-done | bytes 131104 | tf_op jit(solution)/shard_map/ppermute | solution.py:213
  141.0 1.5 %finish.9 = (bf16[512,640]{1,0:T(8,128)(2,1)}, f32[8,128]{1,0:T(8,128)}) custom-call(s32[2]{0:T(128)S(1)} %pad_add_fusion.refs_0_, f32[8,8]{1,0:T(8,128)S(1)} %convert_element_type.3.refs_1_, s32[1]{0:T(128)S(6)} %copy.53.refs_1_.refs_2_, bf16[512,128]{1,0:T(8,128)(2,1)S(1)} %bitcast.35, ...), custom_call_target="tpu_custom_call", output_to_operand_aliasing={{0}: (8, {})} | custom-call | tf_op jit(solution)/shard_map/finish/pallas_call | solution.py:46
  (93 shorter events, 19.8 us)
Async XLA Ops:
  0.0 29.5 %copy-start = (bf16[2048,1,512]{2,0,1:T(8,128)(2,1)S(1)}, bf16[2048,1,512]{2,0,1:T(8,128)(2,1)}, u32[]{:S(2)}) copy-start(bf16[2048,1,512]{2,0,1:T(8,128)(2,1)} %param.7) | copy-start | bytes 6291460
  0.9 1.1 copy-start.1
  2.6 14.0 %collective-permute-start.2 = (bf16[512,128]{1,0:T(8,128)(2,1)S(1)}, bf16[512,128]{1,0:T(8,128)(2,1)S(1)}, u32[]{:S(2)}, u32[]{:S(2)}) collective-permute-start(bf16[512,128]{1,0:T(8,128)(2,1)S(1)} %get-tuple-element.111.refs_2_), channel_id=1, source_target_pairs={{0,16},{4,20},{8,24},{12,28},{16,0},{20,4},{24,8},{28,12},{1,17},{... | collective-permute-start | bytes 393224 | tf_op jit(solution)/shard_map/ppermute | solution.py:213
  6.7 9.9 %collective-permute-start.3 = (bf16[512,128]{1,0:T(8,128)(2,1)S(1)}, bf16[512,128]{1,0:T(8,128)(2,1)S(1)}, u32[]{:S(2)}, u32[]{:S(2)}) collective-permute-start(bf16[512,128]{1,0:T(8,128)(2,1)S(1)} %get-tuple-element.111.refs_2_), channel_id=1, source_target_pairs={{0,4},{4,0},{8,12},{12,8},{16,20},{20,16},{24,28},{28,24},{1,5},{5... | collective-permute-start | bytes 393224 | tf_op jit(solution)/shard_map/ppermute | solution.py:213
  8.8 12.4 %collective-permute-start = (bf16[512,128]{1,0:T(8,128)(2,1)S(1)}, bf16[512,128]{1,0:T(8,128)(2,1)S(1)}, u32[]{:S(2)}, u32[]{:S(2)}) collective-permute-start(bf16[512,128]{1,0:T(8,128)(2,1)S(1)} %get-tuple-element.110.refs_2_), channel_id=1, source_target_pairs={{0,16},{4,20},{8,24},{12,28},{16,0},{20,4},{24,8},{28,12},{1,17},{... | collective-permute-start | bytes 393224 | tf_op jit(solution)/shard_map/ppermute | solution.py:213
  9.2 12.0 %collective-permute-start.1 = (bf16[512,128]{1,0:T(8,128)(2,1)S(1)}, bf16[512,128]{1,0:T(8,128)(2,1)S(1)}, u32[]{:S(2)}, u32[]{:S(2)}) collective-permute-start(bf16[512,128]{1,0:T(8,128)(2,1)S(1)} %get-tuple-element.110.refs_2_), channel_id=1, source_target_pairs={{0,4},{4,0},{8,12},{12,8},{16,20},{20,16},{24,28},{28,24},{1,5},{5... | collective-permute-start | bytes 393224 | tf_op jit(solution)/shard_map/ppermute | solution.py:213
  16.6 6.0 %collective-permute-start.5 = (bf16[512,128]{1,0:T(8,128)(2,1)S(1)}, bf16[512,128]{1,0:T(8,128)(2,1)S(1)}, u32[]{:S(2)}, u32[]{:S(2)}) collective-permute-start(bf16[512,128]{1,0:T(8,128)(2,1)S(1)} %get-tuple-element.117.refs_3_), channel_id=1, source_target_pairs={{0,4},{4,0},{8,12},{12,8},{16,20},{20,16},{24,28},{28,24},{1,5},{5... | collective-permute-start | bytes 393224 | tf_op jit(solution)/shard_map/ppermute | solution.py:213
  19.2 1.1 copy-start.2
  20.9 7.3 %collective-permute-start.7 = (bf16[512,128]{1,0:T(8,128)(2,1)S(1)}, bf16[512,128]{1,0:T(8,128)(2,1)S(1)}, u32[]{:S(2)}, u32[]{:S(2)}) collective-permute-start(bf16[512,128]{1,0:T(8,128)(2,1)S(1)} %get-tuple-element.121.refs_2_), channel_id=1, source_target_pairs={{0,16},{4,20},{8,24},{12,28},{16,0},{20,4},{24,8},{28,12},{1,17},{... | collective-permute-start | bytes 393224 | tf_op jit(solution)/shard_map/ppermute | solution.py:213
  21.0 7.3 %collective-permute-start.8 = (bf16[512,128]{1,0:T(8,128)(2,1)S(1)}, bf16[512,128]{1,0:T(8,128)(2,1)S(1)}, u32[]{:S(2)}, u32[]{:S(2)}) collective-permute-start(bf16[512,128]{1,0:T(8,128)(2,1)S(1)} %get-tuple-element.121.refs_2_), channel_id=1, source_target_pairs={{0,4},{4,0},{8,12},{12,8},{16,20},{20,16},{24,28},{28,24},{1,5},{5... | collective-permute-start | bytes 393224 | tf_op jit(solution)/shard_map/ppermute | solution.py:213
  23.4 6.1 %collective-permute-start.6 = (bf16[1,512,128]{2,1,0:T(8,128)(2,1)S(1)}, bf16[1,512,128]{2,1,0:T(8,128)(2,1)S(1)}, u32[]{:S(2)}, u32[]{:S(2)}) collective-permute-start(bf16[1,512,128]{2,1,0:T(8,128)(2,1)S(1)} %get-tuple-element.120), channel_id=1, source_target_pairs={{0,8},{4,12},{8,0},{12,4},{16,24},{20,28},{24,16},{28,20},{1,9},{5... | collective-permute-start | bytes 393224 | tf_op jit(solution)/shard_map/ppermute | solution.py:213
  25.4 1.1 copy-start.3
  26.5 13.3 %copy-start.4 = (bf16[512,1,640]{2,0,1:T(8,128)(2,1)S(1)}, bf16[512,1,640]{2,0,1:T(8,128)(2,1)}, u32[]{:S(2)}) copy-start(bf16[512,1,640]{2,0,1:T(8,128)(2,1)} %param.4) | copy-start | bytes 1966084
  32.1 8.3 %collective-permute-start.14 = (bf16[2,512,128]{2,1,0:T(8,128)(2,1)S(1)}, bf16[2,512,128]{2,1,0:T(8,128)(2,1)S(1)}, u32[]{:S(2)}, u32[]{:S(2)}) collective-permute-start(bf16[2,512,128]{2,1,0:T(8,128)(2,1)S(1)} %get-tuple-element.131), channel_id=1, source_target_pairs={{0,1},{1,0},{2,3},{3,2},{4,5},{5,4},{6,7},{7,6},{8,9},{9,8},{10,11... | collective-permute-start | bytes 786440 | tf_op jit(solution)/shard_map/ppermute | solution.py:213
  32.2 6.4 %collective-permute-start.4 = (bf16[512,128]{1,0:T(8,128)(2,1)S(1)}, bf16[512,128]{1,0:T(8,128)(2,1)S(1)}, u32[]{:S(2)}, u32[]{:S(2)}) collective-permute-start(bf16[512,128]{1,0:T(8,128)(2,1)S(1)} %get-tuple-element.115.refs_3_), channel_id=1, source_target_pairs={{0,4},{4,0},{8,12},{12,8},{16,20},{20,16},{24,28},{28,24},{1,5},{5... | collective-permute-start | bytes 393224 | tf_op jit(solution)/shard_map/ppermute | solution.py:213
  33.6 9.4 %collective-permute-start.12 = (bf16[512,128]{1,0:T(8,128)(2,1)S(1)}, bf16[512,128]{1,0:T(8,128)(2,1)S(1)}, u32[]{:S(2)}, u32[]{:S(2)}) collective-permute-start(bf16[512,128]{1,0:T(8,128)(2,1)S(1)} %get-tuple-element.129.refs_2_), channel_id=1, source_target_pairs={{0,16},{4,20},{8,24},{12,28},{16,0},{20,4},{24,8},{28,12},{1,17},{... | collective-permute-start | bytes 393224 | tf_op jit(solution)/shard_map/ppermute | solution.py:213
  34.4 8.6 %collective-permute-start.13 = (bf16[512,128]{1,0:T(8,128)(2,1)S(1)}, bf16[512,128]{1,0:T(8,128)(2,1)S(1)}, u32[]{:S(2)}, u32[]{:S(2)}) collective-permute-start(bf16[512,128]{1,0:T(8,128)(2,1)S(1)} %get-tuple-element.129.refs_2_), channel_id=1, source_target_pairs={{0,4},{4,0},{8,12},{12,8},{16,20},{20,16},{24,28},{28,24},{1,5},{5... | collective-permute-start | bytes 393224 | tf_op jit(solution)/shard_map/ppermute | solution.py:213
  39.3 6.4 %collective-permute-start.11 = (bf16[1,512,128]{2,1,0:T(8,128)(2,1)S(1)}, bf16[1,512,128]{2,1,0:T(8,128)(2,1)S(1)}, u32[]{:S(2)}, u32[]{:S(2)}) collective-permute-start(bf16[1,512,128]{2,1,0:T(8,128)(2,1)S(1)} %get-tuple-element.128), channel_id=1, source_target_pairs={{0,8},{4,12},{8,0},{12,4},{16,24},{20,28},{24,16},{28,20},{1,9},{5... | collective-permute-start | bytes 393224 | tf_op jit(solution)/shard_map/ppermute | solution.py:213
  48.2 7.4 %collective-permute-start.15 = (bf16[2,512,128]{2,1,0:T(8,128)(2,1)S(1)}, bf16[2,512,128]{2,1,0:T(8,128)(2,1)S(1)}, u32[]{:S(2)}, u32[]{:S(2)}) collective-permute-start(bf16[2,512,128]{2,1,0:T(8,128)(2,1)S(1)} %get-tuple-element.136), channel_id=1, source_target_pairs={{0,1},{1,0},{2,3},{3,2},{4,5},{5,4},{6,7},{7,6},{8,9},{9,8},{10,11... | collective-permute-start | bytes 786440 | tf_op jit(solution)/shard_map/ppermute | solution.py:213
  48.3 6.3 %collective-permute-start.17 = (bf16[512,128]{1,0:T(8,128)(2,1)S(1)}, bf16[512,128]{1,0:T(8,128)(2,1)S(1)}, u32[]{:S(2)}, u32[]{:S(2)}) collective-permute-start(bf16[512,128]{1,0:T(8,128)(2,1)S(1)} %get-tuple-element.138.refs_3_), channel_id=1, source_target_pairs={{0,4},{4,0},{8,12},{12,8},{16,20},{20,16},{24,28},{28,24},{1,5},{5... | collective-permute-start | bytes 393224 | tf_op jit(solution)/shard_map/ppermute | solution.py:213
  49.0 6.5 %collective-permute-start.16 = (bf16[1,512,128]{2,1,0:T(8,128)(2,1)S(1)}, bf16[1,512,128]{2,1,0:T(8,128)(2,1)S(1)}, u32[]{:S(2)}, u32[]{:S(2)}) collective-permute-start(bf16[1,512,128]{2,1,0:T(8,128)(2,1)S(1)} %get-tuple-element.137), channel_id=1, source_target_pairs={{0,2},{1,3},{2,0},{3,1},{4,6},{5,7},{6,4},{7,5},{8,10},{9,11},{10,... | collective-permute-start | bytes 393224 | tf_op jit(solution)/shard_map/ppermute | solution.py:213
  50.5 6.5 %collective-permute-start.10 = (bf16[512,128]{1,0:T(8,128)(2,1)S(1)}, bf16[512,128]{1,0:T(8,128)(2,1)S(1)}, u32[]{:S(2)}, u32[]{:S(2)}) collective-permute-start(bf16[512,128]{1,0:T(8,128)(2,1)S(1)} %get-tuple-element.127.refs_2_), channel_id=1, source_target_pairs={{0,4},{4,0},{8,12},{12,8},{16,20},{20,16},{24,28},{28,24},{1,5},{5... | collective-permute-start | bytes 393224 | tf_op jit(solution)/shard_map/ppermute | solution.py:213
  51.9 8.1 %collective-permute-start.9 = (bf16[512,128]{1,0:T(8,128)(2,1)S(1)}, bf16[512,128]{1,0:T(8,128)(2,1)S(1)}, u32[]{:S(2)}, u32[]{:S(2)}) collective-permute-start(bf16[512,128]{1,0:T(8,128)(2,1)S(1)} %get-tuple-element.127.refs_2_), channel_id=1, source_target_pairs={{0,16},{4,20},{8,24},{12,28},{16,0},{20,4},{24,8},{28,12},{1,17},{... | collective-permute-start | bytes 393224 | tf_op jit(solution)/shard_map/ppermute | solution.py:213
  55.4 7.3 %collective-permute-start.21 = (bf16[1,512,128]{2,1,0:T(8,128)(2,1)S(1)}, bf16[1,512,128]{2,1,0:T(8,128)(2,1)S(1)}, u32[]{:S(2)}, u32[]{:S(2)}) collective-permute-start(bf16[1,512,128]{2,1,0:T(8,128)(2,1)S(1)} %get-tuple-element.147), channel_id=1, source_target_pairs={{0,8},{4,12},{8,0},{12,4},{16,24},{20,28},{24,16},{28,20},{1,9},{5... | collective-permute-start | bytes 393224 | tf_op jit(solution)/shard_map/ppermute | solution.py:213
  65.3 8.1 %collective-permute-start.22 = (bf16[2,512,128]{2,1,0:T(8,128)(2,1)S(1)}, bf16[2,512,128]{2,1,0:T(8,128)(2,1)S(1)}, u32[]{:S(2)}, u32[]{:S(2)}) collective-permute-start(bf16[2,512,128]{2,1,0:T(8,128)(2,1)S(1)} %get-tuple-element.150), channel_id=1, source_target_pairs={{0,1},{1,0},{2,3},{3,2},{4,5},{5,4},{6,7},{7,6},{8,9},{9,8},{10,11... | collective-permute-start | bytes 786440 | tf_op jit(solution)/shard_map/ppermute | solution.py:213
  65.4 6.4 %collective-permute-start.24 = (bf16[512,128]{1,0:T(8,128)(2,1)S(1)}, bf16[512,128]{1,0:T(8,128)(2,1)S(1)}, u32[]{:S(2)}, u32[]{:S(2)}) collective-permute-start(bf16[512,128]{1,0:T(8,128)(2,1)S(1)} %get-tuple-element.152.refs_3_), channel_id=1, source_target_pairs={{0,4},{4,0},{8,12},{12,8},{16,20},{20,16},{24,28},{28,24},{1,5},{5... | collective-permute-start | bytes 393224 | tf_op jit(solution)/shard_map/ppermute | solution.py:213
  66.1 7.1 %collective-permute-start.23 = (bf16[1,512,128]{2,1,0:T(8,128)(2,1)S(1)}, bf16[1,512,128]{2,1,0:T(8,128)(2,1)S(1)}, u32[]{:S(2)}, u32[]{:S(2)}) collective-permute-start(bf16[1,512,128]{2,1,0:T(8,128)(2,1)S(1)} %get-tuple-element.151), channel_id=1, source_target_pairs={{0,2},{1,3},{2,0},{3,1},{4,6},{5,7},{6,4},{7,5},{8,10},{9,11},{10,... | collective-permute-start | bytes 393224 | tf_op jit(solution)/shard_map/ppermute | solution.py:213
  66.9 8.3 %collective-permute-start.19 = (bf16[512,128]{1,0:T(8,128)(2,1)S(1)}, bf16[512,128]{1,0:T(8,128)(2,1)S(1)}, u32[]{:S(2)}, u32[]{:S(2)}) collective-permute-start(bf16[512,128]{1,0:T(8,128)(2,1)S(1)} %bitcast.36), channel_id=1, source_target_pairs={{0,16},{4,20},{8,24},{12,28},{16,0},{20,4},{24,8},{28,12},{1,17},{... | collective-permute-start | bytes 393224 | tf_op jit(solution)/shard_map/ppermute | solution.py:213
  66.9 8.3 %collective-permute-start.20 = (bf16[512,128]{1,0:T(8,128)(2,1)S(1)}, bf16[512,128]{1,0:T(8,128)(2,1)S(1)}, u32[]{:S(2)}, u32[]{:S(2)}) collective-permute-start(bf16[512,128]{1,0:T(8,128)(2,1)S(1)} %bitcast.37), channel_id=1, source_target_pairs={{0,4},{4,0},{8,12},{12,8},{16,20},{20,16},{24,28},{28,24},{1,5},{5... | collective-permute-start | bytes 393224 | tf_op jit(solution)/shard_map/ppermute | solution.py:213
  71.7 5.2 %collective-permute-start.18 = (bf16[512,128]{1,0:T(8,128)(2,1)S(1)}, bf16[512,128]{1,0:T(8,128)(2,1)S(1)}, u32[]{:S(2)}, u32[]{:S(2)}) collective-permute-start(bf16[512,128]{1,0:T(8,128)(2,1)S(1)} %get-tuple-element.144.refs_3_), channel_id=1, source_target_pairs={{0,4},{4,0},{8,12},{12,8},{16,20},{20,16},{24,28},{28,24},{1,5},{5... | collective-permute-start | bytes 393224 | tf_op jit(solution)/shard_map/ppermute | solution.py:213
  73.2 5.0 %collective-permute-start.29 = (bf16[1,512,128]{2,1,0:T(8,128)(2,1)S(1)}, bf16[1,512,128]{2,1,0:T(8,128)(2,1)S(1)}, u32[]{:S(2)}, u32[]{:S(2)}) collective-permute-start(bf16[1,512,128]{2,1,0:T(8,128)(2,1)S(1)} %get-tuple-element.163), channel_id=1, source_target_pairs={{0,8},{4,12},{8,0},{12,4},{16,24},{20,28},{24,16},{28,20},{1,9},{5... | collective-permute-start | bytes 393224 | tf_op jit(solution)/shard_map/ppermute | solution.py:213
  80.8 6.1 %collective-permute-start.30 = (bf16[2,512,128]{2,1,0:T(8,128)(2,1)S(1)}, bf16[2,512,128]{2,1,0:T(8,128)(2,1)S(1)}, u32[]{:S(2)}, u32[]{:S(2)}) collective-permute-start(bf16[2,512,128]{2,1,0:T(8,128)(2,1)S(1)} %get-tuple-element.166), channel_id=1, source_target_pairs={{0,1},{1,0},{2,3},{3,2},{4,5},{5,4},{6,7},{7,6},{8,9},{9,8},{10,11... | collective-permute-start | bytes 786440 | tf_op jit(solution)/shard_map/ppermute | solution.py:213
  80.9 5.9 %collective-permute-start.31 = (bf16[1,512,128]{2,1,0:T(8,128)(2,1)S(1)}, bf16[1,512,128]{2,1,0:T(8,128)(2,1)S(1)}, u32[]{:S(2)}, u32[]{:S(2)}) collective-permute-start(bf16[1,512,128]{2,1,0:T(8,128)(2,1)S(1)} %get-tuple-element.167), channel_id=1, source_target_pairs={{0,2},{1,3},{2,0},{3,1},{4,6},{5,7},{6,4},{7,5},{8,10},{9,11},{10,... | collective-permute-start | bytes 393224 | tf_op jit(solution)/shard_map/ppermute | solution.py:213
  82.3 8.8 %collective-permute-start.27 = (bf16[512,128]{1,0:T(8,128)(2,1)S(1)}, bf16[512,128]{1,0:T(8,128)(2,1)S(1)}, u32[]{:S(2)}, u32[]{:S(2)}) collective-permute-start(bf16[512,128]{1,0:T(8,128)(2,1)S(1)} %bitcast.20), channel_id=1, source_target_pairs={{0,16},{4,20},{8,24},{12,28},{16,0},{20,4},{24,8},{28,12},{1,17},{... | collective-permute-start | bytes 393224 | tf_op jit(solution)/shard_map/ppermute | solution.py:213
  82.4 8.8 %collective-permute-start.28 = (bf16[512,128]{1,0:T(8,128)(2,1)S(1)}, bf16[512,128]{1,0:T(8,128)(2,1)S(1)}, u32[]{:S(2)}, u32[]{:S(2)}) collective-permute-start(bf16[512,128]{1,0:T(8,128)(2,1)S(1)} %bitcast.21), channel_id=1, source_target_pairs={{0,4},{4,0},{8,12},{12,8},{16,20},{20,16},{24,28},{28,24},{1,5},{5... | collective-permute-start | bytes 393224 | tf_op jit(solution)/shard_map/ppermute | solution.py:213
  83.7 7.4 %collective-permute-start.26 = (bf16[512,128]{1,0:T(8,128)(2,1)S(1)}, bf16[512,128]{1,0:T(8,128)(2,1)S(1)}, u32[]{:S(2)}, u32[]{:S(2)}) collective-permute-start(bf16[512,128]{1,0:T(8,128)(2,1)S(1)} %get-tuple-element.160.refs_3_.refs_4_), channel_id=1, source_target_pairs={{0,4},{4,0},{8,12},{12,8},{16,20},{20,16},{24,28},{28,24},{1,5},{5... | collective-permute-start | bytes 393224 | tf_op jit(solution)/shard_map/ppermute | solution.py:213
  86.8 7.0 %collective-permute-start.25 = (bf16[1,512,128]{2,1,0:T(8,128)(2,1)S(1)}, bf16[1,512,128]{2,1,0:T(8,128)(2,1)S(1)}, u32[]{:S(2)}, u32[]{:S(2)}) collective-permute-start(bf16[1,512,128]{2,1,0:T(8,128)(2,1)S(1)} %get-tuple-element.159), channel_id=1, source_target_pairs={{0,8},{4,12},{8,0},{12,4},{16,24},{20,28},{24,16},{28,20},{1,9},{5... | collective-permute-start | bytes 393224 | tf_op jit(solution)/shard_map/ppermute | solution.py:213
  96.4 10.4 %collective-permute-start.32 = (bf16[2,512,128]{2,1,0:T(8,128)(2,1)S(1)}, bf16[2,512,128]{2,1,0:T(8,128)(2,1)S(1)}, u32[]{:S(2)}, u32[]{:S(2)}) collective-permute-start(bf16[2,512,128]{2,1,0:T(8,128)(2,1)S(1)} %get-tuple-element.174), channel_id=1, source_target_pairs={{0,1},{1,0},{2,3},{3,2},{4,5},{5,4},{6,7},{7,6},{8,9},{9,8},{10,11... | collective-permute-start | bytes 786440 | tf_op jit(solution)/shard_map/ppermute | solution.py:213
  96.4 5.9 %collective-permute-start.34 = (bf16[1,512,128]{2,1,0:T(8,128)(2,1)S(1)}, bf16[1,512,128]{2,1,0:T(8,128)(2,1)S(1)}, u32[]{:S(2)}, u32[]{:S(2)}) collective-permute-start(bf16[1,512,128]{2,1,0:T(8,128)(2,1)S(1)} %get-tuple-element.176), channel_id=1, source_target_pairs={{0,2},{1,3},{2,0},{3,1},{4,6},{5,7},{6,4},{7,5},{8,10},{9,11},{10,... | collective-permute-start | bytes 393224 | tf_op jit(solution)/shard_map/ppermute | solution.py:213
  97.4 7.9 %collective-permute-start.33 = (bf16[1,512,128]{2,1,0:T(8,128)(2,1)S(1)}, bf16[1,512,128]{2,1,0:T(8,128)(2,1)S(1)}, u32[]{:S(2)}, u32[]{:S(2)}) collective-permute-start(bf16[1,512,128]{2,1,0:T(8,128)(2,1)S(1)} %get-tuple-element.175), channel_id=1, source_target_pairs={{0,8},{4,12},{8,0},{12,4},{16,24},{20,28},{24,16},{28,20},{1,9},{5... | collective-permute-start | bytes 393224 | tf_op jit(solution)/shard_map/ppermute | solution.py:213
  97.4 10.3 %collective-permute-start.37 = (bf16[512,128]{1,0:T(8,128)(2,1)S(1)}, bf16[512,128]{1,0:T(8,128)(2,1)S(1)}, u32[]{:S(2)}, u32[]{:S(2)}) collective-permute-start(bf16[512,128]{1,0:T(8,128)(2,1)S(1)} %bitcast.24), channel_id=1, source_target_pairs={{0,16},{4,20},{8,24},{12,28},{16,0},{20,4},{24,8},{28,12},{1,17},{... | collective-permute-start | bytes 393224 | tf_op jit(solution)/shard_map/ppermute | solution.py:213
  100.1 7.7 %collective-permute-start.38 = (bf16[512,128]{1,0:T(8,128)(2,1)S(1)}, bf16[512,128]{1,0:T(8,128)(2,1)S(1)}, u32[]{:S(2)}, u32[]{:S(2)}) collective-permute-start(bf16[512,128]{1,0:T(8,128)(2,1)S(1)} %bitcast.25), channel_id=1, source_target_pairs={{0,4},{4,0},{8,12},{12,8},{16,20},{20,16},{24,28},{28,24},{1,5},{5... | collective-permute-start | bytes 393224 | tf_op jit(solution)/shard_map/ppermute | solution.py:213
  102.4 5.5 %collective-permute-start.36 = (bf16[512,128]{1,0:T(8,128)(2,1)S(1)}, bf16[512,128]{1,0:T(8,128)(2,1)S(1)}, u32[]{:S(2)}, u32[]{:S(2)}) collective-permute-start(bf16[512,128]{1,0:T(8,128)(2,1)S(1)} %get-tuple-element.181.refs_3_.refs_4_), channel_id=1, source_target_pairs={{0,4},{4,0},{8,12},{12,8},{16,20},{20,16},{24,28},{28,24},{1,5},{5... | collective-permute-start | bytes 393224 | tf_op jit(solution)/shard_map/ppermute | solution.py:213
  106.9 6.4 %collective-permute-start.35 = (bf16[1,512,128]{2,1,0:T(8,128)(2,1)S(1)}, bf16[1,512,128]{2,1,0:T(8,128)(2,1)S(1)}, u32[]{:S(2)}, u32[]{:S(2)}) collective-permute-start(bf16[1,512,128]{2,1,0:T(8,128)(2,1)S(1)} %get-tuple-element.180), channel_id=1, source_target_pairs={{0,2},{1,3},{2,0},{3,1},{4,6},{5,7},{6,4},{7,5},{8,10},{9,11},{10,... | collective-permute-start | bytes 393224 | tf_op jit(solution)/shard_map/ppermute | solution.py:213
  108.7 6.7 %collective-permute-start.44 = (bf16[1,512,128]{2,1,0:T(8,128)(2,1)S(1)}, bf16[1,512,128]{2,1,0:T(8,128)(2,1)S(1)}, u32[]{:S(2)}, u32[]{:S(2)}) collective-permute-start(bf16[1,512,128]{2,1,0:T(8,128)(2,1)S(1)} %get-tuple-element.191), channel_id=1, source_target_pairs={{0,8},{4,12},{8,0},{12,4},{16,24},{20,28},{24,16},{28,20},{1,9},{5... | collective-permute-start | bytes 393224 | tf_op jit(solution)/shard_map/ppermute | solution.py:213
  109.0 8.2 %collective-permute-start.42 = (bf16[512,128]{1,0:T(8,128)(2,1)S(1)}, bf16[512,128]{1,0:T(8,128)(2,1)S(1)}, u32[]{:S(2)}, u32[]{:S(2)}) collective-permute-start(bf16[512,128]{1,0:T(8,128)(2,1)S(1)} %bitcast.28), channel_id=1, source_target_pairs={{0,16},{4,20},{8,24},{12,28},{16,0},{20,4},{24,8},{28,12},{1,17},{... | collective-permute-start | bytes 393224 | tf_op jit(solution)/shard_map/ppermute | solution.py:213
  111.2 6.0 %collective-permute-start.43 = (bf16[512,128]{1,0:T(8,128)(2,1)S(1)}, bf16[512,128]{1,0:T(8,128)(2,1)S(1)}, u32[]{:S(2)}, u32[]{:S(2)}) collective-permute-start(bf16[512,128]{1,0:T(8,128)(2,1)S(1)} %bitcast.29), channel_id=1, source_target_pairs={{0,4},{4,0},{8,12},{12,8},{16,20},{20,16},{24,28},{28,24},{1,5},{5... | collective-permute-start | bytes 393224 | tf_op jit(solution)/shard_map/ppermute | solution.py:213
  112.2 5.7 %collective-permute-start.41 = (bf16[512,128]{1,0:T(8,128)(2,1)S(1)}, bf16[512,128]{1,0:T(8,128)(2,1)S(1)}, u32[]{:S(2)}, u32[]{:S(2)}) collective-permute-start(bf16[512,128]{1,0:T(8,128)(2,1)S(1)} %get-tuple-element.188.refs_3_.refs_4_), channel_id=1, source_target_pairs={{0,4},{4,0},{8,12},{12,8},{16,20},{20,16},{24,28},{28,24},{1,5},{5... | collective-permute-start | bytes 393224 | tf_op jit(solution)/shard_map/ppermute | solution.py:213
  118.7 6.8 %collective-permute-start.45 = (bf16[1,512,128]{2,1,0:T(8,128)(2,1)S(1)}, bf16[1,512,128]{2,1,0:T(8,128)(2,1)S(1)}, u32[]{:S(2)}, u32[]{:S(2)}) collective-permute-start(bf16[1,512,128]{2,1,0:T(8,128)(2,1)S(1)} %get-tuple-element.196), channel_id=1, source_target_pairs={{0,8},{4,12},{8,0},{12,4},{16,24},{20,28},{24,16},{28,20},{1,9},{5... | collective-permute-start | bytes 393224 | tf_op jit(solution)/shard_map/ppermute | solution.py:213
  119.2 7.8 %collective-permute-start.39 = (bf16[512,128]{1,0:T(8,128)(2,1)S(1)}, bf16[512,128]{1,0:T(8,128)(2,1)S(1)}, u32[]{:S(2)}, u32[]{:S(2)}) collective-permute-start(bf16[512,128]{1,0:T(8,128)(2,1)S(1)} %bitcast.32), channel_id=1, source_target_pairs={{0,16},{4,20},{8,24},{12,28},{16,0},{20,4},{24,8},{28,12},{1,17},{... | collective-permute-start | bytes 393224 | tf_op jit(solution)/shard_map/ppermute | solution.py:213
  121.4 5.6 %collective-permute-start.40 = (bf16[512,128]{1,0:T(8,128)(2,1)S(1)}, bf16[512,128]{1,0:T(8,128)(2,1)S(1)}, u32[]{:S(2)}, u32[]{:S(2)}) collective-permute-start(bf16[512,128]{1,0:T(8,128)(2,1)S(1)} %bitcast.33), channel_id=1, source_target_pairs={{0,4},{4,0},{8,12},{12,8},{16,20},{20,16},{24,28},{28,24},{1,5},{5... | collective-permute-start | bytes 393224 | tf_op jit(solution)/shard_map/ppermute | solution.py:213
  122.4 5.5 %collective-permute-start.47 = (bf16[512,128]{1,0:T(8,128)(2,1)S(1)}, bf16[512,128]{1,0:T(8,128)(2,1)S(1)}, u32[]{:S(2)}, u32[]{:S(2)}) collective-permute-start(bf16[512,128]{1,0:T(8,128)(2,1)S(1)} %get-tuple-element.202.refs_3_.refs_4_), channel_id=1, source_target_pairs={{0,4},{4,0},{8,12},{12,8},{16,20},{20,16},{24,28},{28,24},{1,5},{5... | collective-permute-start | bytes 393224 | tf_op jit(solution)/shard_map/ppermute | solution.py:213
  128.7 5.0 %collective-permute-start.48 = (bf16[1,512,128]{2,1,0:T(8,128)(2,1)S(1)}, bf16[1,512,128]{2,1,0:T(8,128)(2,1)S(1)}, u32[]{:S(2)}, u32[]{:S(2)}) collective-permute-start(bf16[1,512,128]{2,1,0:T(8,128)(2,1)S(1)} %get-tuple-element.205), channel_id=1, source_target_pairs={{0,8},{4,12},{8,0},{12,4},{16,24},{20,28},{24,16},{28,20},{1,9},{5... | collective-permute-start | bytes 393224 | tf_op jit(solution)/shard_map/ppermute | solution.py:213
  129.0 6.2 %collective-permute-start.46 = (bf16[512,128]{1,0:T(8,128)(2,1)S(1)}, bf16[512,128]{1,0:T(8,128)(2,1)S(1)}, u32[]{:S(2)}, u32[]{:S(2)}) collective-permute-start(bf16[512,128]{1,0:T(8,128)(2,1)S(1)} %get-tuple-element.200.refs_3_.refs_4_), channel_id=1, source_target_pairs={{0,4},{4,0},{8,12},{12,8},{16,20},{20,16},{24,28},{28,24},{1,5},{5... | collective-permute-start | bytes 393224 | tf_op jit(solution)/shard_map/ppermute | solution.py:213
  136.0 5.0 %collective-permute-start.49 = (bf16[1,512,128]{2,1,0:T(8,128)(2,1)S(1)}, bf16[1,512,128]{2,1,0:T(8,128)(2,1)S(1)}, u32[]{:S(2)}, u32[]{:S(2)}) collective-permute-start(bf16[1,512,128]{2,1,0:T(8,128)(2,1)S(1)} %get-tuple-element.209), channel_id=1, source_target_pairs={{0,8},{4,12},{8,0},{12,4},{16,24},{20,28},{24,16},{28,20},{1,9},{5... | collective-permute-start | bytes 393224 | tf_op jit(solution)/shard_map/ppermute | solution.py:213

commit v3 on v2

v3 whole, which is shorter than its diff:
```python
import functools

import jax
import jax.numpy as jnp
from jax import lax
from jax.experimental import pallas as pl
from jax.experimental.pallas import tpu as pltpu
from jax.sharding import PartitionSpec as P

F32 = jnp.float32
BF16 = jnp.bfloat16
SLAB = 64
MATMUL_ROWS = 256
VMEM_LIMIT = 16 * 1024 * 1024
smem = pl.BlockSpec(memory_space=pltpu.SMEM)
vmem = pl.BlockSpec(memory_space=pltpu.VMEM)
unread = pl.BlockSpec(memory_space=pl.ANY)


def chunk_bounds(columns):
    width = 128 if columns % 128 == 0 else columns
    return [(lo, width) for lo in range(0, columns, width)]


def call(kernel, name, out_shape, arrays, scalars=(), scratch=(), out_specs=None, whole=(), after=(), aliases=None):
    count = len(scalars) + len(arrays) + len(whole)

    def body(*refs):
        kernel(*refs[:count], *refs[count + len(after):])

    return pl.pallas_call(
        body, name=name, out_shape=list(out_shape),
        in_specs=[smem] * len(scalars) + [vmem] * len(arrays) + [unread] * (len(whole) + len(after)),
        out_specs=out_specs or [vmem] * len(out_shape),
        scratch_shapes=list(scratch),
        input_output_aliases=aliases or {},
        compiler_params=pltpu.CompilerParams(vmem_limit_bytes=VMEM_LIMIT),
        cost_estimate=pl.CostEstimate(flops=0, transcendentals=0, bytes_accessed=0),
    )(*scalars, *arrays, *whole, *after)


def like(array):
    return jax.ShapeDtypeStruct(array.shape, array.dtype)


def slabs(rows, body, step=SLAB):
    step = step if rows % step == 0 else rows

    @pl.loop(0, rows // step)
    def _(i):
        body(pl.ds(pl.multiple_of(i * step, step), step))


def masked(total, at, left):
    row = lax.broadcasted_iota(jnp.int32, total.shape, 0) + at.start
    return jnp.where(row < left, total, 0.0).astype(BF16)


def stacked(count, rows, width):
    return jax.ShapeDtypeStruct((count, rows, width), BF16)


def mask_first(block_rows, own, lo, width):
    rows = own.shape[0]

    def kernel(length_ref, own_ref, out_ref, left_ref):
        left = length_ref[0] - lax.axis_index("row") * rows
        left_ref[...] = jnp.full(left_ref.shape, left, jnp.int32)

        def body(at):
            out_ref[at, :] = masked(own_ref[at, lo:lo + width].astype(F32), at, left)

        slabs(rows, body)

    outs = [jax.ShapeDtypeStruct((rows, width), BF16), jax.ShapeDtypeStruct((8, width), jnp.int32)]
    return call(kernel, "mask_first", outs, [own], [block_rows])


def mask_chunk(left, own, lo, width, after):
    rows = own.shape[0]

    def kernel(left_ref, own_ref, out_ref):
        def body(at):
            out_ref[at, :] = masked(own_ref[at, lo:lo + width].astype(F32), at, left_ref[0:1, :])

        slabs(rows, body)

    return call(kernel, "mask_chunk", [jax.ShapeDtypeStruct((rows, width), BF16)], [left, own], after=after)[0]


def coefficients(matrix, n_chan, entries, width):
    count = -(-len(entries) // 8) * 8

    def kernel(matrix_ref, table_ref):
        c = lax.axis_index("chan")
        for i, (t, m) in enumerate(entries):
            table_ref[i:i + 1, :] = jnp.full((1, width), matrix_ref[c ^ t, c ^ m], F32)

    return call(kernel, "coefficients", [jax.ShapeDtypeStruct((count, width), F32)], [], [matrix])[0]


def mixed(table_ref, entries, held, at, target):
    total = None
    for source, ref in held:
        entry = entries.index((target, source))
        term = ref[at, :].astype(F32) * table_ref[entry:entry + 1, :]
        total = term if total is None else total + term
    return total


def mix(table, entries, held, targets, received):
    rows, width = held[0][1].shape

    def kernel(table_ref, *refs):
        held_refs = [(m, ref) for (m, _), ref in zip(held, refs)]
        received_refs = refs[len(held):-1]
        out_ref = refs[-1]

        def body(at):
            for i, t in enumerate(targets):
                total = mixed(table_ref, entries, held_refs, at, t)
                for (_, names), ref in zip(received, received_refs):
                    if t in names:
                        total = total + ref[names.index(t), at, :].astype(F32)
                out_ref[i, at, :] = total.astype(BF16)

        slabs(rows, body)

    arrays = [table] + [b for _, b in held] + [r for r, _ in received]
    return call(kernel, "mix", [stacked(len(targets), rows, width)], arrays)[0]


def mix_multiply(table, entries, held, received, weights, sent, kept):
    rows, width = held[0][1].shape
    group = weights.shape[0] // (len(sent) + len(kept))

    def kernel(table_ref, *refs):
        held_refs = [(m, ref) for (m, _), ref in zip(held, refs)]
        received_refs = refs[len(held):len(held) + len(received)]
        weights_ref, sent_ref, kept_ref, cross_ref = refs[len(held) + len(received):]
        g = lax.axis_index("row")

        def body(at):
            total = mixed(table_ref, entries, held_refs, at, 0)
            for ref in received_refs:
                total = total + ref[0, at, :].astype(F32)
            cross_ref[at, :] = total.astype(BF16)

        slabs(rows, body)
        for names, out_ref in ((sent, sent_ref), (kept, kept_ref)):
            for i, d in enumerate(names):
                base = (g ^ d) * group

                def rows_of(at):
                    from_row = pl.ds(pl.multiple_of(base + at.start, at.size), at.size)
                    out_ref[i, at, :] = jnp.dot(
                        weights_ref[from_row, :], cross_ref[...], preferred_element_type=F32).astype(BF16)

                slabs(group, rows_of, MATMUL_ROWS)

    arrays = [table] + [b for _, b in held] + received + [weights]
    outs = [stacked(len(sent), group, width), stacked(len(kept), group, width)]
    return call(kernel, "mix_multiply", outs, arrays, scratch=[pltpu.VMEM((rows, width), BF16)])


def add_up(stacks, targets):
    _, rows, width = stacks[0][0].shape

    def kernel(*refs):
        def body(at):
            for i, t in enumerate(targets):
                terms = [ref[names.index(t), at, :].astype(F32) for (_, names), ref in zip(stacks, refs) if t in names]
                refs[-1][i, at, :] = functools.reduce(lambda a, b: a + b, terms).astype(BF16)

        slabs(rows, body)

    return call(kernel, "add_up", [stacked(len(targets), rows, width)], [s for s, _ in stacks])[0]


def finish(table, entries, left, held, received, lo, columns, result):
    rows, width = held[0][1].shape

    def kernel(table_ref, left_ref, *refs):
        held_refs = [(m, ref) for (m, _), ref in zip(held, refs)]
        received_refs = refs[len(held):len(held) + len(received)]
        out_ref, chunk_ref, done = refs[-3:]

        def body(at):
            total = mixed(table_ref, entries, held_refs, at, 0)
            for ref in received_refs:
                total = total + ref[0, at, :].astype(F32)
            chunk_ref[at, :] = masked(total, at, left_ref[0:1, :])

        slabs(rows, body)
        copy = pltpu.make_async_copy(chunk_ref, out_ref.at[:, lo:lo + width], done)
        copy.start()
        copy.wait()

    arrays = [table, left] + [b for _, b in held] + received
    whole = [] if result is None else [result]
    return call(
        kernel, "finish", [jax.ShapeDtypeStruct((rows, columns), BF16)], arrays,
        scratch=[pltpu.VMEM((rows, width), BF16), pltpu.SemaphoreType.DMA(())], out_specs=[unread],
        whole=whole, aliases={len(arrays): 0} if whole else {})[0]


def solution(mesh):
    n_chan, n_row = mesh.shape["chan"], mesh.shape["row"]
    chan_bits = [1 << b for b in range(n_chan.bit_length() - 1)]
    row_bits = [1 << b for b in range(n_row.bit_length() - 1)]
    far, near = chan_bits[-1], chan_bits[0]
    reduce_bits = [b for b in reversed(chan_bits) if b not in (far, near)]

    def swap(x, axis, size, bit):
        return lax.ppermute(x, axis, [(i, i ^ bit) for i in range(size)])

    def span(bits):
        targets = [0]
        for bit in bits:
            targets = targets + [t ^ bit for t in targets]
        return targets

    def split(targets, bit):
        return [t for t in targets if t & bit], [t for t in targets if not t & bit]

    def gather(block):
        other = swap(block, "chan", n_chan, far)
        beside = swap(block, "chan", n_chan, near)
        corner = swap(other, "chan", n_chan, near)
        return [(0, block), (far, other), (near, beside), (far ^ near, corner)]

    def exchange_partials(table, entries, held):
        targets, received = span(reduce_bits), []
        for bit in reduce_bits:
            sent, targets = split(targets, bit)
            part = mix(table, entries, held, sent, received)
            received.append((swap(part, "chan", n_chan, bit), [t ^ bit for t in sent]))
        return [r for r, _ in received]

    def sum_rows(multiply):
        sent, targets = split(list(range(n_row)), row_bits[0])
        parts, kept = multiply(sent, targets)
        stacks = [(kept, targets), (swap(parts, "row", n_row, row_bits[0]), targets)]
        for bit in row_bits[1:]:
            sent, targets = split(targets, bit)
            stacks.append((swap(add_up(stacks, sent), "row", n_row, bit), targets))
        return add_up(stacks, targets)[0]

    def on_device(amplitudes, block_rows, recoupling, interaction):
        rows, _, columns = amplitudes.shape
        own = amplitudes.reshape(rows, columns)
        weights = interaction.reshape(interaction.shape[0], interaction.shape[2])
        bounds = chunk_bounds(columns)
        width = bounds[0][1]
        entries = [(t, m) for t in span(reduce_bits) for m in (0, far, near, far ^ near)]
        matrix = recoupling.astype(F32)
        table_in = coefficients(matrix, n_chan, entries, width)
        table_out = coefficients(matrix.T, n_chan, entries, width)

        first, left = mask_first(block_rows, own, *bounds[0])
        gathered = [gather(first)]
        for i, bound in enumerate(bounds[1:], 1):
            after = [gathered[0][2][1]] if i == 1 else [gathered[i - 2][1][1]]
            gathered.append(gather(mask_chunk(left, own, *bound, after)))
        result = None
        for (lo, _), held in zip(bounds, gathered):
            received = exchange_partials(table_in, entries, held)
            summed = sum_rows(lambda sent, kept: mix_multiply(table_in, entries, held, received, weights, sent, kept))
            held = gather(summed)
            received = exchange_partials(table_out, entries, held)
            result = finish(table_out, entries, left, held, received, lo, columns, result)
        return result.reshape(amplitudes.shape)

    return jax.shard_map(
        on_device,
        mesh=mesh,
        in_specs=(P("row", "chan", None), P("chan"), P(), P(None, "chan", "row")),
        out_specs=P("row", "chan", None),
        check_vma=False,
    )
```

time: 143 us -> 117 us (0.82)
  waiting for transfers between devices: 61.9 us -> 41 us
  Pallas kernels: 31.7 us -> 17.6 us
  starting transfers between devices: 43.6 us -> 56.2 us
  local copies, waits for them, and re-layouts: 3.27 us -> 1.16 us
    ppermute x50, waiting for transfers between devices: 61.9 us -> 41 us  [swap(): return lax.ppermute(x, axis, [(i, i ^ bit) for i in range(size)])]
    pallas_call x45 -> x37, Pallas kernels: 31.7 us -> 17.6 us  [call(): pl.pallas_call(body, name=name, out_shape=list(out_shape), in_specs=[smem...]
    ppermute x50, starting transfers between devices: 43.6 us -> 56.2 us  [swap(): return lax.ppermute(x, axis, [(i, i ^ bit) for i in range(size)])]
    unnamed x10 -> x6, local copies, waits for them, and re-layouts: 3.27 us -> 1.09 us
  transfers between devices with their start and end apart: 50 -> 50, of which waited for: 28 -> 18; matrix products, arithmetic and copies ran while one was open for 0% -> 0% of each run, Pallas kernels for 10% -> 14%
where the time goes in v3:
time: 117 us
  starting transfers between devices  56.2 us (48%)
  waiting for transfers between devices  41 us (35%)
  Pallas kernels  17.6 us (15%)
    ppermute x50, starting transfers between devices, swap(): return lax.ppermute(x, axis, [(i, i ^ bit) for i in range(size)])  56.2 us
    ppermute x50, waiting for transfers between devices, swap(): return lax.ppermute(x, axis, [(i, i ^ bit) for i in range(size)])  41 us
    pallas_call x37, Pallas kernels, call(): pl.pallas_call(body, name=name, out_shape=list(out_shape), in_specs=[smem...  17.6 us
  transfers between devices with their start and end apart: 50, of which 18 were waited for; matrix products, arithmetic and copies ran while one was open for 0% of the time, Pallas kernels for 14%

profile of v3, /device:TPU:0, one launch (start us, length us, event | category | flops | bytes accessed | tf_op | source)
XLA Modules:
  0.0 117.1 jit_solution(14208960221007785729)
XLA Ops:
  0.7 1.1 copy-done.1
  1.8 3.0 %collective-permute-start.12 = (bf16[512,128]{1,0:T(8,128)(2,1)S(1)}, bf16[512,128]{1,0:T(8,128)(2,1)S(1)}, u32[]{:S(2)}, u32[]{:S(2)}) collective-permute-start(bf16[512,128]{1,0:T(8,128)(2,1)S(1)} %get-tuple-element.18.refs_1_), channel_id=1, source_target_pairs={{0,4},{4,0},{8,12},{12,8},{16,20},{20,16},{24,28},{28,24},{1,5},{5... | collective-permute-start | bytes 393224 | tf_op jit(solution)/shard_map/ppermute | solution.py:215
  4.8 2.6 %collective-permute-start = (bf16[512,128]{1,0:T(8,128)(2,1)S(1)}, bf16[512,128]{1,0:T(8,128)(2,1)S(1)}, u32[]{:S(2)}, u32[]{:S(2)}) collective-permute-start(bf16[512,128]{1,0:T(8,128)(2,1)S(1)} %get-tuple-element.18.refs_1_), channel_id=1, source_target_pairs={{0,16},{4,20},{8,24},{12,28},{16,0},{20,4},{24,8},{28,12},{1,17},{... | collective-permute-start | bytes 393224 | tf_op jit(solution)/shard_map/ppermute | solution.py:215
  7.4 0.9 collective-permute-done.12.refs_2_.refs_3_
  8.4 2.9 %collective-permute-start.13 = (bf16[512,128]{1,0:T(8,128)(2,1)S(1)}, bf16[512,128]{1,0:T(8,128)(2,1)S(1)}, u32[]{:S(2)}, u32[]{:S(2)}) collective-permute-start(bf16[512,128]{1,0:T(8,128)(2,1)S(1)} %mask_chunk.6.refs_1_), channel_id=1, source_target_pairs={{0,16},{4,20},{8,24},{12,28},{16,0},{20,4},{24,8},{28,12},{1,17},{... | collective-permute-start | bytes 393224 | tf_op jit(solution)/shard_map/ppermute | solution.py:215
  11.3 6.2 %collective-permute-done.refs_2_ = bf16[512,128]{1,0:T(8,128)(2,1)S(1)} collective-permute-done((bf16[512,128]{1,0:T(8,128)(2,1)S(1)}, bf16[512,128]{1,0:T(8,128)(2,1)S(1)}, u32[]{:S(2)}, u32[]{:S(2)}) %collective-permute-start) | collective-permute-done | bytes 131104 | tf_op jit(solution)/shard_map/ppermute | solution.py:215
  17.6 0.5 collective-permute-start.42
  18.2 1.6 %collective-permute-start.33 = (bf16[512,128]{1,0:T(8,128)(2,1)S(1)}, bf16[512,128]{1,0:T(8,128)(2,1)S(1)}, u32[]{:S(2)}, u32[]{:S(2)}) collective-permute-start(bf16[512,128]{1,0:T(8,128)(2,1)S(1)} %mask_chunk.6.refs_1_), channel_id=1, source_target_pairs={{0,4},{4,0},{8,12},{12,8},{16,20},{20,16},{24,28},{28,24},{1,5},{5... | collective-permute-start | bytes 393224 | tf_op jit(solution)/shard_map/ppermute | solution.py:215
  20.3 1.5 %collective-permute-start.34 = (bf16[512,128]{1,0:T(8,128)(2,1)S(1)}, bf16[512,128]{1,0:T(8,128)(2,1)S(1)}, u32[]{:S(2)}, u32[]{:S(2)}) collective-permute-start(bf16[512,128]{1,0:T(8,128)(2,1)S(1)} %collective-permute-done.13.refs_2_), channel_id=1, source_target_pairs={{0,4},{4,0},{8,12},{12,8},{16,20},{20,16},{24,28},{28,24},{1,5},{5... | collective-permute-start | bytes 393224 | tf_op jit(solution)/shard_map/ppermute | solution.py:215
  21.9 5.6 %collective-permute-done.1.refs_2_ = bf16[512,128]{1,0:T(8,128)(2,1)S(1)} collective-permute-done((bf16[512,128]{1,0:T(8,128)(2,1)S(1)}, bf16[512,128]{1,0:T(8,128)(2,1)S(1)}, u32[]{:S(2)}, u32[]{:S(2)}) %collective-permute-start.1) | collective-permute-done | bytes 131104 | tf_op jit(solution)/shard_map/ppermute | solution.py:215
  27.6 3.0 %collective-permute-start.2 = (bf16[512,128]{1,0:T(8,128)(2,1)S(1)}, bf16[512,128]{1,0:T(8,128)(2,1)S(1)}, u32[]{:S(2)}, u32[]{:S(2)}) collective-permute-start(bf16[512,128]{1,0:T(8,128)(2,1)S(1)} %mask_chunk.5.refs_1_), channel_id=1, source_target_pairs={{0,16},{4,20},{8,24},{12,28},{16,0},{20,4},{24,8},{28,12},{1,17},{... | collective-permute-start | bytes 393224 | tf_op jit(solution)/shard_map/ppermute | solution.py:215
  30.9 1.7 %collective-permute-start.3 = (bf16[512,128]{1,0:T(8,128)(2,1)S(1)}, bf16[512,128]{1,0:T(8,128)(2,1)S(1)}, u32[]{:S(2)}, u32[]{:S(2)}) collective-permute-start(bf16[512,128]{1,0:T(8,128)(2,1)S(1)} %mask_chunk.5.refs_1_), channel_id=1, source_target_pairs={{0,4},{4,0},{8,12},{12,8},{16,20},{20,16},{24,28},{28,24},{1,5},{5... | collective-permute-start | bytes 393224 | tf_op jit(solution)/shard_map/ppermute | solution.py:215
  33.0 6.0 %collective-permute-done.14.refs_2_ = bf16[512,128]{1,0:T(8,128)(2,1)S(1)} collective-permute-done((bf16[512,128]{1,0:T(8,128)(2,1)S(1)}, bf16[512,128]{1,0:T(8,128)(2,1)S(1)}, u32[]{:S(2)}, u32[]{:S(2)}) %collective-permute-start.14) | collective-permute-done | bytes 131104 | tf_op jit(solution)/shard_map/ppermute | solution.py:215
  39.3 1.0 collective-permute-done.2.refs_2_
  40.3 0.6 collective-permute-start.4
  41.0 0.6 coefficients.3.refs_0_
  41.8 3.4 %collective-permute-start.43 = (bf16[1,512,128]{2,1,0:T(8,128)(2,1)S(1)}, bf16[1,512,128]{2,1,0:T(8,128)(2,1)S(1)}, u32[]{:S(2)}, u32[]{:S(2)}) collective-permute-start(bf16[1,512,128]{2,1,0:T(8,128)(2,1)S(1)} %mix.18), channel_id=1, source_target_pairs={{0,8},{4,12},{8,0},{12,4},{16,24},{20,28},{24,16},{28,20},{1,9},{5... | collective-permute-start | bytes 393224 | tf_op jit(solution)/shard_map/ppermute | solution.py:215
  45.5 2.4 %collective-permute-start.26 = (bf16[1,512,128]{2,1,0:T(8,128)(2,1)S(1)}, bf16[1,512,128]{2,1,0:T(8,128)(2,1)S(1)}, u32[]{:S(2)}, u32[]{:S(2)}) collective-permute-start(bf16[1,512,128]{2,1,0:T(8,128)(2,1)S(1)} %mix.14), channel_id=1, source_target_pairs={{0,8},{4,12},{8,0},{12,4},{16,24},{20,28},{24,16},{28,20},{1,9},{5... | collective-permute-start | bytes 393224 | tf_op jit(solution)/shard_map/ppermute | solution.py:215
  48.4 2.1 %collective-permute-start.5 = (bf16[1,512,128]{2,1,0:T(8,128)(2,1)S(1)}, bf16[1,512,128]{2,1,0:T(8,128)(2,1)S(1)}, u32[]{:S(2)}, u32[]{:S(2)}) collective-permute-start(bf16[1,512,128]{2,1,0:T(8,128)(2,1)S(1)} %mix.10), channel_id=1, source_target_pairs={{0,8},{4,12},{8,0},{12,4},{16,24},{20,28},{24,16},{28,20},{1,9},{5... | collective-permute-start | bytes 393224 | tf_op jit(solution)/shard_map/ppermute | solution.py:215
  50.4 1.9 %mix_multiply.9 = (bf16[2,512,128]{2,1,0:T(8,128)(2,1)S(1)}, bf16[2,512,128]{2,1,0:T(8,128)(2,1)S(1)}) custom-call(f32[8,128]{1,0:T(8,128)S(1)} %coefficients.3.refs_0_, bf16[512,128]{1,0:T(8,128)(2,1)S(1)} %get-tuple-element.18.refs_1_, bf16[512,128]{1,0:T(8,128)(2,1)S(1)} %collective-permute-done.refs_2_, ...), custom_call_target="tpu_custom_call" | custom-call | tf_op jit(solution)/shard_map/mix_multiply/pallas_call | solution.py:31
  52.4 1.9 %mix_multiply.8 = (bf16[2,512,128]{2,1,0:T(8,128)(2,1)S(1)}, bf16[2,512,128]{2,1,0:T(8,128)(2,1)S(1)}) custom-call(f32[8,128]{1,0:T(8,128)S(1)} %coefficients.3.refs_0_, bf16[512,128]{1,0:T(8,128)(2,1)S(1)} %mask_chunk.6.refs_1_, bf16[512,128]{1,0:T(8,128)(2,1)S(1)} %collective-permute-done.13.refs_2_, bf16[512,128]{1,0:T(8,128)(2,1)S(1)} %collective-permute-done.33.refs_3_, ...), custom_call_target="tpu_custom_call" | custom-call | tf_op jit(solution)/shard_map/mix_multiply/pallas_call | solution.py:31
  54.3 0.5 collective-permute-start.36
  55.2 1.8 %mix_multiply.7 = (bf16[2,512,128]{2,1,0:T(8,128)(2,1)S(1)}, bf16[2,512,128]{2,1,0:T(8,128)(2,1)S(1)}) custom-call(f32[8,128]{1,0:T(8,128)S(1)} %coefficients.3.refs_0_, bf16[512,128]{1,0:T(8,128)(2,1)S(1)} %mask_chunk.4.refs_1_, bf16[512,128]{1,0:T(8,128)(2,1)S(1)} %collective-permute-done.1.refs_2_, bf16[512,128]{1,0:T(8,128)(2,1)S(1)} %collective-permute-done.24.refs_3_, ...), custom_call_target="tpu_custom_call" | custom-call | tf_op jit(solution)/shard_map/mix_multiply/pallas_call | solution.py:31
  57.1 1.9 %mix_multiply.6 = (bf16[2,512,128]{2,1,0:T(8,128)(2,1)S(1)}, bf16[2,512,128]{2,1,0:T(8,128)(2,1)S(1)}) custom-call(f32[8,128]{1,0:T(8,128)S(1)} %coefficients.3.refs_0_, bf16[512,128]{1,0:T(8,128)(2,1)S(1)} %mask_chunk.7.refs_1_, bf16[512,128]{1,0:T(8,128)(2,1)S(1)} %collective-permute-done.14.refs_2_, bf16[512,128]{1,0:T(8,128)(2,1)S(1)} %collective-permute-done.15.refs_3_, ...), custom_call_target="tpu_custom_call" | custom-call | tf_op jit(solution)/shard_map/mix_multiply/pallas_call | solution.py:31
  59.0 0.5 collective-permute-start.18
  59.5 1.9 %mix_multiply.5 = (bf16[2,512,128]{2,1,0:T(8,128)(2,1)S(1)}, bf16[2,512,128]{2,1,0:T(8,128)(2,1)S(1)}) custom-call(f32[8,128]{1,0:T(8,128)S(1)} %coefficients.3.refs_0_, bf16[512,128]{1,0:T(8,128)(2,1)S(1)} %mask_chunk.5.refs_1_, bf16[512,128]{1,0:T(8,128)(2,1)S(1)} %collective-permute-done.2.refs_2_, bf16[512,128]{1,0:T(8,128)(2,1)S(1)} %collective-permute-done.3.refs_3_, ...), custom_call_target="tpu_custom_call" | custom-call | tf_op jit(solution)/shard_map/mix_multiply/pallas_call | solution.py:31
  61.6 1.6 %collective-permute-start.45 = (bf16[1,512,128]{2,1,0:T(8,128)(2,1)S(1)}, bf16[1,512,128]{2,1,0:T(8,128)(2,1)S(1)}, u32[]{:S(2)}, u32[]{:S(2)}) collective-permute-start(bf16[1,512,128]{2,1,0:T(8,128)(2,1)S(1)} %add_up.18), channel_id=1, source_target_pairs={{0,2},{1,3},{2,0},{3,1},{4,6},{5,7},{6,4},{7,5},{8,10},{9,11},{10,... | collective-permute-start | bytes 393224 | tf_op jit(solution)/shard_map/ppermute | solution.py:215
  63.3 0.5 collective-permute-start.37
  63.9 1.6 %collective-permute-start.28 = (bf16[1,512,128]{2,1,0:T(8,128)(2,1)S(1)}, bf16[1,512,128]{2,1,0:T(8,128)(2,1)S(1)}, u32[]{:S(2)}, u32[]{:S(2)}) collective-permute-start(bf16[1,512,128]{2,1,0:T(8,128)(2,1)S(1)} %add_up.14), channel_id=1, source_target_pairs={{0,2},{1,3},{2,0},{3,1},{4,6},{5,7},{6,4},{7,5},{8,10},{9,11},{10,... | collective-permute-start | bytes 393224 | tf_op jit(solution)/shard_map/ppermute | solution.py:215
  65.6 0.5 collective-permute-start.19
  66.2 1.6 %collective-permute-start.7 = (bf16[1,512,128]{2,1,0:T(8,128)(2,1)S(1)}, bf16[1,512,128]{2,1,0:T(8,128)(2,1)S(1)}, u32[]{:S(2)}, u32[]{:S(2)}) collective-permute-start(bf16[1,512,128]{2,1,0:T(8,128)(2,1)S(1)} %add_up.10), channel_id=1, source_target_pairs={{0,2},{1,3},{2,0},{3,1},{4,6},{5,7},{6,4},{7,5},{8,10},{9,11},{10,... | collective-permute-start | bytes 393224 | tf_op jit(solution)/shard_map/ppermute | solution.py:215
  68.1 1.4 %collective-permute-start.46 = (bf16[512,128]{1,0:T(8,128)(2,1)S(1)}, bf16[512,128]{1,0:T(8,128)(2,1)S(1)}, u32[]{:S(2)}, u32[]{:S(2)}) collective-permute-start(bf16[512,128]{1,0:T(8,128)(2,1)S(1)} %bitcast.20), channel_id=1, source_target_pairs={{0,16},{4,20},{8,24},{12,28},{16,0},{20,4},{24,8},{28,12},{1,17},{... | collective-permute-start | bytes 393224 | tf_op jit(solution)/shard_map/ppermute | solution.py:215
  69.5 1.3 %collective-permute-done.37.refs_2_ = bf16[1,512,128]{2,1,0:T(8,128)(2,1)S(1)} collective-permute-done((bf16[1,512,128]{2,1,0:T(8,128)(2,1)S(1)}, bf16[1,512,128]{2,1,0:T(8,128)(2,1)S(1)}, u32[]{:S(2)}, u32[]{:S(2)}) %collective-permute-start.37) | collective-permute-done | bytes 131104 | tf_op jit(solution)/shard_map/ppermute | solution.py:215
  70.8 0.6 collective-permute-start.47
  71.5 2.1 %collective-permute-done.28.refs_2_ = bf16[1,512,128]{2,1,0:T(8,128)(2,1)S(1)} collective-permute-done((bf16[1,512,128]{2,1,0:T(8,128)(2,1)S(1)}, bf16[1,512,128]{2,1,0:T(8,128)(2,1)S(1)}, u32[]{:S(2)}, u32[]{:S(2)}) %collective-permute-start.28) | collective-permute-done | bytes 131104 | tf_op jit(solution)/shard_map/ppermute | solution.py:215
  73.6 1.3 %collective-permute-start.38 = (bf16[512,128]{1,0:T(8,128)(2,1)S(1)}, bf16[512,128]{1,0:T(8,128)(2,1)S(1)}, u32[]{:S(2)}, u32[]{:S(2)}) collective-permute-start(bf16[512,128]{1,0:T(8,128)(2,1)S(1)} %bitcast.24), channel_id=1, source_target_pairs={{0,16},{4,20},{8,24},{12,28},{16,0},{20,4},{24,8},{28,12},{1,17},{... | collective-permute-start | bytes 393224 | tf_op jit(solution)/shard_map/ppermute | solution.py:215
  75.0 1.4 %collective-permute-done.19.refs_2_ = bf16[1,512,128]{2,1,0:T(8,128)(2,1)S(1)} collective-permute-done((bf16[1,512,128]{2,1,0:T(8,128)(2,1)S(1)}, bf16[1,512,128]{2,1,0:T(8,128)(2,1)S(1)}, u32[]{:S(2)}, u32[]{:S(2)}) %collective-permute-start.19) | collective-permute-done | bytes 131104 | tf_op jit(solution)/shard_map/ppermute | solution.py:215
  76.4 0.6 collective-permute-start.39
  77.0 1.8 %collective-permute-done.7.refs_2_ = bf16[1,512,128]{2,1,0:T(8,128)(2,1)S(1)} collective-permute-done((bf16[1,512,128]{2,1,0:T(8,128)(2,1)S(1)}, bf16[1,512,128]{2,1,0:T(8,128)(2,1)S(1)}, u32[]{:S(2)}, u32[]{:S(2)}) %collective-permute-start.7) | collective-permute-done | bytes 131104 | tf_op jit(solution)/shard_map/ppermute | solution.py:215
  78.8 1.2 %collective-permute-start.29 = (bf16[512,128]{1,0:T(8,128)(2,1)S(1)}, bf16[512,128]{1,0:T(8,128)(2,1)S(1)}, u32[]{:S(2)}, u32[]{:S(2)}) collective-permute-start(bf16[512,128]{1,0:T(8,128)(2,1)S(1)} %bitcast.28), channel_id=1, source_target_pairs={{0,16},{4,20},{8,24},{12,28},{16,0},{20,4},{24,8},{28,12},{1,17},{... | collective-permute-start | bytes 393224 | tf_op jit(solution)/shard_map/ppermute | solution.py:215
  80.2 0.5 collective-permute-start.30
  80.7 1.6 %collective-permute-start.48 = (bf16[512,128]{1,0:T(8,128)(2,1)S(1)}, bf16[512,128]{1,0:T(8,128)(2,1)S(1)}, u32[]{:S(2)}, u32[]{:S(2)}) collective-permute-start(bf16[512,128]{1,0:T(8,128)(2,1)S(1)} %collective-permute-done.46.refs_2_.refs_3_), channel_id=1, source_target_pairs={{0,4},{4,0},{8,12},{12,8},{16,20},{20,16},{24,28},{28,24},{1,5},{5... | collective-permute-start | bytes 393224 | tf_op jit(solution)/shard_map/ppermute | solution.py:215
  82.3 1.7 %collective-permute-start.20 = (bf16[512,128]{1,0:T(8,128)(2,1)S(1)}, bf16[512,128]{1,0:T(8,128)(2,1)S(1)}, u32[]{:S(2)}, u32[]{:S(2)}) collective-permute-start(bf16[512,128]{1,0:T(8,128)(2,1)S(1)} %bitcast.36), channel_id=1, source_target_pairs={{0,16},{4,20},{8,24},{12,28},{16,0},{20,4},{24,8},{28,12},{1,17},{... | collective-permute-start | bytes 393224 | tf_op jit(solution)/shard_map/ppermute | solution.py:215
  84.0 0.6 collective-permute-start.40
  84.6 6.9 %collective-permute-done.29.refs_2_.refs_3_ = bf16[512,128]{1,0:T(8,128)(2,1)S(1)} collective-permute-done((bf16[512,128]{1,0:T(8,128)(2,1)S(1)}, bf16[512,128]{1,0:T(8,128)(2,1)S(1)}, u32[]{:S(2)}, u32[]{:S(2)}) %collective-permute-start.29) | collective-permute-done | bytes 131104 | tf_op jit(solution)/shard_map/ppermute | solution.py:215
  91.5 0.5 collective-permute-start.31
  92.0 1.5 %collective-permute-start.21 = (bf16[512,128]{1,0:T(8,128)(2,1)S(1)}, bf16[512,128]{1,0:T(8,128)(2,1)S(1)}, u32[]{:S(2)}, u32[]{:S(2)}) collective-permute-start(bf16[512,128]{1,0:T(8,128)(2,1)S(1)} %bitcast.37), channel_id=1, source_target_pairs={{0,4},{4,0},{8,12},{12,8},{16,20},{20,16},{24,28},{28,24},{1,5},{5... | collective-permute-start | bytes 393224 | tf_op jit(solution)/shard_map/ppermute | solution.py:215
  93.5 3.6 %collective-permute-done.20.refs_2_.refs_3_ = bf16[512,128]{1,0:T(8,128)(2,1)S(1)} collective-permute-done((bf16[512,128]{1,0:T(8,128)(2,1)S(1)}, bf16[512,128]{1,0:T(8,128)(2,1)S(1)}, u32[]{:S(2)}, u32[]{:S(2)}) %collective-permute-start.20) | collective-permute-done | bytes 131104 | tf_op jit(solution)/shard_map/ppermute | solution.py:215
  97.1 0.5 collective-permute-start.22
  97.6 1.5 %collective-permute-start.9 = (bf16[512,128]{1,0:T(8,128)(2,1)S(1)}, bf16[512,128]{1,0:T(8,128)(2,1)S(1)}, u32[]{:S(2)}, u32[]{:S(2)}) collective-permute-start(bf16[512,128]{1,0:T(8,128)(2,1)S(1)} %bitcast.33), channel_id=1, source_target_pairs={{0,4},{4,0},{8,12},{12,8},{16,20},{20,16},{24,28},{28,24},{1,5},{5... | collective-permute-start | bytes 393224 | tf_op jit(solution)/shard_map/ppermute | solution.py:215
  99.1 0.5 collective-permute-start.10
  99.7 0.6 coefficients.2.refs_0_
  100.9 2.1 %collective-permute-start.41 = (bf16[1,512,128]{2,1,0:T(8,128)(2,1)S(1)}, bf16[1,512,128]{2,1,0:T(8,128)(2,1)S(1)}, u32[]{:S(2)}, u32[]{:S(2)}) collective-permute-start(bf16[1,512,128]{2,1,0:T(8,128)(2,1)S(1)} %mix.17), channel_id=1, source_target_pairs={{0,8},{4,12},{8,0},{12,4},{16,24},{20,28},{24,16},{28,20},{1,9},{5... | collective-permute-start | bytes 393224 | tf_op jit(solution)/shard_map/ppermute | solution.py:215
  103.4 1.9 %collective-permute-start.32 = (bf16[1,512,128]{2,1,0:T(8,128)(2,1)S(1)}, bf16[1,512,128]{2,1,0:T(8,128)(2,1)S(1)}, u32[]{:S(2)}, u32[]{:S(2)}) collective-permute-start(bf16[1,512,128]{2,1,0:T(8,128)(2,1)S(1)} %mix.15), channel_id=1, source_target_pairs={{0,8},{4,12},{8,0},{12,4},{16,24},{20,28},{24,16},{28,20},{1,9},{5... | collective-permute-start | bytes 393224 | tf_op jit(solution)/shard_map/ppermute | solution.py:215
  105.5 2.4 %collective-permute-start.23 = (bf16[1,512,128]{2,1,0:T(8,128)(2,1)S(1)}, bf16[1,512,128]{2,1,0:T(8,128)(2,1)S(1)}, u32[]{:S(2)}, u32[]{:S(2)}) collective-permute-start(bf16[1,512,128]{2,1,0:T(8,128)(2,1)S(1)} %mix.13), channel_id=1, source_target_pairs={{0,8},{4,12},{8,0},{12,4},{16,24},{20,28},{24,16},{28,20},{1,9},{5... | collective-permute-start | bytes 393224 | tf_op jit(solution)/shard_map/ppermute | solution.py:215
  108.1 1.5 %collective-permute-start.11 = (bf16[1,512,128]{2,1,0:T(8,128)(2,1)S(1)}, bf16[1,512,128]{2,1,0:T(8,128)(2,1)S(1)}, u32[]{:S(2)}, u32[]{:S(2)}) collective-permute-start(bf16[1,512,128]{2,1,0:T(8,128)(2,1)S(1)} %mix.11), channel_id=1, source_target_pairs={{0,8},{4,12},{8,0},{12,4},{16,24},{20,28},{24,16},{28,20},{1,9},{5... | collective-permute-start | bytes 393224 | tf_op jit(solution)/shard_map/ppermute | solution.py:215
  109.5 0.9 finish.5.refs_7_
  110.4 0.9 finish.6.refs_7_
  111.3 1.5 %collective-permute-done.32.refs_6_ = bf16[1,512,128]{2,1,0:T(8,128)(2,1)S(1)} collective-permute-done((bf16[1,512,128]{2,1,0:T(8,128)(2,1)S(1)}, bf16[1,512,128]{2,1,0:T(8,128)(2,1)S(1)}, u32[]{:S(2)}, u32[]{:S(2)}) %collective-permute-start.32) | collective-permute-done | bytes 131104 | tf_op jit(solution)/shard_map/ppermute | solution.py:215
  112.8 0.9 finish.7.refs_7_
  113.6 1.2 %collective-permute-done.23.refs_6_ = bf16[1,512,128]{2,1,0:T(8,128)(2,1)S(1)} collective-permute-done((bf16[1,512,128]{2,1,0:T(8,128)(2,1)S(1)}, bf16[1,512,128]{2,1,0:T(8,128)(2,1)S(1)}, u32[]{:S(2)}, u32[]{:S(2)}) %collective-permute-start.23) | collective-permute-done | bytes 131104 | tf_op jit(solution)/shard_map/ppermute | solution.py:215
  114.9 0.9 finish.8.refs_7_
  115.7 0.5 collective-permute-done.11.refs_6_
  116.3 0.9 finish.9
  (81 shorter events, 5.9 us)
Async XLA Ops:
  0.7 1.1 copy-start.1
  1.7 39.2 %copy-start.2 = (bf16[8,8]{1,0:T(8,128)(2,1)S(1)}, bf16[8,8]{1,0:T(8,128)(2,1)}, u32[]{:S(2)}) copy-start(bf16[8,8]{1,0:T(8,128)(2,1)} %param.6) | copy-start | bytes 388
  1.8 6.5 %collective-permute-start.12 = (bf16[512,128]{1,0:T(8,128)(2,1)S(1)}, bf16[512,128]{1,0:T(8,128)(2,1)S(1)}, u32[]{:S(2)}, u32[]{:S(2)}) collective-permute-start(bf16[512,128]{1,0:T(8,128)(2,1)S(1)} %get-tuple-element.18.refs_1_), channel_id=1, source_target_pairs={{0,4},{4,0},{8,12},{12,8},{16,20},{20,16},{24,28},{28,24},{1,5},{5... | collective-permute-start | bytes 393224 | tf_op jit(solution)/shard_map/ppermute | solution.py:215
  4.8 12.6 %collective-permute-start = (bf16[512,128]{1,0:T(8,128)(2,1)S(1)}, bf16[512,128]{1,0:T(8,128)(2,1)S(1)}, u32[]{:S(2)}, u32[]{:S(2)}) collective-permute-start(bf16[512,128]{1,0:T(8,128)(2,1)S(1)} %get-tuple-element.18.refs_1_), channel_id=1, source_target_pairs={{0,16},{4,20},{8,24},{12,28},{16,0},{20,4},{24,8},{28,12},{1,17},{... | collective-permute-start | bytes 393224 | tf_op jit(solution)/shard_map/ppermute | solution.py:215
  8.4 11.9 %collective-permute-start.13 = (bf16[512,128]{1,0:T(8,128)(2,1)S(1)}, bf16[512,128]{1,0:T(8,128)(2,1)S(1)}, u32[]{:S(2)}, u32[]{:S(2)}) collective-permute-start(bf16[512,128]{1,0:T(8,128)(2,1)S(1)} %mask_chunk.6.refs_1_), channel_id=1, source_target_pairs={{0,16},{4,20},{8,24},{12,28},{16,0},{20,4},{24,8},{28,12},{1,17},{... | collective-permute-start | bytes 393224 | tf_op jit(solution)/shard_map/ppermute | solution.py:215
  17.6 9.9 %collective-permute-start.1 = (bf16[512,128]{1,0:T(8,128)(2,1)S(1)}, bf16[512,128]{1,0:T(8,128)(2,1)S(1)}, u32[]{:S(2)}, u32[]{:S(2)}) collective-permute-start(bf16[512,128]{1,0:T(8,128)(2,1)S(1)} %mask_chunk.4.refs_1_), channel_id=1, source_target_pairs={{0,16},{4,20},{8,24},{12,28},{16,0},{20,4},{24,8},{28,12},{1,17},{... | collective-permute-start | bytes 393224 | tf_op jit(solution)/shard_map/ppermute | solution.py:215
  17.6 9.9 %collective-permute-start.42 = (bf16[512,128]{1,0:T(8,128)(2,1)S(1)}, bf16[512,128]{1,0:T(8,128)(2,1)S(1)}, u32[]{:S(2)}, u32[]{:S(2)}) collective-permute-start(bf16[512,128]{1,0:T(8,128)(2,1)S(1)} %collective-permute-done.refs_2_), channel_id=1, source_target_pairs={{0,4},{4,0},{8,12},{12,8},{16,20},{20,16},{24,28},{28,24},{1,5},{5... | collective-permute-start | bytes 393224 | tf_op jit(solution)/shard_map/ppermute | solution.py:215
  18.2 12.4 %collective-permute-start.33 = (bf16[512,128]{1,0:T(8,128)(2,1)S(1)}, bf16[512,128]{1,0:T(8,128)(2,1)S(1)}, u32[]{:S(2)}, u32[]{:S(2)}) collective-permute-start(bf16[512,128]{1,0:T(8,128)(2,1)S(1)} %mask_chunk.6.refs_1_), channel_id=1, source_target_pairs={{0,4},{4,0},{8,12},{12,8},{16,20},{20,16},{24,28},{28,24},{1,5},{5... | collective-permute-start | bytes 393224 | tf_op jit(solution)/shard_map/ppermute | solution.py:215
  19.7 11.2 %collective-permute-start.24 = (bf16[512,128]{1,0:T(8,128)(2,1)S(1)}, bf16[512,128]{1,0:T(8,128)(2,1)S(1)}, u32[]{:S(2)}, u32[]{:S(2)}) collective-permute-start(bf16[512,128]{1,0:T(8,128)(2,1)S(1)} %mask_chunk.4.refs_1_), channel_id=1, source_target_pairs={{0,4},{4,0},{8,12},{12,8},{16,20},{20,16},{24,28},{28,24},{1,5},{5... | collective-permute-start | bytes 393224 | tf_op jit(solution)/shard_map/ppermute | solution.py:215
  20.3 12.3 %collective-permute-start.34 = (bf16[512,128]{1,0:T(8,128)(2,1)S(1)}, bf16[512,128]{1,0:T(8,128)(2,1)S(1)}, u32[]{:S(2)}, u32[]{:S(2)}) collective-permute-start(bf16[512,128]{1,0:T(8,128)(2,1)S(1)} %collective-permute-done.13.refs_2_), channel_id=1, source_target_pairs={{0,4},{4,0},{8,12},{12,8},{16,20},{20,16},{24,28},{28,24},{1,5},{5... | collective-permute-start | bytes 393224 | tf_op jit(solution)/shard_map/ppermute | solution.py:215
  21.9 28.6 %copy-start = (bf16[2048,1,512]{2,0,1:T(8,128)(2,1)S(1)}, bf16[2048,1,512]{2,0,1:T(8,128)(2,1)}, u32[]{:S(2)}) copy-start(bf16[2048,1,512]{2,0,1:T(8,128)(2,1)} %param.7) | copy-start | bytes 6291460
  27.5 11.5 %collective-permute-start.14 = (bf16[512,128]{1,0:T(8,128)(2,1)S(1)}, bf16[512,128]{1,0:T(8,128)(2,1)S(1)}, u32[]{:S(2)}, u32[]{:S(2)}) collective-permute-start(bf16[512,128]{1,0:T(8,128)(2,1)S(1)} %mask_chunk.7.refs_1_), channel_id=1, source_target_pairs={{0,16},{4,20},{8,24},{12,28},{16,0},{20,4},{24,8},{28,12},{1,17},{... | collective-permute-start | bytes 393224 | tf_op jit(solution)/shard_map/ppermute | solution.py:215
  27.6 12.8 %collective-permute-start.2 = (bf16[512,128]{1,0:T(8,128)(2,1)S(1)}, bf16[512,128]{1,0:T(8,128)(2,1)S(1)}, u32[]{:S(2)}, u32[]{:S(2)}) collective-permute-start(bf16[512,128]{1,0:T(8,128)(2,1)S(1)} %mask_chunk.5.refs_1_), channel_id=1, source_target_pairs={{0,16},{4,20},{8,24},{12,28},{16,0},{20,4},{24,8},{28,12},{1,17},{... | collective-permute-start | bytes 393224 | tf_op jit(solution)/shard_map/ppermute | solution.py:215
  30.6 14.7 %collective-permute-start.15 = (bf16[512,128]{1,0:T(8,128)(2,1)S(1)}, bf16[512,128]{1,0:T(8,128)(2,1)S(1)}, u32[]{:S(2)}, u32[]{:S(2)}) collective-permute-start(bf16[512,128]{1,0:T(8,128)(2,1)S(1)} %mask_chunk.7.refs_1_), channel_id=1, source_target_pairs={{0,4},{4,0},{8,12},{12,8},{16,20},{20,16},{24,28},{28,24},{1,5},{5... | collective-permute-start | bytes 393224 | tf_op jit(solution)/shard_map/ppermute | solution.py:215
  30.9 17.2 %collective-permute-start.3 = (bf16[512,128]{1,0:T(8,128)(2,1)S(1)}, bf16[512,128]{1,0:T(8,128)(2,1)S(1)}, u32[]{:S(2)}, u32[]{:S(2)}) collective-permute-start(bf16[512,128]{1,0:T(8,128)(2,1)S(1)} %mask_chunk.5.refs_1_), channel_id=1, source_target_pairs={{0,4},{4,0},{8,12},{12,8},{16,20},{20,16},{24,28},{28,24},{1,5},{5... | collective-permute-start | bytes 393224 | tf_op jit(solution)/shard_map/ppermute | solution.py:215
  32.6 9.2 %collective-permute-start.25 = (bf16[512,128]{1,0:T(8,128)(2,1)S(1)}, bf16[512,128]{1,0:T(8,128)(2,1)S(1)}, u32[]{:S(2)}, u32[]{:S(2)}) collective-permute-start(bf16[512,128]{1,0:T(8,128)(2,1)S(1)} %collective-permute-done.1.refs_2_), channel_id=1, source_target_pairs={{0,4},{4,0},{8,12},{12,8},{16,20},{20,16},{24,28},{28,24},{1,5},{5... | collective-permute-start | bytes 393224 | tf_op jit(solution)/shard_map/ppermute | solution.py:215
  38.9 6.6 %collective-permute-start.16 = (bf16[512,128]{1,0:T(8,128)(2,1)S(1)}, bf16[512,128]{1,0:T(8,128)(2,1)S(1)}, u32[]{:S(2)}, u32[]{:S(2)}) collective-permute-start(bf16[512,128]{1,0:T(8,128)(2,1)S(1)} %collective-permute-done.14.refs_2_), channel_id=1, source_target_pairs={{0,4},{4,0},{8,12},{12,8},{16,20},{20,16},{24,28},{28,24},{1,5},{5... | collective-permute-start | bytes 393224 | tf_op jit(solution)/shard_map/ppermute | solution.py:215
  40.3 7.9 %collective-permute-start.4 = (bf16[512,128]{1,0:T(8,128)(2,1)S(1)}, bf16[512,128]{1,0:T(8,128)(2,1)S(1)}, u32[]{:S(2)}, u32[]{:S(2)}) collective-permute-start(bf16[512,128]{1,0:T(8,128)(2,1)S(1)} %collective-permute-done.2.refs_2_), channel_id=1, source_target_pairs={{0,4},{4,0},{8,12},{12,8},{16,20},{20,16},{24,28},{28,24},{1,5},{5... | collective-permute-start | bytes 393224 | tf_op jit(solution)/shard_map/ppermute | solution.py:215
  41.8 8.7 %collective-permute-start.43 = (bf16[1,512,128]{2,1,0:T(8,128)(2,1)S(1)}, bf16[1,512,128]{2,1,0:T(8,128)(2,1)S(1)}, u32[]{:S(2)}, u32[]{:S(2)}) collective-permute-start(bf16[1,512,128]{2,1,0:T(8,128)(2,1)S(1)} %mix.18), channel_id=1, source_target_pairs={{0,8},{4,12},{8,0},{12,4},{16,24},{20,28},{24,16},{28,20},{1,9},{5... | collective-permute-start | bytes 393224 | tf_op jit(solution)/shard_map/ppermute | solution.py:215
  45.3 7.1 %collective-permute-start.35 = (bf16[1,512,128]{2,1,0:T(8,128)(2,1)S(1)}, bf16[1,512,128]{2,1,0:T(8,128)(2,1)S(1)}, u32[]{:S(2)}, u32[]{:S(2)}) collective-permute-start(bf16[1,512,128]{2,1,0:T(8,128)(2,1)S(1)} %mix.16), channel_id=1, source_target_pairs={{0,8},{4,12},{8,0},{12,4},{16,24},{20,28},{24,16},{28,20},{1,9},{5... | collective-permute-start | bytes 393224 | tf_op jit(solution)/shard_map/ppermute | solution.py:215
  45.5 9.6 %collective-permute-start.26 = (bf16[1,512,128]{2,1,0:T(8,128)(2,1)S(1)}, bf16[1,512,128]{2,1,0:T(8,128)(2,1)S(1)}, u32[]{:S(2)}, u32[]{:S(2)}) collective-permute-start(bf16[1,512,128]{2,1,0:T(8,128)(2,1)S(1)} %mix.14), channel_id=1, source_target_pairs={{0,8},{4,12},{8,0},{12,4},{16,24},{20,28},{24,16},{28,20},{1,9},{5... | collective-permute-start | bytes 393224 | tf_op jit(solution)/shard_map/ppermute | solution.py:215
  48.1 9.0 %collective-permute-start.17 = (bf16[1,512,128]{2,1,0:T(8,128)(2,1)S(1)}, bf16[1,512,128]{2,1,0:T(8,128)(2,1)S(1)}, u32[]{:S(2)}, u32[]{:S(2)}) collective-permute-start(bf16[1,512,128]{2,1,0:T(8,128)(2,1)S(1)} %mix.12), channel_id=1, source_target_pairs={{0,8},{4,12},{8,0},{12,4},{16,24},{20,28},{24,16},{28,20},{1,9},{5... | collective-permute-start | bytes 393224 | tf_op jit(solution)/shard_map/ppermute | solution.py:215
  48.4 11.1 %collective-permute-start.5 = (bf16[1,512,128]{2,1,0:T(8,128)(2,1)S(1)}, bf16[1,512,128]{2,1,0:T(8,128)(2,1)S(1)}, u32[]{:S(2)}, u32[]{:S(2)}) collective-permute-start(bf16[1,512,128]{2,1,0:T(8,128)(2,1)S(1)} %mix.10), channel_id=1, source_target_pairs={{0,8},{4,12},{8,0},{12,4},{16,24},{20,28},{24,16},{28,20},{1,9},{5... | collective-permute-start | bytes 393224 | tf_op jit(solution)/shard_map/ppermute | solution.py:215
  52.3 9.2 %collective-permute-start.44 = (bf16[2,512,128]{2,1,0:T(8,128)(2,1)S(1)}, bf16[2,512,128]{2,1,0:T(8,128)(2,1)S(1)}, u32[]{:S(2)}, u32[]{:S(2)}) collective-permute-start(bf16[2,512,128]{2,1,0:T(8,128)(2,1)S(1)} %get-tuple-element.28), channel_id=1, source_target_pairs={{0,1},{1,0},{2,3},{3,2},{4,5},{5,4},{6,7},{7,6},{8,9},{9,8},{10,11... | collective-permute-start | bytes 786440 | tf_op jit(solution)/shard_map/ppermute | solution.py:215
  54.3 8.9 %collective-permute-start.36 = (bf16[2,512,128]{2,1,0:T(8,128)(2,1)S(1)}, bf16[2,512,128]{2,1,0:T(8,128)(2,1)S(1)}, u32[]{:S(2)}, u32[]{:S(2)}) collective-permute-start(bf16[2,512,128]{2,1,0:T(8,128)(2,1)S(1)} %get-tuple-element.26), channel_id=1, source_target_pairs={{0,1},{1,0},{2,3},{3,2},{4,5},{5,4},{6,7},{7,6},{8,9},{9,8},{10,11... | collective-permute-start | bytes 786440 | tf_op jit(solution)/shard_map/ppermute | solution.py:215
  57.0 6.8 %collective-permute-start.27 = (bf16[2,512,128]{2,1,0:T(8,128)(2,1)S(1)}, bf16[2,512,128]{2,1,0:T(8,128)(2,1)S(1)}, u32[]{:S(2)}, u32[]{:S(2)}) collective-permute-start(bf16[2,512,128]{2,1,0:T(8,128)(2,1)S(1)} %get-tuple-element.24), channel_id=1, source_target_pairs={{0,1},{1,0},{2,3},{3,2},{4,5},{5,4},{6,7},{7,6},{8,9},{9,8},{10,11... | collective-permute-start | bytes 786440 | tf_op jit(solution)/shard_map/ppermute | solution.py:215
  59.0 6.6 %collective-permute-start.18 = (bf16[2,512,128]{2,1,0:T(8,128)(2,1)S(1)}, bf16[2,512,128]{2,1,0:T(8,128)(2,1)S(1)}, u32[]{:S(2)}, u32[]{:S(2)}) collective-permute-start(bf16[2,512,128]{2,1,0:T(8,128)(2,1)S(1)} %get-tuple-element.22), channel_id=1, source_target_pairs={{0,1},{1,0},{2,3},{3,2},{4,5},{5,4},{6,7},{7,6},{8,9},{9,8},{10,11... | collective-permute-start | bytes 786440 | tf_op jit(solution)/shard_map/ppermute | solution.py:215
  61.4 4.8 %collective-permute-start.6 = (bf16[2,512,128]{2,1,0:T(8,128)(2,1)S(1)}, bf16[2,512,128]{2,1,0:T(8,128)(2,1)S(1)}, u32[]{:S(2)}, u32[]{:S(2)}) collective-permute-start(bf16[2,512,128]{2,1,0:T(8,128)(2,1)S(1)} %get-tuple-element.20), channel_id=1, source_target_pairs={{0,1},{1,0},{2,3},{3,2},{4,5},{5,4},{6,7},{7,6},{8,9},{9,8},{10,11... | collective-permute-start | bytes 786440 | tf_op jit(solution)/shard_map/ppermute | solution.py:215
  61.6 6.4 %collective-permute-start.45 = (bf16[1,512,128]{2,1,0:T(8,128)(2,1)S(1)}, bf16[1,512,128]{2,1,0:T(8,128)(2,1)S(1)}, u32[]{:S(2)}, u32[]{:S(2)}) collective-permute-start(bf16[1,512,128]{2,1,0:T(8,128)(2,1)S(1)} %add_up.18), channel_id=1, source_target_pairs={{0,2},{1,3},{2,0},{3,1},{4,6},{5,7},{6,4},{7,5},{8,10},{9,11},{10,... | collective-permute-start | bytes 393224 | tf_op jit(solution)/shard_map/ppermute | solution.py:215
  63.3 7.5 %collective-permute-start.37 = (bf16[1,512,128]{2,1,0:T(8,128)(2,1)S(1)}, bf16[1,512,128]{2,1,0:T(8,128)(2,1)S(1)}, u32[]{:S(2)}, u32[]{:S(2)}) collective-permute-start(bf16[1,512,128]{2,1,0:T(8,128)(2,1)S(1)} %add_up.16), channel_id=1, source_target_pairs={{0,2},{1,3},{2,0},{3,1},{4,6},{5,7},{6,4},{7,5},{8,10},{9,11},{10,... | collective-permute-start | bytes 393224 | tf_op jit(solution)/shard_map/ppermute | solution.py:215
  63.9 9.7 %collective-permute-start.28 = (bf16[1,512,128]{2,1,0:T(8,128)(2,1)S(1)}, bf16[1,512,128]{2,1,0:T(8,128)(2,1)S(1)}, u32[]{:S(2)}, u32[]{:S(2)}) collective-permute-start(bf16[1,512,128]{2,1,0:T(8,128)(2,1)S(1)} %add_up.14), channel_id=1, source_target_pairs={{0,2},{1,3},{2,0},{3,1},{4,6},{5,7},{6,4},{7,5},{8,10},{9,11},{10,... | collective-permute-start | bytes 393224 | tf_op jit(solution)/shard_map/ppermute | solution.py:215
  65.6 10.8 %collective-permute-start.19 = (bf16[1,512,128]{2,1,0:T(8,128)(2,1)S(1)}, bf16[1,512,128]{2,1,0:T(8,128)(2,1)S(1)}, u32[]{:S(2)}, u32[]{:S(2)}) collective-permute-start(bf16[1,512,128]{2,1,0:T(8,128)(2,1)S(1)} %add_up.12), channel_id=1, source_target_pairs={{0,2},{1,3},{2,0},{3,1},{4,6},{5,7},{6,4},{7,5},{8,10},{9,11},{10,... | collective-permute-start | bytes 393224 | tf_op jit(solution)/shard_map/ppermute | solution.py:215
  66.2 12.5 %collective-permute-start.7 = (bf16[1,512,128]{2,1,0:T(8,128)(2,1)S(1)}, bf16[1,512,128]{2,1,0:T(8,128)(2,1)S(1)}, u32[]{:S(2)}, u32[]{:S(2)}) collective-permute-start(bf16[1,512,128]{2,1,0:T(8,128)(2,1)S(1)} %add_up.10), channel_id=1, source_target_pairs={{0,2},{1,3},{2,0},{3,1},{4,6},{5,7},{6,4},{7,5},{8,10},{9,11},{10,... | collective-permute-start | bytes 393224 | tf_op jit(solution)/shard_map/ppermute | solution.py:215
  68.1 12.1 %collective-permute-start.46 = (bf16[512,128]{1,0:T(8,128)(2,1)S(1)}, bf16[512,128]{1,0:T(8,128)(2,1)S(1)}, u32[]{:S(2)}, u32[]{:S(2)}) collective-permute-start(bf16[512,128]{1,0:T(8,128)(2,1)S(1)} %bitcast.20), channel_id=1, source_target_pairs={{0,16},{4,20},{8,24},{12,28},{16,0},{20,4},{24,8},{28,12},{1,17},{... | collective-permute-start | bytes 393224 | tf_op jit(solution)/shard_map/ppermute | solution.py:215
  70.8 9.9 %collective-permute-start.47 = (bf16[512,128]{1,0:T(8,128)(2,1)S(1)}, bf16[512,128]{1,0:T(8,128)(2,1)S(1)}, u32[]{:S(2)}, u32[]{:S(2)}) collective-permute-start(bf16[512,128]{1,0:T(8,128)(2,1)S(1)} %bitcast.21), channel_id=1, source_target_pairs={{0,4},{4,0},{8,12},{12,8},{16,20},{20,16},{24,28},{28,24},{1,5},{5... | collective-permute-start | bytes 393224 | tf_op jit(solution)/shard_map/ppermute | solution.py:215
  73.6 8.7 %collective-permute-start.38 = (bf16[512,128]{1,0:T(8,128)(2,1)S(1)}, bf16[512,128]{1,0:T(8,128)(2,1)S(1)}, u32[]{:S(2)}, u32[]{:S(2)}) collective-permute-start(bf16[512,128]{1,0:T(8,128)(2,1)S(1)} %bitcast.24), channel_id=1, source_target_pairs={{0,16},{4,20},{8,24},{12,28},{16,0},{20,4},{24,8},{28,12},{1,17},{... | collective-permute-start | bytes 393224 | tf_op jit(solution)/shard_map/ppermute | solution.py:215
  76.4 7.6 %collective-permute-start.39 = (bf16[512,128]{1,0:T(8,128)(2,1)S(1)}, bf16[512,128]{1,0:T(8,128)(2,1)S(1)}, u32[]{:S(2)}, u32[]{:S(2)}) collective-permute-start(bf16[512,128]{1,0:T(8,128)(2,1)S(1)} %bitcast.25), channel_id=1, source_target_pairs={{0,4},{4,0},{8,12},{12,8},{16,20},{20,16},{24,28},{28,24},{1,5},{5... | collective-permute-start | bytes 393224 | tf_op jit(solution)/shard_map/ppermute | solution.py:215
  78.8 12.7 %collective-permute-start.29 = (bf16[512,128]{1,0:T(8,128)(2,1)S(1)}, bf16[512,128]{1,0:T(8,128)(2,1)S(1)}, u32[]{:S(2)}, u32[]{:S(2)}) collective-permute-start(bf16[512,128]{1,0:T(8,128)(2,1)S(1)} %bitcast.28), channel_id=1, source_target_pairs={{0,16},{4,20},{8,24},{12,28},{16,0},{20,4},{24,8},{28,12},{1,17},{... | collective-permute-start | bytes 393224 | tf_op jit(solution)/shard_map/ppermute | solution.py:215
  80.2 11.3 %collective-permute-start.30 = (bf16[512,128]{1,0:T(8,128)(2,1)S(1)}, bf16[512,128]{1,0:T(8,128)(2,1)S(1)}, u32[]{:S(2)}, u32[]{:S(2)}) collective-permute-start(bf16[512,128]{1,0:T(8,128)(2,1)S(1)} %bitcast.29), channel_id=1, source_target_pairs={{0,4},{4,0},{8,12},{12,8},{16,20},{20,16},{24,28},{28,24},{1,5},{5... | collective-permute-start | bytes 393224 | tf_op jit(solution)/shard_map/ppermute | solution.py:215
  80.7 11.3 %collective-permute-start.48 = (bf16[512,128]{1,0:T(8,128)(2,1)S(1)}, bf16[512,128]{1,0:T(8,128)(2,1)S(1)}, u32[]{:S(2)}, u32[]{:S(2)}) collective-permute-start(bf16[512,128]{1,0:T(8,128)(2,1)S(1)} %collective-permute-done.46.refs_2_.refs_3_), channel_id=1, source_target_pairs={{0,4},{4,0},{8,12},{12,8},{16,20},{20,16},{24,28},{28,24},{1,5},{5... | collective-permute-start | bytes 393224 | tf_op jit(solution)/shard_map/ppermute | solution.py:215
  82.3 14.8 %collective-permute-start.20 = (bf16[512,128]{1,0:T(8,128)(2,1)S(1)}, bf16[512,128]{1,0:T(8,128)(2,1)S(1)}, u32[]{:S(2)}, u32[]{:S(2)}) collective-permute-start(bf16[512,128]{1,0:T(8,128)(2,1)S(1)} %bitcast.36), channel_id=1, source_target_pairs={{0,16},{4,20},{8,24},{12,28},{16,0},{20,4},{24,8},{28,12},{1,17},{... | collective-permute-start | bytes 393224 | tf_op jit(solution)/shard_map/ppermute | solution.py:215
  84.0 13.6 %collective-permute-start.40 = (bf16[512,128]{1,0:T(8,128)(2,1)S(1)}, bf16[512,128]{1,0:T(8,128)(2,1)S(1)}, u32[]{:S(2)}, u32[]{:S(2)}) collective-permute-start(bf16[512,128]{1,0:T(8,128)(2,1)S(1)} %collective-permute-done.38.refs_2_.refs_3_), channel_id=1, source_target_pairs={{0,4},{4,0},{8,12},{12,8},{16,20},{20,16},{24,28},{28,24},{1,5},{5... | collective-permute-start | bytes 393224 | tf_op jit(solution)/shard_map/ppermute | solution.py:215
  91.5 7.7 %collective-permute-start.8 = (bf16[512,128]{1,0:T(8,128)(2,1)S(1)}, bf16[512,128]{1,0:T(8,128)(2,1)S(1)}, u32[]{:S(2)}, u32[]{:S(2)}) collective-permute-start(bf16[512,128]{1,0:T(8,128)(2,1)S(1)} %bitcast.32), channel_id=1, source_target_pairs={{0,16},{4,20},{8,24},{12,28},{16,0},{20,4},{24,8},{28,12},{1,17},{... | collective-permute-start | bytes 393224 | tf_op jit(solution)/shard_map/ppermute | solution.py:215
  91.5 9.2 %collective-permute-start.31 = (bf16[512,128]{1,0:T(8,128)(2,1)S(1)}, bf16[512,128]{1,0:T(8,128)(2,1)S(1)}, u32[]{:S(2)}, u32[]{:S(2)}) collective-permute-start(bf16[512,128]{1,0:T(8,128)(2,1)S(1)} %collective-permute-done.29.refs_2_.refs_3_), channel_id=1, source_target_pairs={{0,4},{4,0},{8,12},{12,8},{16,20},{20,16},{24,28},{28,24},{1,5},{5... | collective-permute-start | bytes 393224 | tf_op jit(solution)/shard_map/ppermute | solution.py:215
  92.0 8.9 %collective-permute-start.21 = (bf16[512,128]{1,0:T(8,128)(2,1)S(1)}, bf16[512,128]{1,0:T(8,128)(2,1)S(1)}, u32[]{:S(2)}, u32[]{:S(2)}) collective-permute-start(bf16[512,128]{1,0:T(8,128)(2,1)S(1)} %bitcast.37), channel_id=1, source_target_pairs={{0,4},{4,0},{8,12},{12,8},{16,20},{20,16},{24,28},{28,24},{1,5},{5... | collective-permute-start | bytes 393224 | tf_op jit(solution)/shard_map/ppermute | solution.py:215
  97.1 6.4 %collective-permute-start.22 = (bf16[512,128]{1,0:T(8,128)(2,1)S(1)}, bf16[512,128]{1,0:T(8,128)(2,1)S(1)}, u32[]{:S(2)}, u32[]{:S(2)}) collective-permute-start(bf16[512,128]{1,0:T(8,128)(2,1)S(1)} %collective-permute-done.20.refs_2_.refs_3_), channel_id=1, source_target_pairs={{0,4},{4,0},{8,12},{12,8},{16,20},{20,16},{24,28},{28,24},{1,5},{5... | collective-permute-start | bytes 393224 | tf_op jit(solution)/shard_map/ppermute | solution.py:215
  97.6 7.9 %collective-permute-start.9 = (bf16[512,128]{1,0:T(8,128)(2,1)S(1)}, bf16[512,128]{1,0:T(8,128)(2,1)S(1)}, u32[]{:S(2)}, u32[]{:S(2)}) collective-permute-start(bf16[512,128]{1,0:T(8,128)(2,1)S(1)} %bitcast.33), channel_id=1, source_target_pairs={{0,4},{4,0},{8,12},{12,8},{16,20},{20,16},{24,28},{28,24},{1,5},{5... | collective-permute-start | bytes 393224 | tf_op jit(solution)/shard_map/ppermute | solution.py:215
  99.1 8.8 %collective-permute-start.10 = (bf16[512,128]{1,0:T(8,128)(2,1)S(1)}, bf16[512,128]{1,0:T(8,128)(2,1)S(1)}, u32[]{:S(2)}, u32[]{:S(2)}) collective-permute-start(bf16[512,128]{1,0:T(8,128)(2,1)S(1)} %collective-permute-done.8.refs_2_.refs_3_), channel_id=1, source_target_pairs={{0,4},{4,0},{8,12},{12,8},{16,20},{20,16},{24,28},{28,24},{1,5},{5... | collective-permute-start | bytes 393224 | tf_op jit(solution)/shard_map/ppermute | solution.py:215
  100.7 8.9 %collective-permute-start.49 = (bf16[1,512,128]{2,1,0:T(8,128)(2,1)S(1)}, bf16[1,512,128]{2,1,0:T(8,128)(2,1)S(1)}, u32[]{:S(2)}, u32[]{:S(2)}) collective-permute-start(bf16[1,512,128]{2,1,0:T(8,128)(2,1)S(1)} %mix.19), channel_id=1, source_target_pairs={{0,8},{4,12},{8,0},{12,4},{16,24},{20,28},{24,16},{28,20},{1,9},{5... | collective-permute-start | bytes 393224 | tf_op jit(solution)/shard_map/ppermute | solution.py:215
  100.9 9.5 %collective-permute-start.41 = (bf16[1,512,128]{2,1,0:T(8,128)(2,1)S(1)}, bf16[1,512,128]{2,1,0:T(8,128)(2,1)S(1)}, u32[]{:S(2)}, u32[]{:S(2)}) collective-permute-start(bf16[1,512,128]{2,1,0:T(8,128)(2,1)S(1)} %mix.17), channel_id=1, source_target_pairs={{0,8},{4,12},{8,0},{12,4},{16,24},{20,28},{24,16},{28,20},{1,9},{5... | collective-permute-start | bytes 393224 | tf_op jit(solution)/shard_map/ppermute | solution.py:215
  103.4 9.3 %collective-permute-start.32 = (bf16[1,512,128]{2,1,0:T(8,128)(2,1)S(1)}, bf16[1,512,128]{2,1,0:T(8,128)(2,1)S(1)}, u32[]{:S(2)}, u32[]{:S(2)}) collective-permute-start(bf16[1,512,128]{2,1,0:T(8,128)(2,1)S(1)} %mix.15), channel_id=1, source_target_pairs={{0,8},{4,12},{8,0},{12,4},{16,24},{20,28},{24,16},{28,20},{1,9},{5... | collective-permute-start | bytes 393224 | tf_op jit(solution)/shard_map/ppermute | solution.py:215
  105.5 9.4 %collective-permute-start.23 = (bf16[1,512,128]{2,1,0:T(8,128)(2,1)S(1)}, bf16[1,512,128]{2,1,0:T(8,128)(2,1)S(1)}, u32[]{:S(2)}, u32[]{:S(2)}) collective-permute-start(bf16[1,512,128]{2,1,0:T(8,128)(2,1)S(1)} %mix.13), channel_id=1, source_target_pairs={{0,8},{4,12},{8,0},{12,4},{16,24},{20,28},{24,16},{28,20},{1,9},{5... | collective-permute-start | bytes 393224 | tf_op jit(solution)/shard_map/ppermute | solution.py:215
  108.1 8.2 %collective-permute-start.11 = (bf16[1,512,128]{2,1,0:T(8,128)(2,1)S(1)}, bf16[1,512,128]{2,1,0:T(8,128)(2,1)S(1)}, u32[]{:S(2)}, u32[]{:S(2)}) collective-permute-start(bf16[1,512,128]{2,1,0:T(8,128)(2,1)S(1)} %mix.11), channel_id=1, source_target_pairs={{0,8},{4,12},{8,0},{12,4},{16,24},{20,28},{24,16},{28,20},{1,9},{5... | collective-permute-start | bytes 393224 | tf_op jit(solution)/shard_map/ppermute | solution.py:215

commit v4 on v3

v4 whole, which is shorter than its diff:
```python
import functools
import heapq

import jax
import jax.numpy as jnp
from jax import lax
from jax.experimental import pallas as pl
from jax.experimental.pallas import tpu as pltpu
from jax.sharding import PartitionSpec as P

F32 = jnp.float32
BF16 = jnp.bfloat16
SLAB = 64
MATMUL_ROWS = 256
VMEM_LIMIT = 16 * 1024 * 1024
LINK_SHARE = {"far": 0.041, "near": 0.0205, "partial": 0.0205, "core": 0.012, "row": 0.0205}
LATENCY = 1.5

smem = pl.BlockSpec(memory_space=pltpu.SMEM)
vmem = pl.BlockSpec(memory_space=pltpu.VMEM)
unread = pl.BlockSpec(memory_space=pl.ANY)


def chunk_bounds(columns):
    if columns % 128:
        return [(0, columns)]
    marks = list(range(0, columns, 256))
    return [(lo, min(256, columns - lo)) for lo in marks]


class Chain:
    def __init__(self):
        self.token = []

    def call(self, kernel, name, out_shape, arrays, scalars=(), scratch=(), out_specs=None, whole=(), after=(), aliases=None):
        count = len(scalars) + len(arrays) + len(whole)
        outs = count + len(after) + len(self.token)

        def body(*refs):
            kernel(*refs[:count], *refs[outs:outs + len(out_shape)], *refs[outs + len(out_shape) + 1:])

        *results, token = pl.pallas_call(
            body, name=name, out_shape=[*out_shape, jax.ShapeDtypeStruct((8, 128), F32)],
            in_specs=[smem] * len(scalars) + [vmem] * len(arrays) + [unread] * (outs - len(scalars) - len(arrays)),
            out_specs=[*(out_specs or [vmem] * len(out_shape)), unread],
            scratch_shapes=list(scratch),
            input_output_aliases=aliases or {},
            compiler_params=pltpu.CompilerParams(vmem_limit_bytes=VMEM_LIMIT),
            cost_estimate=pl.CostEstimate(flops=0, transcendentals=0, bytes_accessed=0),
        )(*scalars, *arrays, *whole, *after, *self.token)
        self.token = [token]
        return results

    def pin(self, *arrays):
        return self.call(
            lambda *refs: None, "pin", [like(a) for a in arrays], [], out_specs=[unread] * len(arrays), whole=arrays,
            aliases={i: i for i in range(len(arrays))})


def like(array):
    return jax.ShapeDtypeStruct(array.shape, array.dtype)


def slabs(rows, body, step=SLAB):
    step = step if rows % step == 0 else rows

    @pl.loop(0, rows // step)
    def _(i):
        body(pl.ds(pl.multiple_of(i * step, step), step))


def masked(total, at, left):
    row = lax.broadcasted_iota(jnp.int32, total.shape, 0) + at.start
    return jnp.where(row < left, total, 0.0).astype(BF16)


def stacked(count, rows, width):
    return jax.ShapeDtypeStruct((count, rows, width), BF16)


def mask_first(chain, block_rows, own, lo, width):
    rows = own.shape[0]

    def kernel(length_ref, own_ref, out_ref, left_ref):
        left = length_ref[0] - lax.axis_index("row") * rows
        left_ref[...] = jnp.full(left_ref.shape, left, jnp.int32)

        def body(at):
            out_ref[at, :] = masked(own_ref[at, lo:lo + width].astype(F32), at, left)

        slabs(rows, body)

    outs = [jax.ShapeDtypeStruct((rows, width), BF16), jax.ShapeDtypeStruct((8, width), jnp.int32)]
    return chain.call(kernel, "mask_first", outs, [own], [block_rows])


def mask_chunk(chain, left, own, lo, width, after):
    rows = own.shape[0]

    def kernel(left_ref, own_ref, out_ref):
        def body(at):
            out_ref[at, :] = masked(own_ref[at, lo:lo + width].astype(F32), at, left_ref[0:1, :width])

        slabs(rows, body)

    return chain.call(kernel, "mask_chunk", [jax.ShapeDtypeStruct((rows, width), BF16)], [left, own], after=after)[0]


def coefficients(chain, matrix, n_chan, entries, width):
    count = -(-len(entries) // 8) * 8

    def kernel(matrix_ref, table_ref):
        c = lax.axis_index("chan")
        for i, (t, m) in enumerate(entries):
            table_ref[i:i + 1, :] = jnp.full((1, width), matrix_ref[c ^ t, c ^ m], F32)

    return chain.call(kernel, "coefficients", [jax.ShapeDtypeStruct((count, width), F32)], [], [matrix])[0]


def mixed(table_ref, entries, held, at, target):
    total = None
    for source, ref in held:
        entry = entries.index((target, source))
        term = ref[at, :].astype(F32) * table_ref[entry:entry + 1, :ref.shape[1]]
        total = term if total is None else total + term
    return total


def mix(chain, table, entries, held, targets, received):
    rows, width = held[0][1].shape

    def kernel(table_ref, *refs):
        held_refs = [(m, ref) for (m, _), ref in zip(held, refs)]
        received_refs = refs[len(held):-1]
        out_ref = refs[-1]

        def body(at):
            for i, t in enumerate(targets):
                total = mixed(table_ref, entries, held_refs, at, t)
                for (_, names), ref in zip(received, received_refs):
                    if t in names:
                        total = total + ref[names.index(t), at, :].astype(F32)
                out_ref[i, at, :] = total.astype(BF16)

        slabs(rows, body)

    arrays = [table] + [b for _, b in held] + [r for r, _ in received]
    return chain.call(kernel, "mix", [stacked(len(targets), rows, width)], arrays)[0]


def mix_multiply(chain, table, entries, held, received, weights, n_row):
    rows, width = held[0][1].shape
    group = weights.shape[0] // n_row

    def kernel(table_ref, *refs):
        held_refs = [(m, ref) for (m, _), ref in zip(held, refs)]
        received_refs = refs[len(held):len(held) + len(received)]
        weights_ref, *out_refs, cross_ref = refs[len(held) + len(received):]
        g = lax.axis_index("row")

        def body(at):
            total = mixed(table_ref, entries, held_refs, at, 0)
            for ref in received_refs:
                total = total + ref[0, at, :].astype(F32)
            cross_ref[at, :] = total.astype(BF16)

        slabs(rows, body)
        for d, out_ref in enumerate(out_refs):
            base = (g ^ d) * group

            def rows_of(at):
                from_row = pl.ds(pl.multiple_of(base + at.start, at.size), at.size)
                out_ref[at, :] = jnp.dot(weights_ref[from_row, :], cross_ref[...], preferred_element_type=F32).astype(BF16)

            slabs(group, rows_of, MATMUL_ROWS)

    arrays = [table] + [b for _, b in held] + received + [weights]
    outs = [jax.ShapeDtypeStruct((group, width), BF16)] * n_row
    return chain.call(kernel, "mix_multiply", outs, arrays, scratch=[pltpu.VMEM((rows, width), BF16)])


def add_up(chain, blocks):
    def kernel(*refs):
        def body(at):
            terms = [ref[at, :].astype(F32) for ref in refs[:-1]]
            refs[-1][at, :] = functools.reduce(lambda a, b: a + b, terms).astype(BF16)

        slabs(blocks[0].shape[0], body)

    return chain.call(kernel, "add_up", [like(blocks[0])], blocks)[0]


def finish(chain, table, entries, left, held, received, lo, columns, result):
    rows, width = held[0][1].shape

    def kernel(table_ref, left_ref, *refs):
        held_refs = [(m, ref) for (m, _), ref in zip(held, refs)]
        received_refs = refs[len(held):len(held) + len(received)]
        out_ref, chunk_ref, done = refs[-3:]

        def body(at):
            total = mixed(table_ref, entries, held_refs, at, 0)
            for ref in received_refs:
                total = total + ref[0, at, :].astype(F32)
            chunk_ref[at, :] = masked(total, at, left_ref[0:1, :width])

        slabs(rows, body)
        copy = pltpu.make_async_copy(chunk_ref, out_ref.at[:, lo:lo + width], done)
        copy.start()
        copy.wait()

    arrays = [table, left] + [b for _, b in held] + received
    whole = [] if result is None else [result]
    return chain.call(
        kernel, "finish", [jax.ShapeDtypeStruct((rows, columns), BF16)], arrays,
        scratch=[pltpu.VMEM((rows, width), BF16), pltpu.SemaphoreType.DMA(())], out_specs=[unread],
        whole=whole, aliases={len(arrays): 0} if whole else {})[0]


def solution(mesh):
    n_chan, n_row = mesh.shape["chan"], mesh.shape["row"]
    chan_bits = [1 << b for b in range(n_chan.bit_length() - 1)]
    row_bits = [1 << b for b in range(n_row.bit_length() - 1)]
    far, near = chan_bits[-1], chan_bits[0]
    reduce_bits = [b for b in reversed(chan_bits) if b not in (far, near)]

    def swap(x, axis, size, bit):
        return lax.ppermute(x, axis, [(i, i ^ bit) for i in range(size)])

    def span(bits):
        targets = [0]
        for bit in bits:
            targets = targets + [t ^ bit for t in targets]
        return targets

    def split(targets, bit):
        return [t for t in targets if t & bit], [t for t in targets if not t & bit]

    def on_device(amplitudes, block_rows, recoupling, interaction):
        rows, _, columns = amplitudes.shape
        own = amplitudes.reshape(rows, columns)
        weights = interaction.reshape(interaction.shape[0], interaction.shape[2])
        bounds = chunk_bounds(columns)
        lanes = max(width for _, width in bounds)
        entries = [(t, m) for t in span(reduce_bits) for m in (0, far, near, far ^ near)]
        matrix = recoupling.astype(F32)
        chain = Chain()
        tables, result, left, last_far = {}, None, None, None

        def table(transposed):
            if transposed not in tables:
                tables[transposed] = coefficients(chain, matrix.T if transposed else matrix, n_chan, entries, lanes)
            return tables[transposed]

        def mixing(block, transposed, note_far=None):
            other = swap(block, "chan", n_chan, far)
            beside = swap(block, "chan", n_chan, near)
            if note_far:
                note_far(other)
            yield "far"
            other, beside = chain.pin(other, beside)
            corner = swap(other, "chan", n_chan, near)
            held = [(0, block), (far, other), (near, beside), (far ^ near, corner)]
            targets, received = span(reduce_bits), []
            yield "near"
            for bit in reduce_bits:
                sent, targets = split(targets, bit)
                part = mix(chain, table(transposed), entries, held, sent, received)
                received.append((swap(part, "chan", n_chan, bit), [t ^ bit for t in sent]))
                yield "partial"
            return held, [r for r, _ in received]

        def one_chunk(lo, width):
            nonlocal result, left, last_far

            def note_far(array):
                nonlocal last_far
                last_far = array

            if left is None:
                block, left = mask_first(chain, block_rows, own, lo, width)
            else:
                block = mask_chunk(chain, left, own, lo, width, [last_far])
            held, received = yield from mixing(block, False, note_far)
            parts = mix_multiply(chain, table(False), entries, held, received, weights, n_row)
            terms, targets = {d: [part] for d, part in enumerate(parts)}, list(range(n_row))
            for bit in row_bits:
                sent, targets = split(targets, bit)
                for t in sent:
                    block = terms[t][0] if len(terms[t]) == 1 else add_up(chain, terms[t])
                    terms[t ^ bit].append(swap(block, "row", n_row, bit))
                yield "core" if bit == row_bits[0] else "row"
            block = add_up(chain, terms[0])
            held, received = yield from mixing(block, True)
            result = finish(chain, table(True), entries, left, held, received, lo, columns, result)

        free = dict.fromkeys(LINK_SHARE, 0.0)
        queue, start = [], 0.0
        for i, (lo, width) in enumerate(bounds):
            queue.append((start, i, one_chunk(lo, width)))
            start += LINK_SHARE["far"] * width
        while queue:
            time, i, work = heapq.heappop(queue)
            kind = next(work, None)
            if kind is not None:
                free[kind] = max(time, free[kind]) + LINK_SHARE[kind] * bounds[i][1]
                heapq.heappush(queue, (free[kind] + LATENCY, i, work))
        return result.reshape(amplitudes.shape)

    return jax.shard_map(
        on_device,
        mesh=mesh,
        in_specs=(P("row", "chan", None), P("chan"), P(), P(None, "chan", "row")),
        out_specs=P("row", "chan", None),
        check_vma=False,
    )
```

time: 117 us -> 119 us (1.017)
  starting transfers between devices: 56.2 us -> 23.6 us
  waiting for transfers between devices: 41 us -> 72.3 us
  local copies, waits for them, and re-layouts: 1.16 us -> 5.11 us
    ppermute x50 -> x33, starting transfers between devices: 56.2 us -> 23.6 us  [swap(): return lax.ppermute(x, axis, [(i, i ^ bit) for i in range(size)])]
    ppermute x50 -> x33, waiting for transfers between devices: 41 us -> 72.3 us  [swap(): return lax.ppermute(x, axis, [(i, i ^ bit) for i in range(size)])]
    unnamed x6 -> x21, local copies, waits for them, and re-layouts: 1.09 us -> 4.36 us
    pallas_call x37 -> x29, Pallas kernels: 17.6 us -> 16.9 us  [call(): pl.pallas_call(body, name=name, out_shape=[*out_shape, jax.ShapeDtypeStru...]
  transfers between devices with their start and end apart: 50 -> 33, of which waited for: 18 -> 20; matrix products, arithmetic and copies ran while one was open for 0% -> 1% of each run, Pallas kernels for 14% -> 13%
where the time goes in v4:
time: 119 us
  waiting for transfers between devices  72.3 us (61%)
  starting transfers between devices  23.6 us (20%)
  Pallas kernels  16.9 us (14%)
  local copies, waits for them, and re-layouts  5.11 us (4%)
    ppermute x33, waiting for transfers between devices, swap(): return lax.ppermute(x, axis, [(i, i ^ bit) for i in range(size)])  72.3 us
    ppermute x33, starting transfers between devices, swap(): return lax.ppermute(x, axis, [(i, i ^ bit) for i in range(size)])  23.6 us
    pallas_call x29, Pallas kernels, call(): pl.pallas_call(body, name=name, out_shape=[*out_shape, jax.ShapeDtypeStru...  16.9 us
    unnamed x21, local copies, waits for them, and re-layouts  4.36 us
  transfers between devices with their start and end apart: 33, of which 20 were waited for; matrix products, arithmetic and copies ran while one was open for 1% of the time, Pallas kernels for 13%

profile of v4, /device:TPU:0, one launch (start us, length us, event | category | flops | bytes accessed | tf_op | source)
XLA Modules:
  0.0 118.9 jit_solution(14887546941417003995)
XLA Ops:
  0.7 1.1 copy-done.1
  1.9 4.1 %collective-permute-start = (bf16[512,256]{1,0:T(8,128)(2,1)S(1)}, bf16[512,256]{1,0:T(8,128)(2,1)S(1)}, u32[]{:S(2)}, u32[]{:S(2)}) collective-permute-start(bf16[512,256]{1,0:T(8,128)(2,1)S(1)} %get-tuple-element.78.refs_1_), channel_id=1, source_target_pairs={{0,16},{4,20},{8,24},{12,28},{16,0},{20,4},{24,8},{28,12},{1,17},{... | collective-permute-start | bytes 786440 | tf_op jit(solution)/shard_map/ppermute | solution.py:228
  6.0 1.5 %collective-permute-start.1 = (bf16[512,256]{1,0:T(8,128)(2,1)S(1)}, bf16[512,256]{1,0:T(8,128)(2,1)S(1)}, u32[]{:S(2)}, u32[]{:S(2)}) collective-permute-start(bf16[512,256]{1,0:T(8,128)(2,1)S(1)} %get-tuple-element.78.refs_1_), channel_id=1, source_target_pairs={{0,4},{4,0},{8,12},{12,8},{16,20},{20,16},{24,28},{28,24},{1,5},{5... | collective-permute-start | bytes 786440 | tf_op jit(solution)/shard_map/ppermute | solution.py:228
  7.5 10.4 %collective-permute-done.refs_2_.refs_0_ = bf16[512,256]{1,0:T(8,128)(2,1)S(1)} collective-permute-done((bf16[512,256]{1,0:T(8,128)(2,1)S(1)}, bf16[512,256]{1,0:T(8,128)(2,1)S(1)}, u32[]{:S(2)}, u32[]{:S(2)}) %collective-permute-start) | collective-permute-done | bytes 262176 | tf_op jit(solution)/shard_map/ppermute | solution.py:228
  17.9 0.8 mask_chunk.2
  18.7 0.7 copy-done.3
  19.4 1.5 %collective-permute-start.3 = (bf16[512,256]{1,0:T(8,128)(2,1)S(1)}, bf16[512,256]{1,0:T(8,128)(2,1)}, u32[]{:S(2)}, u32[]{:S(2)}) collective-permute-start(bf16[512,256]{1,0:T(8,128)(2,1)S(1)} %get-tuple-element.85.refs_2_), channel_id=1, source_target_pairs={{0,4},{4,0},{8,12},{12,8},{16,20},{20,16},{24,28},{28,24},{1,5},{5... | collective-permute-start | bytes 786440 | tf_op jit(solution)/shard_map/ppermute | solution.py:228
  21.0 0.5 collective-permute-start.7
  21.5 0.7 copy.19
  22.1 0.7 copy.20.refs_0_
  22.9 0.6 coefficients.2
  23.5 5.3 %collective-permute-done.3.refs_4_ = bf16[512,256]{1,0:T(8,128)(2,1)} collective-permute-done((bf16[512,256]{1,0:T(8,128)(2,1)S(1)}, bf16[512,256]{1,0:T(8,128)(2,1)}, u32[]{:S(2)}, u32[]{:S(2)}) %collective-permute-start.3) | collective-permute-done | bytes 262176 | tf_op jit(solution)/shard_map/ppermute | solution.py:228
  28.8 0.9 copy-done.4
  29.7 0.9 copy-done.7
  30.7 1.2 %mix.6 = (bf16[1,512,256]{2,1,0:T(8,128)(2,1)S(1)}, f32[8,128]{1,0:T(8,128)S(1)}) custom-call(f32[8,256]{1,0:T(8,128)S(1)} %get-tuple-element.83.refs_0_, bf16[512,256]{1,0:T(8,128)(2,1)S(1)} %copy-done.7, bf16[512,256]{1,0:T(8,128)(2,1)S(1)} %get-tuple-element.85.refs_2_, bf16[512,256]{1,0:T(8,128)(2,1)S(1)} %copy-done.4, ...), custom_call_target="tpu_custom_call" | custom-call | tf_op jit(solution)/shard_map/mix/pallas_call | solution.py:42
  31.9 0.7 collective-permute-start.6
  32.6 2.1 %collective-permute-done.2.refs_2_.refs_0_ = bf16[512,256]{1,0:T(8,128)(2,1)S(1)} collective-permute-done((bf16[512,256]{1,0:T(8,128)(2,1)}, bf16[512,256]{1,0:T(8,128)(2,1)S(1)}, u32[]{:S(2)}, u32[]{:S(2)}) %collective-permute-start.2) | collective-permute-done | bytes 262176 | tf_op jit(solution)/shard_map/ppermute | solution.py:228
  34.8 0.8 collective-permute-start.10
  35.7 2.0 %collective-permute-start.4 = (bf16[512,128]{1,0:T(8,128)(2,1)S(1)}, bf16[512,128]{1,0:T(8,128)(2,1)S(1)}, u32[]{:S(2)}, u32[]{:S(2)}) collective-permute-start(bf16[512,128]{1,0:T(8,128)(2,1)S(1)} %get-tuple-element.89.refs_1_), channel_id=1, source_target_pairs={{0,16},{4,20},{8,24},{12,28},{16,0},{20,4},{24,8},{28,12},{1,17},{... | collective-permute-start | bytes 393224 | tf_op jit(solution)/shard_map/ppermute | solution.py:228
  37.7 0.5 collective-permute-start.5
  38.2 4.6 %collective-permute-done.6.refs_5_ = bf16[1,512,256]{2,1,0:T(8,128)(2,1)S(1)} collective-permute-done((bf16[1,512,256]{2,1,0:T(8,128)(2,1)S(1)}, bf16[1,512,256]{2,1,0:T(8,128)(2,1)S(1)}, u32[]{:S(2)}, u32[]{:S(2)}) %collective-permute-start.6) | collective-permute-done | bytes 262176 | tf_op jit(solution)/shard_map/ppermute | solution.py:228
  42.8 3.1 %mix_multiply.3 = (bf16[512,256]{1,0:T(8,128)(2,1)S(1)}, bf16[512,256]{1,0:T(8,128)(2,1)S(1)}, bf16[512,256]{1,0:T(8,128)(2,1)S(1)}, bf16[512,256]{1,0:T(8,128)(2,1)S(1)}, f32[8,128]{1,0:T(8,128)S(1)}) custom-call(f32[8,256]{1,0:T(8,128)S(1)} %get-tuple-element.83.refs_0_, bf16[512,256]{1,0:T(8,128)(2,1)S(1)} %copy-done.7, ...), custom_call_target="tpu_custom_call" | custom-call | tf_op jit(solution)/shard_map/mix_multiply/pallas_call | solution.py:42
  46.0 1.2 %mix.7 = (bf16[1,512,256]{2,1,0:T(8,128)(2,1)S(1)}, f32[8,128]{1,0:T(8,128)S(1)}) custom-call(f32[8,256]{1,0:T(8,128)S(1)} %get-tuple-element.83.refs_0_, bf16[512,256]{1,0:T(8,128)(2,1)} %get-tuple-element.84.refs_1_, bf16[512,256]{1,0:T(8,128)(2,1)S(1)} %get-tuple-element.98.refs_2_, bf16[512,256]{1,0:T(8,128)(2,1)S(1)} %get-tuple-element.99.refs_3_, ...), custom_call_target="tpu_custom_call" | custom-call | tf_op jit(solution)/shard_map/mix/pallas_call | solution.py:42
  47.3 1.1 collective-permute-start.8
  48.4 0.2 collective-permute-start.12
  48.6 1.3 %collective-permute-start.13 = (bf16[512,256]{1,0:T(8,128)(2,1)S(1)}, bf16[512,256]{1,0:T(8,128)(2,1)S(1)}, u32[]{:S(2)}, u32[]{:S(2)}) collective-permute-start(bf16[512,256]{1,0:T(8,128)(2,1)S(1)} %get-tuple-element.106), channel_id=1, source_target_pairs={{0,2},{1,3},{2,0},{3,1},{4,6},{5,7},{6,4},{7,5},{8,10},{9,11},{10,... | collective-permute-start | bytes 786440 | tf_op jit(solution)/shard_map/ppermute | solution.py:228
  50.0 3.2 %collective-permute-done.8.refs_4_ = bf16[512,128]{1,0:T(8,128)(2,1)S(1)} collective-permute-done((bf16[512,128]{1,0:T(8,128)(2,1)S(1)}, bf16[512,128]{1,0:T(8,128)(2,1)S(1)}, u32[]{:S(2)}, u32[]{:S(2)}) %collective-permute-start.8) | collective-permute-done | bytes 131104 | tf_op jit(solution)/shard_map/ppermute | solution.py:228
  53.2 0.1 mix.8
  53.4 2.6 %collective-permute-done.14.refs_5_ = bf16[1,512,256]{2,1,0:T(8,128)(2,1)S(1)} collective-permute-done((bf16[1,512,256]{2,1,0:T(8,128)(2,1)S(1)}, bf16[1,512,256]{2,1,0:T(8,128)(2,1)S(1)}, u32[]{:S(2)}, u32[]{:S(2)}) %collective-permute-start.14) | collective-permute-done | bytes 262176 | tf_op jit(solution)/shard_map/ppermute | solution.py:228
  55.9 3.1 %mix_multiply.4 = (bf16[512,256]{1,0:T(8,128)(2,1)S(1)}, bf16[512,256]{1,0:T(8,128)(2,1)S(1)}, bf16[512,256]{1,0:T(8,128)(2,1)S(1)}, bf16[512,256]{1,0:T(8,128)(2,1)S(1)}, f32[8,128]{1,0:T(8,128)S(1)}) custom-call(f32[8,256]{1,0:T(8,128)S(1)} %get-tuple-element.83.refs_0_, bf16[512,256]{1,0:T(8,128)(2,1)} %get-tuple-element.84.refs_1_, ...), custom_call_target="tpu_custom_call" | custom-call | tf_op jit(solution)/shard_map/mix_multiply/pallas_call | solution.py:42
  59.1 0.3 collective-permute-start.11
  59.4 0.2 collective-permute-start.21
  59.6 0.1 add_up.7
  59.7 5.3 %collective-permute-done.11.refs_5_ = bf16[1,512,128]{2,1,0:T(8,128)(2,1)S(1)} collective-permute-done((bf16[1,512,128]{2,1,0:T(8,128)(2,1)S(1)}, bf16[1,512,128]{2,1,0:T(8,128)(2,1)S(1)}, u32[]{:S(2)}, u32[]{:S(2)}) %collective-permute-start.11) | collective-permute-done | bytes 131104 | tf_op jit(solution)/shard_map/ppermute | solution.py:228
  65.0 1.8 %mix_multiply.5 = (bf16[512,128]{1,0:T(8,128)(2,1)S(1)}, bf16[512,128]{1,0:T(8,128)(2,1)S(1)}, bf16[512,128]{1,0:T(8,128)(2,1)S(1)}, bf16[512,128]{1,0:T(8,128)(2,1)S(1)}, f32[8,128]{1,0:T(8,128)S(1)}) custom-call(f32[8,256]{1,0:T(8,128)S(1)} %get-tuple-element.83.refs_0_, bf16[512,128]{1,0:T(8,128)(2,1)S(1)} %get-tuple-element.89.refs_1_, ...), custom_call_target="tpu_custom_call" | custom-call | tf_op jit(solution)/shard_map/mix_multiply/pallas_call | solution.py:42
  67.0 1.7 %collective-permute-start.22 = (bf16[512,256]{1,0:T(8,128)(2,1)S(1)}, bf16[512,256]{1,0:T(8,128)(2,1)S(1)}, u32[]{:S(2)}, u32[]{:S(2)}) collective-permute-start(bf16[512,256]{1,0:T(8,128)(2,1)S(1)} %get-tuple-element.123), channel_id=1, source_target_pairs={{0,2},{1,3},{2,0},{3,1},{4,6},{5,7},{6,4},{7,5},{8,10},{9,11},{10,... | collective-permute-start | bytes 786440 | tf_op jit(solution)/shard_map/ppermute | solution.py:228
  68.7 1.1 collective-permute-start.20
  69.7 1.3 %collective-permute-done.16.refs_1_ = bf16[512,128]{1,0:T(8,128)(2,1)S(1)} collective-permute-done((bf16[512,128]{1,0:T(8,128)(2,1)S(1)}, bf16[512,128]{1,0:T(8,128)(2,1)S(1)}, u32[]{:S(2)}, u32[]{:S(2)}) %collective-permute-start.16) | collective-permute-done | bytes 131104 | tf_op jit(solution)/shard_map/ppermute | solution.py:228
  71.1 3.7 %collective-permute-done.22.refs_2_ = bf16[512,256]{1,0:T(8,128)(2,1)S(1)} collective-permute-done((bf16[512,256]{1,0:T(8,128)(2,1)S(1)}, bf16[512,256]{1,0:T(8,128)(2,1)S(1)}, u32[]{:S(2)}, u32[]{:S(2)}) %collective-permute-start.22) | collective-permute-done | bytes 262176 | tf_op jit(solution)/shard_map/ppermute | solution.py:228
  75.0 7.5 %collective-permute-done.19.refs_0_ = bf16[512,256]{1,0:T(8,128)(2,1)S(1)} collective-permute-done((bf16[512,256]{1,0:T(8,128)(2,1)S(1)}, bf16[512,256]{1,0:T(8,128)(2,1)S(1)}, u32[]{:S(2)}, u32[]{:S(2)}) %collective-permute-start.19) | collective-permute-done | bytes 262176 | tf_op jit(solution)/shard_map/ppermute | solution.py:228
  82.5 0.7 collective-permute-start.25
  83.2 1.4 %collective-permute-start.28 = (bf16[512,256]{1,0:T(8,128)(2,1)S(1)}, bf16[512,256]{1,0:T(8,128)(2,1)S(1)}, u32[]{:S(2)}, u32[]{:S(2)}) collective-permute-start(bf16[512,256]{1,0:T(8,128)(2,1)S(1)} %get-tuple-element.134.refs_1_.refs_2_), channel_id=1, source_target_pairs={{0,4},{4,0},{8,12},{12,8},{16,20},{20,16},{24,28},{28,24},{1,5},{5... | collective-permute-start | bytes 786440 | tf_op jit(solution)/shard_map/ppermute | solution.py:228
  84.5 0.4 collective-permute-start.18
  84.9 0.9 collective-permute-done.15.refs_1_
  85.9 4.6 %collective-permute-done.18.refs_2_ = bf16[512,128]{1,0:T(8,128)(2,1)S(1)} collective-permute-done((bf16[512,128]{1,0:T(8,128)(2,1)S(1)}, bf16[512,128]{1,0:T(8,128)(2,1)S(1)}, u32[]{:S(2)}, u32[]{:S(2)}) %collective-permute-start.18) | collective-permute-done | bytes 131104 | tf_op jit(solution)/shard_map/ppermute | solution.py:228
  90.5 0.6 coefficients.3
  91.2 0.5 collective-permute-done.25.refs_4_.refs_5_
  91.7 0.2 mix.9
  91.9 0.9 collective-permute-start.26
  92.8 3.8 %collective-permute-done.27.refs_0_ = bf16[512,256]{1,0:T(8,128)(2,1)S(1)} collective-permute-done((bf16[512,256]{1,0:T(8,128)(2,1)S(1)}, bf16[512,256]{1,0:T(8,128)(2,1)S(1)}, u32[]{:S(2)}, u32[]{:S(2)}) %collective-permute-start.27) | collective-permute-done | bytes 262176 | tf_op jit(solution)/shard_map/ppermute | solution.py:228
  96.6 0.4 collective-permute-start.30
  97.0 1.6 %collective-permute-start.24 = (bf16[512,128]{1,0:T(8,128)(2,1)S(1)}, bf16[512,128]{1,0:T(8,128)(2,1)S(1)}, u32[]{:S(2)}, u32[]{:S(2)}) collective-permute-start(bf16[512,128]{1,0:T(8,128)(2,1)S(1)} %get-tuple-element.129.refs_1_.refs_2_), channel_id=1, source_target_pairs={{0,4},{4,0},{8,12},{12,8},{16,20},{20,16},{24,28},{28,24},{1,5},{5... | collective-permute-start | bytes 393224 | tf_op jit(solution)/shard_map/ppermute | solution.py:228
  98.7 5.2 %collective-permute-done.26.refs_6_ = bf16[1,512,256]{2,1,0:T(8,128)(2,1)S(1)} collective-permute-done((bf16[1,512,256]{2,1,0:T(8,128)(2,1)S(1)}, bf16[1,512,256]{2,1,0:T(8,128)(2,1)S(1)}, u32[]{:S(2)}, u32[]{:S(2)}) %collective-permute-start.26) | collective-permute-done | bytes 262176 | tf_op jit(solution)/shard_map/ppermute | solution.py:228
  103.9 1.0 finish.3
  104.9 0.8 collective-permute-done.23.refs_0_
  105.8 1.8 %collective-permute-done.24.refs_1_ = bf16[512,128]{1,0:T(8,128)(2,1)S(1)} collective-permute-done((bf16[512,128]{1,0:T(8,128)(2,1)S(1)}, bf16[512,128]{1,0:T(8,128)(2,1)S(1)}, u32[]{:S(2)}, u32[]{:S(2)}) %collective-permute-start.24) | collective-permute-done | bytes 131104 | tf_op jit(solution)/shard_map/ppermute | solution.py:228
  107.6 0.3 collective-permute-start.29
  107.9 0.2 mix.10
  108.3 4.3 %collective-permute-done.29.refs_4_.refs_5_ = bf16[512,128]{1,0:T(8,128)(2,1)S(1)} collective-permute-done((bf16[512,128]{1,0:T(8,128)(2,1)S(1)}, bf16[512,128]{1,0:T(8,128)(2,1)S(1)}, u32[]{:S(2)}, u32[]{:S(2)}) %collective-permute-start.29) | collective-permute-done | bytes 131104 | tf_op jit(solution)/shard_map/ppermute | solution.py:228
  112.6 0.1 mix.11
  112.8 3.9 %collective-permute-done.32.refs_6_ = bf16[1,512,256]{2,1,0:T(8,128)(2,1)S(1)} collective-permute-done((bf16[1,512,256]{2,1,0:T(8,128)(2,1)S(1)}, bf16[1,512,256]{2,1,0:T(8,128)(2,1)S(1)}, u32[]{:S(2)}, u32[]{:S(2)}) %collective-permute-start.32) | collective-permute-done | bytes 262176 | tf_op jit(solution)/shard_map/ppermute | solution.py:228
  116.7 1.0 finish.4
  117.7 0.4 collective-permute-done.31.refs_6_
  118.1 0.9 finish.5
  (54 shorter events, 1.1 us)
Async XLA Ops:
  0.0 21.5 %copy-start.9 = (bf16[8,8]{1,0:T(8,128)(2,1)S(1)}, bf16[8,8]{1,0:T(8,128)(2,1)}, u32[]{:S(2)}) copy-start(bf16[8,8]{1,0:T(8,128)(2,1)} %param.6) | copy-start | bytes 388
  0.7 1.1 copy-start.1
  1.8 33.0 %copy-start.2 = (bf16[512,1,640]{2,0,1:T(8,128)(2,1)S(1)}, bf16[512,1,640]{2,0,1:T(8,128)(2,1)}, u32[]{:S(2)}) copy-start(bf16[512,1,640]{2,0,1:T(8,128)(2,1)} %param.4) | copy-start | bytes 1966084
  1.9 19.1 %copy-start.6 = (bf16[512,256]{1,0:T(8,128)(2,1)}, bf16[512,256]{1,0:T(8,128)(2,1)S(1)}, u32[]{:S(2)}) copy-start(bf16[512,256]{1,0:T(8,128)(2,1)S(1)} %get-tuple-element.78.refs_1_) | copy-start | bytes 786436
  1.9 40.9 %copy-start = (bf16[2048,1,512]{2,0,1:T(8,128)(2,1)S(1)}, bf16[2048,1,512]{2,0,1:T(8,128)(2,1)}, u32[]{:S(2)}) copy-start(bf16[2048,1,512]{2,0,1:T(8,128)(2,1)} %param.7) | copy-start | bytes 6291460
  1.9 16.0 %collective-permute-start = (bf16[512,256]{1,0:T(8,128)(2,1)S(1)}, bf16[512,256]{1,0:T(8,128)(2,1)S(1)}, u32[]{:S(2)}, u32[]{:S(2)}) collective-permute-start(bf16[512,256]{1,0:T(8,128)(2,1)S(1)} %get-tuple-element.78.refs_1_), channel_id=1, source_target_pairs={{0,16},{4,20},{8,24},{12,28},{16,0},{20,4},{24,8},{28,12},{1,17},{... | collective-permute-start | bytes 786440 | tf_op jit(solution)/shard_map/ppermute | solution.py:228
  6.0 12.7 %collective-permute-start.1 = (bf16[512,256]{1,0:T(8,128)(2,1)S(1)}, bf16[512,256]{1,0:T(8,128)(2,1)S(1)}, u32[]{:S(2)}, u32[]{:S(2)}) collective-permute-start(bf16[512,256]{1,0:T(8,128)(2,1)S(1)} %get-tuple-element.78.refs_1_), channel_id=1, source_target_pairs={{0,4},{4,0},{8,12},{12,8},{16,20},{20,16},{24,28},{28,24},{1,5},{5... | collective-permute-start | bytes 786440 | tf_op jit(solution)/shard_map/ppermute | solution.py:228
  18.7 0.7 copy-start.3
  19.4 9.3 %collective-permute-start.3 = (bf16[512,256]{1,0:T(8,128)(2,1)S(1)}, bf16[512,256]{1,0:T(8,128)(2,1)}, u32[]{:S(2)}, u32[]{:S(2)}) collective-permute-start(bf16[512,256]{1,0:T(8,128)(2,1)S(1)} %get-tuple-element.85.refs_2_), channel_id=1, source_target_pairs={{0,4},{4,0},{8,12},{12,8},{16,20},{20,16},{24,28},{28,24},{1,5},{5... | collective-permute-start | bytes 786440 | tf_op jit(solution)/shard_map/ppermute | solution.py:228
  21.0 13.7 %collective-permute-start.2 = (bf16[512,256]{1,0:T(8,128)(2,1)}, bf16[512,256]{1,0:T(8,128)(2,1)S(1)}, u32[]{:S(2)}, u32[]{:S(2)}) collective-permute-start(bf16[512,256]{1,0:T(8,128)(2,1)} %get-tuple-element.84.refs_1_), channel_id=1, source_target_pairs={{0,16},{4,20},{8,24},{12,28},{16,0},{20,4},{24,8},{28,12},{1,17},{... | collective-permute-start | bytes 786440 | tf_op jit(solution)/shard_map/ppermute | solution.py:228
  21.0 13.8 %collective-permute-start.7 = (bf16[512,256]{1,0:T(8,128)(2,1)}, bf16[512,256]{1,0:T(8,128)(2,1)S(1)}, u32[]{:S(2)}, u32[]{:S(2)}) collective-permute-start(bf16[512,256]{1,0:T(8,128)(2,1)} %get-tuple-element.84.refs_1_), channel_id=1, source_target_pairs={{0,4},{4,0},{8,12},{12,8},{16,20},{20,16},{24,28},{28,24},{1,5},{5... | collective-permute-start | bytes 786440 | tf_op jit(solution)/shard_map/ppermute | solution.py:228
  28.8 1.0 copy-start.4
  29.7 0.9 copy-start.7
  30.7 12.1 %copy-start.5 = (bf16[512,256]{1,0:T(8,128)(2,1)S(1)}, bf16[512,256]{1,0:T(8,128)(2,1)}, u32[]{:S(2)}) copy-start(bf16[512,256]{1,0:T(8,128)(2,1)} %copy-done.3) | copy-start | bytes 786436
  31.9 10.9 %collective-permute-start.6 = (bf16[1,512,256]{2,1,0:T(8,128)(2,1)S(1)}, bf16[1,512,256]{2,1,0:T(8,128)(2,1)S(1)}, u32[]{:S(2)}, u32[]{:S(2)}) collective-permute-start(bf16[1,512,256]{2,1,0:T(8,128)(2,1)S(1)} %get-tuple-element.90), channel_id=1, source_target_pairs={{0,8},{4,12},{8,0},{12,4},{16,24},{20,28},{24,16},{28,20},{1,9},{5... | collective-permute-start | bytes 786440 | tf_op jit(solution)/shard_map/ppermute | solution.py:228
  34.8 11.2 %collective-permute-start.10 = (bf16[512,256]{1,0:T(8,128)(2,1)S(1)}, bf16[512,256]{1,0:T(8,128)(2,1)S(1)}, u32[]{:S(2)}, u32[]{:S(2)}) collective-permute-start(bf16[512,256]{1,0:T(8,128)(2,1)S(1)} %get-tuple-element.98.refs_2_), channel_id=1, source_target_pairs={{0,4},{4,0},{8,12},{12,8},{16,20},{20,16},{24,28},{28,24},{1,5},{5... | collective-permute-start | bytes 786440 | tf_op jit(solution)/shard_map/ppermute | solution.py:228
  35.7 10.3 %collective-permute-start.4 = (bf16[512,128]{1,0:T(8,128)(2,1)S(1)}, bf16[512,128]{1,0:T(8,128)(2,1)S(1)}, u32[]{:S(2)}, u32[]{:S(2)}) collective-permute-start(bf16[512,128]{1,0:T(8,128)(2,1)S(1)} %get-tuple-element.89.refs_1_), channel_id=1, source_target_pairs={{0,16},{4,20},{8,24},{12,28},{16,0},{20,4},{24,8},{28,12},{1,17},{... | collective-permute-start | bytes 393224 | tf_op jit(solution)/shard_map/ppermute | solution.py:228
  37.7 8.3 %collective-permute-start.5 = (bf16[512,128]{1,0:T(8,128)(2,1)S(1)}, bf16[512,128]{1,0:T(8,128)(2,1)S(1)}, u32[]{:S(2)}, u32[]{:S(2)}) collective-permute-start(bf16[512,128]{1,0:T(8,128)(2,1)S(1)} %get-tuple-element.89.refs_1_), channel_id=1, source_target_pairs={{0,4},{4,0},{8,12},{12,8},{16,20},{20,16},{24,28},{28,24},{1,5},{5... | collective-permute-start | bytes 393224 | tf_op jit(solution)/shard_map/ppermute | solution.py:228
  45.9 2.7 %collective-permute-start.9 = (bf16[512,256]{1,0:T(8,128)(2,1)S(1)}, bf16[512,256]{1,0:T(8,128)(2,1)S(1)}, u32[]{:S(2)}, u32[]{:S(2)}) collective-permute-start(bf16[512,256]{1,0:T(8,128)(2,1)S(1)} %get-tuple-element.97), channel_id=1, source_target_pairs={{0,1},{1,0},{2,3},{3,2},{4,5},{5,4},{6,7},{7,6},{8,9},{9,8},{10,11... | collective-permute-start | bytes 786440 | tf_op jit(solution)/shard_map/ppermute | solution.py:228
  47.2 8.7 %collective-permute-start.14 = (bf16[1,512,256]{2,1,0:T(8,128)(2,1)S(1)}, bf16[1,512,256]{2,1,0:T(8,128)(2,1)S(1)}, u32[]{:S(2)}, u32[]{:S(2)}) collective-permute-start(bf16[1,512,256]{2,1,0:T(8,128)(2,1)S(1)} %get-tuple-element.107), channel_id=1, source_target_pairs={{0,8},{4,12},{8,0},{12,4},{16,24},{20,28},{24,16},{28,20},{1,9},{5... | collective-permute-start | bytes 786440 | tf_op jit(solution)/shard_map/ppermute | solution.py:228
  47.3 5.9 %collective-permute-start.8 = (bf16[512,128]{1,0:T(8,128)(2,1)S(1)}, bf16[512,128]{1,0:T(8,128)(2,1)S(1)}, u32[]{:S(2)}, u32[]{:S(2)}) collective-permute-start(bf16[512,128]{1,0:T(8,128)(2,1)S(1)} %get-tuple-element.94.refs_2_), channel_id=1, source_target_pairs={{0,4},{4,0},{8,12},{12,8},{16,20},{20,16},{24,28},{28,24},{1,5},{5... | collective-permute-start | bytes 393224 | tf_op jit(solution)/shard_map/ppermute | solution.py:228
  48.4 11.2 %collective-permute-start.12 = (bf16[512,256]{1,0:T(8,128)(2,1)S(1)}, bf16[512,256]{1,0:T(8,128)(2,1)S(1)}, u32[]{:S(2)}, u32[]{:S(2)}) collective-permute-start(bf16[512,256]{1,0:T(8,128)(2,1)S(1)} %get-tuple-element.105), channel_id=1, source_target_pairs={{0,1},{1,0},{2,3},{3,2},{4,5},{5,4},{6,7},{7,6},{8,9},{9,8},{10,11... | collective-permute-start | bytes 786440 | tf_op jit(solution)/shard_map/ppermute | solution.py:228
  48.6 10.9 %collective-permute-start.13 = (bf16[512,256]{1,0:T(8,128)(2,1)S(1)}, bf16[512,256]{1,0:T(8,128)(2,1)S(1)}, u32[]{:S(2)}, u32[]{:S(2)}) collective-permute-start(bf16[512,256]{1,0:T(8,128)(2,1)S(1)} %get-tuple-element.106), channel_id=1, source_target_pairs={{0,2},{1,3},{2,0},{3,1},{4,6},{5,7},{6,4},{7,5},{8,10},{9,11},{10,... | collective-permute-start | bytes 786440 | tf_op jit(solution)/shard_map/ppermute | solution.py:228
  59.0 7.8 %collective-permute-start.17 = (bf16[512,256]{1,0:T(8,128)(2,1)S(1)}, bf16[512,256]{1,0:T(8,128)(2,1)S(1)}, u32[]{:S(2)}, u32[]{:S(2)}) collective-permute-start(bf16[512,256]{1,0:T(8,128)(2,1)S(1)} %get-tuple-element.116), channel_id=1, source_target_pairs={{0,1},{1,0},{2,3},{3,2},{4,5},{5,4},{6,7},{7,6},{8,9},{9,8},{10,11... | collective-permute-start | bytes 786440 | tf_op jit(solution)/shard_map/ppermute | solution.py:228
  59.1 5.9 %collective-permute-start.11 = (bf16[1,512,128]{2,1,0:T(8,128)(2,1)S(1)}, bf16[1,512,128]{2,1,0:T(8,128)(2,1)S(1)}, u32[]{:S(2)}, u32[]{:S(2)}) collective-permute-start(bf16[1,512,128]{2,1,0:T(8,128)(2,1)S(1)} %get-tuple-element.103), channel_id=1, source_target_pairs={{0,8},{4,12},{8,0},{12,4},{16,24},{20,28},{24,16},{28,20},{1,9},{5... | collective-permute-start | bytes 393224 | tf_op jit(solution)/shard_map/ppermute | solution.py:228
  59.4 11.7 %collective-permute-start.21 = (bf16[512,256]{1,0:T(8,128)(2,1)S(1)}, bf16[512,256]{1,0:T(8,128)(2,1)S(1)}, u32[]{:S(2)}, u32[]{:S(2)}) collective-permute-start(bf16[512,256]{1,0:T(8,128)(2,1)S(1)} %get-tuple-element.122), channel_id=1, source_target_pairs={{0,1},{1,0},{2,3},{3,2},{4,5},{5,4},{6,7},{7,6},{8,9},{9,8},{10,11... | collective-permute-start | bytes 786440 | tf_op jit(solution)/shard_map/ppermute | solution.py:228
  65.0 19.9 %copy-start.8 = (bf16[8,8]{0,1:T(8,128)(2,1)S(1)}, bf16[8,8]{0,1:T(8,128)(2,1)}, u32[]{:S(2)}) copy-start(bf16[8,8]{0,1:T(8,128)(2,1)} %copy.19) | copy-start | bytes 388
  67.0 7.9 %collective-permute-start.22 = (bf16[512,256]{1,0:T(8,128)(2,1)S(1)}, bf16[512,256]{1,0:T(8,128)(2,1)S(1)}, u32[]{:S(2)}, u32[]{:S(2)}) collective-permute-start(bf16[512,256]{1,0:T(8,128)(2,1)S(1)} %get-tuple-element.123), channel_id=1, source_target_pairs={{0,2},{1,3},{2,0},{3,1},{4,6},{5,7},{6,4},{7,5},{8,10},{9,11},{10,... | collective-permute-start | bytes 786440 | tf_op jit(solution)/shard_map/ppermute | solution.py:228
  68.7 13.8 %collective-permute-start.19 = (bf16[512,256]{1,0:T(8,128)(2,1)S(1)}, bf16[512,256]{1,0:T(8,128)(2,1)S(1)}, u32[]{:S(2)}, u32[]{:S(2)}) collective-permute-start(bf16[512,256]{1,0:T(8,128)(2,1)S(1)} %get-tuple-element.120.refs_1_.refs_2_), channel_id=1, source_target_pairs={{0,16},{4,20},{8,24},{12,28},{16,0},{20,4},{24,8},{28,12},{1,17},{... | collective-permute-start | bytes 786440 | tf_op jit(solution)/shard_map/ppermute | solution.py:228
  68.7 13.8 %collective-permute-start.20 = (bf16[512,256]{1,0:T(8,128)(2,1)S(1)}, bf16[512,256]{1,0:T(8,128)(2,1)S(1)}, u32[]{:S(2)}, u32[]{:S(2)}) collective-permute-start(bf16[512,256]{1,0:T(8,128)(2,1)S(1)} %get-tuple-element.120.refs_1_.refs_2_), channel_id=1, source_target_pairs={{0,4},{4,0},{8,12},{12,8},{16,20},{20,16},{24,28},{28,24},{1,5},{5... | collective-permute-start | bytes 786440 | tf_op jit(solution)/shard_map/ppermute | solution.py:228
  69.7 1.3 %collective-permute-start.16 = (bf16[512,128]{1,0:T(8,128)(2,1)S(1)}, bf16[512,128]{1,0:T(8,128)(2,1)S(1)}, u32[]{:S(2)}, u32[]{:S(2)}) collective-permute-start(bf16[512,128]{1,0:T(8,128)(2,1)S(1)} %get-tuple-element.114), channel_id=1, source_target_pairs={{0,1},{1,0},{2,3},{3,2},{4,5},{5,4},{6,7},{7,6},{8,9},{9,8},{10,11... | collective-permute-start | bytes 393224 | tf_op jit(solution)/shard_map/ppermute | solution.py:228
  82.5 9.2 %collective-permute-start.25 = (bf16[512,256]{1,0:T(8,128)(2,1)S(1)}, bf16[512,256]{1,0:T(8,128)(2,1)S(1)}, u32[]{:S(2)}, u32[]{:S(2)}) collective-permute-start(bf16[512,256]{1,0:T(8,128)(2,1)S(1)} %get-tuple-element.130.refs_2_.refs_3_), channel_id=1, source_target_pairs={{0,4},{4,0},{8,12},{12,8},{16,20},{20,16},{24,28},{28,24},{1,5},{5... | collective-permute-start | bytes 786440 | tf_op jit(solution)/shard_map/ppermute | solution.py:228
  83.2 13.5 %collective-permute-start.27 = (bf16[512,256]{1,0:T(8,128)(2,1)S(1)}, bf16[512,256]{1,0:T(8,128)(2,1)S(1)}, u32[]{:S(2)}, u32[]{:S(2)}) collective-permute-start(bf16[512,256]{1,0:T(8,128)(2,1)S(1)} %get-tuple-element.134.refs_1_.refs_2_), channel_id=1, source_target_pairs={{0,16},{4,20},{8,24},{12,28},{16,0},{20,4},{24,8},{28,12},{1,17},{... | collective-permute-start | bytes 786440 | tf_op jit(solution)/shard_map/ppermute | solution.py:228
  83.2 13.5 %collective-permute-start.28 = (bf16[512,256]{1,0:T(8,128)(2,1)S(1)}, bf16[512,256]{1,0:T(8,128)(2,1)S(1)}, u32[]{:S(2)}, u32[]{:S(2)}) collective-permute-start(bf16[512,256]{1,0:T(8,128)(2,1)S(1)} %get-tuple-element.134.refs_1_.refs_2_), channel_id=1, source_target_pairs={{0,4},{4,0},{8,12},{12,8},{16,20},{20,16},{24,28},{28,24},{1,5},{5... | collective-permute-start | bytes 786440 | tf_op jit(solution)/shard_map/ppermute | solution.py:228
  84.5 1.3 %collective-permute-start.15 = (bf16[512,128]{1,0:T(8,128)(2,1)S(1)}, bf16[512,128]{1,0:T(8,128)(2,1)S(1)}, u32[]{:S(2)}, u32[]{:S(2)}) collective-permute-start(bf16[512,128]{1,0:T(8,128)(2,1)S(1)} %get-tuple-element.112), channel_id=1, source_target_pairs={{0,1},{1,0},{2,3},{3,2},{4,5},{5,4},{6,7},{7,6},{8,9},{9,8},{10,11... | collective-permute-start | bytes 393224 | tf_op jit(solution)/shard_map/ppermute | solution.py:228
  84.5 5.9 %collective-permute-start.18 = (bf16[512,128]{1,0:T(8,128)(2,1)S(1)}, bf16[512,128]{1,0:T(8,128)(2,1)S(1)}, u32[]{:S(2)}, u32[]{:S(2)}) collective-permute-start(bf16[512,128]{1,0:T(8,128)(2,1)S(1)} %get-tuple-element.119), channel_id=1, source_target_pairs={{0,2},{1,3},{2,0},{3,1},{4,6},{5,7},{6,4},{7,5},{8,10},{9,11},{10,... | collective-permute-start | bytes 393224 | tf_op jit(solution)/shard_map/ppermute | solution.py:228
  91.9 12.0 %collective-permute-start.26 = (bf16[1,512,256]{2,1,0:T(8,128)(2,1)S(1)}, bf16[1,512,256]{2,1,0:T(8,128)(2,1)S(1)}, u32[]{:S(2)}, u32[]{:S(2)}) collective-permute-start(bf16[1,512,256]{2,1,0:T(8,128)(2,1)S(1)} %get-tuple-element.133), channel_id=1, source_target_pairs={{0,8},{4,12},{8,0},{12,4},{16,24},{20,28},{24,16},{28,20},{1,9},{5... | collective-permute-start | bytes 786440 | tf_op jit(solution)/shard_map/ppermute | solution.py:228
  96.6 11.3 %collective-permute-start.30 = (bf16[512,256]{1,0:T(8,128)(2,1)S(1)}, bf16[512,256]{1,0:T(8,128)(2,1)S(1)}, u32[]{:S(2)}, u32[]{:S(2)}) collective-permute-start(bf16[512,256]{1,0:T(8,128)(2,1)S(1)} %get-tuple-element.140.refs_2_.refs_3_), channel_id=1, source_target_pairs={{0,4},{4,0},{8,12},{12,8},{16,20},{20,16},{24,28},{28,24},{1,5},{5... | collective-permute-start | bytes 786440 | tf_op jit(solution)/shard_map/ppermute | solution.py:228
  97.0 8.7 %collective-permute-start.23 = (bf16[512,128]{1,0:T(8,128)(2,1)S(1)}, bf16[512,128]{1,0:T(8,128)(2,1)S(1)}, u32[]{:S(2)}, u32[]{:S(2)}) collective-permute-start(bf16[512,128]{1,0:T(8,128)(2,1)S(1)} %get-tuple-element.129.refs_1_.refs_2_), channel_id=1, source_target_pairs={{0,16},{4,20},{8,24},{12,28},{16,0},{20,4},{24,8},{28,12},{1,17},{... | collective-permute-start | bytes 393224 | tf_op jit(solution)/shard_map/ppermute | solution.py:228
  97.0 10.6 %collective-permute-start.24 = (bf16[512,128]{1,0:T(8,128)(2,1)S(1)}, bf16[512,128]{1,0:T(8,128)(2,1)S(1)}, u32[]{:S(2)}, u32[]{:S(2)}) collective-permute-start(bf16[512,128]{1,0:T(8,128)(2,1)S(1)} %get-tuple-element.129.refs_1_.refs_2_), channel_id=1, source_target_pairs={{0,4},{4,0},{8,12},{12,8},{16,20},{20,16},{24,28},{28,24},{1,5},{5... | collective-permute-start | bytes 393224 | tf_op jit(solution)/shard_map/ppermute | solution.py:228
  107.6 5.0 %collective-permute-start.29 = (bf16[512,128]{1,0:T(8,128)(2,1)S(1)}, bf16[512,128]{1,0:T(8,128)(2,1)S(1)}, u32[]{:S(2)}, u32[]{:S(2)}) collective-permute-start(bf16[512,128]{1,0:T(8,128)(2,1)S(1)} %get-tuple-element.138.refs_2_.refs_3_), channel_id=1, source_target_pairs={{0,4},{4,0},{8,12},{12,8},{16,20},{20,16},{24,28},{28,24},{1,5},{5... | collective-permute-start | bytes 393224 | tf_op jit(solution)/shard_map/ppermute | solution.py:228
  108.2 8.5 %collective-permute-start.32 = (bf16[1,512,256]{2,1,0:T(8,128)(2,1)S(1)}, bf16[1,512,256]{2,1,0:T(8,128)(2,1)S(1)}, u32[]{:S(2)}, u32[]{:S(2)}) collective-permute-start(bf16[1,512,256]{2,1,0:T(8,128)(2,1)S(1)} %get-tuple-element.145), channel_id=1, source_target_pairs={{0,8},{4,12},{8,0},{12,4},{16,24},{20,28},{24,16},{28,20},{1,9},{5... | collective-permute-start | bytes 786440 | tf_op jit(solution)/shard_map/ppermute | solution.py:228
  112.7 5.3 %collective-permute-start.31 = (bf16[1,512,128]{2,1,0:T(8,128)(2,1)S(1)}, bf16[1,512,128]{2,1,0:T(8,128)(2,1)S(1)}, u32[]{:S(2)}, u32[]{:S(2)}) collective-permute-start(bf16[1,512,128]{2,1,0:T(8,128)(2,1)S(1)} %get-tuple-element.144), channel_id=1, source_target_pairs={{0,8},{4,12},{8,0},{12,4},{16,24},{20,28},{24,16},{28,20},{1,9},{5... | collective-permute-start | bytes 393224 | tf_op jit(solution)/shard_map/ppermute | solution.py:228

commit v5 on v4

--- a/solution.py
+++ b/solution.py
@@ -13,8 +13,8 @@
 SLAB = 64
 MATMUL_ROWS = 256
 VMEM_LIMIT = 16 * 1024 * 1024
-LINK_SHARE = {"far": 0.041, "near": 0.0205, "partial": 0.0205, "core": 0.012, "row": 0.0205}
-LATENCY = 1.5
+LINK_SHARE = {'far': 0.0312, 'near': 0.0282, 'partial': 0.0371, 'core': 0.0223, 'row': 0.0375}
+LATENCY = 1.156
 
 smem = pl.BlockSpec(memory_space=pltpu.SMEM)
 vmem = pl.BlockSpec(memory_space=pltpu.VMEM)
@@ -24,32 +24,32 @@
 def chunk_bounds(columns):
     if columns % 128:
         return [(0, columns)]
-    marks = list(range(0, columns, 256))
-    return [(lo, min(256, columns - lo)) for lo in marks]
+    units = columns // 128
+    units = [2] + [1] * (units - 2) if units > 2 else [units]
+    out, lo = [], 0
+    for unit in units:
+        out.append((lo, 128 * unit))
+        lo += 128 * unit
+    return out
 
 
 class Chain:
-    def __init__(self):
-        self.token = []
-
     def call(self, kernel, name, out_shape, arrays, scalars=(), scratch=(), out_specs=None, whole=(), after=(), aliases=None):
         count = len(scalars) + len(arrays) + len(whole)
-        outs = count + len(after) + len(self.token)
+        outs = count + len(after)
 
         def body(*refs):
-            kernel(*refs[:count], *refs[outs:outs + len(out_shape)], *refs[outs + len(out_shape) + 1:])
-
-        *results, token = pl.pallas_call(
-            body, name=name, out_shape=[*out_shape, jax.ShapeDtypeStruct((8, 128), F32)],
+            kernel(*refs[:count], *refs[outs:outs + len(out_shape)], *refs[outs + len(out_shape):])
+
+        return pl.pallas_call(
+            body, name=name, out_shape=list(out_shape),
             in_specs=[smem] * len(scalars) + [vmem] * len(arrays) + [unread] * (outs - len(scalars) - len(arrays)),
-            out_specs=[*(out_specs or [vmem] * len(out_shape)), unread],
+            out_specs=out_specs or [vmem] * len(out_shape),
             scratch_shapes=list(scratch),
             input_output_aliases=aliases or {},
             compiler_params=pltpu.CompilerParams(vmem_limit_bytes=VMEM_LIMIT),
             cost_estimate=pl.CostEstimate(flops=0, transcendentals=0, bytes_accessed=0),
-        )(*scalars, *arrays, *whole, *after, *self.token)
-        self.token = [token]
-        return results
+        )(*scalars, *arrays, *whole, *after)
 
     def pin(self, *arrays):
         return self.call(
@@ -90,7 +90,7 @@
 
         slabs(rows, body)
 
-    outs = [jax.ShapeDtypeStruct((rows, width), BF16), jax.ShapeDtypeStruct((8, width), jnp.int32)]
+    outs = [jax.ShapeDtypeStruct((rows, width), BF16), jax.ShapeDtypeStruct((8, 256), jnp.int32)]
     return chain.call(kernel, "mask_first", outs, [own], [block_rows])
 
 
@@ -283,14 +283,9 @@
                 block = mask_chunk(chain, left, own, lo, width, [last_far])
             held, received = yield from mixing(block, False, note_far)
             parts = mix_multiply(chain, table(False), entries, held, received, weights, n_row)
-            terms, targets = {d: [part] for d, part in enumerate(parts)}, list(range(n_row))
-            for bit in row_bits:
-                sent, targets = split(targets, bit)
-                for t in sent:
-                    block = terms[t][0] if len(terms[t]) == 1 else add_up(chain, terms[t])
-                    terms[t ^ bit].append(swap(block, "row", n_row, bit))
-                yield "core" if bit == row_bits[0] else "row"
-            block = add_up(chain, terms[0])
+            got = [swap(parts[d], "row", n_row, d) for d in range(1, n_row)]
+            yield "row"
+            block = add_up(chain, [parts[0], *got])
             held, received = yield from mixing(block, True)
             result = finish(chain, table(True), entries, left, held, received, lo, columns, result)
 

time: 119 us -> 111 us (0.933)
  waiting for transfers between devices: 72.3 us -> 49.3 us
  starting transfers between devices: 23.6 us -> 44.8 us
  local copies, waits for them, and re-layouts: 5.11 us -> 1.16 us
  Pallas kernels: 16.9 us -> 14.7 us
    ppermute x33 -> x44, waiting for transfers between devices: 72.3 us -> 49.3 us  [swap(): return lax.ppermute(x, axis, [(i, i ^ bit) for i in range(size)])]
    ppermute x33 -> x44, starting transfers between devices: 23.6 us -> 44.8 us  [swap(): return lax.ppermute(x, axis, [(i, i ^ bit) for i in range(size)])]
    unnamed x21 -> x8, local copies, waits for them, and re-layouts: 4.36 us -> 1.09 us
    pallas_call x29 -> x34, Pallas kernels: 16.9 us -> 14.7 us  [call(): pl.pallas_call(body, name=name, out_shape=list(out_shape), in_specs=[smem...]
  transfers between devices with their start and end apart: 33 -> 44, of which waited for: 20 -> 20; matrix products, arithmetic and copies ran while one was open for 1% -> 0% of each run, Pallas kernels for 13% -> 12%
where the time goes in v5:
time: 111 us
  waiting for transfers between devices  49.3 us (44%)
  starting transfers between devices  44.8 us (40%)
  Pallas kernels  14.7 us (13%)
  local copies, waits for them, and re-layouts  1.16 us (1%)
    ppermute x44, waiting for transfers between devices, swap(): return lax.ppermute(x, axis, [(i, i ^ bit) for i in range(size)])  49.3 us
    ppermute x44, starting transfers between devices, swap(): return lax.ppermute(x, axis, [(i, i ^ bit) for i in range(size)])  44.8 us
    pallas_call x34, Pallas kernels, call(): pl.pallas_call(body, name=name, out_shape=list(out_shape), in_specs=[smem...  14.7 us
  transfers between devices with their start and end apart: 44, of which 20 were waited for; matrix products, arithmetic and copies ran while one was open for 0% of the time, Pallas kernels for 12%

profile of v5, /device:TPU:0, one launch (start us, length us, event | category | flops | bytes accessed | tf_op | source)
XLA Modules:
  0.0 111.0 jit_solution(4976791390382122670)
XLA Ops:
  0.7 1.1 copy-done.1
  1.9 4.1 %collective-permute-start = (bf16[512,256]{1,0:T(8,128)(2,1)S(1)}, bf16[512,256]{1,0:T(8,128)(2,1)S(1)}, u32[]{:S(2)}, u32[]{:S(2)}) collective-permute-start(bf16[512,256]{1,0:T(8,128)(2,1)S(1)} %get-tuple-element.40.refs_1_), channel_id=1, source_target_pairs={{0,16},{4,20},{8,24},{12,28},{16,0},{20,4},{24,8},{28,12},{1,17},{... | collective-permute-start | bytes 786440 | tf_op jit(solution)/shard_map/ppermute | solution.py:228
  6.0 1.5 %collective-permute-start.34 = (bf16[512,256]{1,0:T(8,128)(2,1)S(1)}, bf16[512,256]{1,0:T(8,128)(2,1)S(1)}, u32[]{:S(2)}, u32[]{:S(2)}) collective-permute-start(bf16[512,256]{1,0:T(8,128)(2,1)S(1)} %get-tuple-element.40.refs_1_), channel_id=1, source_target_pairs={{0,4},{4,0},{8,12},{12,8},{16,20},{20,16},{24,28},{28,24},{1,5},{5... | collective-permute-start | bytes 786440 | tf_op jit(solution)/shard_map/ppermute | solution.py:228
  7.5 10.4 %collective-permute-done.refs_2_.refs_0_ = bf16[512,256]{1,0:T(8,128)(2,1)S(1)} collective-permute-done((bf16[512,256]{1,0:T(8,128)(2,1)S(1)}, bf16[512,256]{1,0:T(8,128)(2,1)S(1)}, u32[]{:S(2)}, u32[]{:S(2)}) %collective-permute-start) | collective-permute-done | bytes 262176 | tf_op jit(solution)/shard_map/ppermute | solution.py:228
  18.0 1.6 %collective-permute-start.35 = (bf16[512,256]{1,0:T(8,128)(2,1)S(1)}, bf16[512,256]{1,0:T(8,128)(2,1)S(1)}, u32[]{:S(2)}, u32[]{:S(2)}) collective-permute-start(bf16[512,256]{1,0:T(8,128)(2,1)S(1)} %get-tuple-element.65.refs_2_), channel_id=1, source_target_pairs={{0,4},{4,0},{8,12},{12,8},{16,20},{20,16},{24,28},{28,24},{1,5},{5... | collective-permute-start | bytes 786440 | tf_op jit(solution)/shard_map/ppermute | solution.py:228
  19.6 0.6 coefficients.3.refs_0_
  20.3 5.3 %collective-permute-done.35.refs_4_ = bf16[512,256]{1,0:T(8,128)(2,1)S(1)} collective-permute-done((bf16[512,256]{1,0:T(8,128)(2,1)S(1)}, bf16[512,256]{1,0:T(8,128)(2,1)S(1)}, u32[]{:S(2)}, u32[]{:S(2)}) %collective-permute-start.35) | collective-permute-done | bytes 262176 | tf_op jit(solution)/shard_map/ppermute | solution.py:228
  25.8 1.5 %collective-permute-start.36 = (bf16[1,512,256]{2,1,0:T(8,128)(2,1)S(1)}, bf16[1,512,256]{2,1,0:T(8,128)(2,1)S(1)}, u32[]{:S(2)}, u32[]{:S(2)}) collective-permute-start(bf16[1,512,256]{2,1,0:T(8,128)(2,1)S(1)} %mix.14), channel_id=1, source_target_pairs={{0,8},{4,12},{8,0},{12,4},{16,24},{20,28},{24,16},{28,20},{1,9},{5... | collective-permute-start | bytes 786440 | tf_op jit(solution)/shard_map/ppermute | solution.py:228
  27.3 1.5 %collective-permute-start.24 = (bf16[512,128]{1,0:T(8,128)(2,1)S(1)}, bf16[512,128]{1,0:T(8,128)(2,1)S(1)}, u32[]{:S(2)}, u32[]{:S(2)}) collective-permute-start(bf16[512,128]{1,0:T(8,128)(2,1)S(1)} %mask_chunk.3.refs_1_), channel_id=1, source_target_pairs={{0,4},{4,0},{8,12},{12,8},{16,20},{20,16},{24,28},{28,24},{1,5},{5... | collective-permute-start | bytes 393224 | tf_op jit(solution)/shard_map/ppermute | solution.py:228
  28.9 3.4 %collective-permute-start.2 = (bf16[512,128]{1,0:T(8,128)(2,1)S(1)}, bf16[512,128]{1,0:T(8,128)(2,1)S(1)}, u32[]{:S(2)}, u32[]{:S(2)}) collective-permute-start(bf16[512,128]{1,0:T(8,128)(2,1)S(1)} %mask_chunk.4.refs_1_), channel_id=1, source_target_pairs={{0,16},{4,20},{8,24},{12,28},{16,0},{20,4},{24,8},{28,12},{1,17},{... | collective-permute-start | bytes 393224 | tf_op jit(solution)/shard_map/ppermute | solution.py:228
  32.4 0.5 collective-permute-start.14
  32.9 1.5 %collective-permute-start.25 = (bf16[512,128]{1,0:T(8,128)(2,1)S(1)}, bf16[512,128]{1,0:T(8,128)(2,1)S(1)}, u32[]{:S(2)}, u32[]{:S(2)}) collective-permute-start(bf16[512,128]{1,0:T(8,128)(2,1)S(1)} %get-tuple-element.57.refs_2_), channel_id=1, source_target_pairs={{0,4},{4,0},{8,12},{12,8},{16,20},{20,16},{24,28},{28,24},{1,5},{5... | collective-permute-start | bytes 393224 | tf_op jit(solution)/shard_map/ppermute | solution.py:228
  34.4 2.0 %collective-permute-done.2.refs_2_.refs_0_ = bf16[512,128]{1,0:T(8,128)(2,1)S(1)} collective-permute-done((bf16[512,128]{1,0:T(8,128)(2,1)S(1)}, bf16[512,128]{1,0:T(8,128)(2,1)S(1)}, u32[]{:S(2)}, u32[]{:S(2)}) %collective-permute-start.2) | collective-permute-done | bytes 131104 | tf_op jit(solution)/shard_map/ppermute | solution.py:228
  36.5 2.2 %collective-permute-start.3 = (bf16[512,128]{1,0:T(8,128)(2,1)S(1)}, bf16[512,128]{1,0:T(8,128)(2,1)S(1)}, u32[]{:S(2)}, u32[]{:S(2)}) collective-permute-start(bf16[512,128]{1,0:T(8,128)(2,1)S(1)} %mask_chunk.5.refs_1_), channel_id=1, source_target_pairs={{0,16},{4,20},{8,24},{12,28},{16,0},{20,4},{24,8},{28,12},{1,17},{... | collective-permute-start | bytes 393224 | tf_op jit(solution)/shard_map/ppermute | solution.py:228
  38.7 1.4 %collective-permute-start.4 = (bf16[512,128]{1,0:T(8,128)(2,1)S(1)}, bf16[512,128]{1,0:T(8,128)(2,1)S(1)}, u32[]{:S(2)}, u32[]{:S(2)}) collective-permute-start(bf16[512,128]{1,0:T(8,128)(2,1)S(1)} %mask_chunk.5.refs_1_), channel_id=1, source_target_pairs={{0,4},{4,0},{8,12},{12,8},{16,20},{20,16},{24,28},{28,24},{1,5},{5... | collective-permute-start | bytes 393224 | tf_op jit(solution)/shard_map/ppermute | solution.py:228
  40.1 0.6 collective-permute-start.15
  40.7 2.1 %mix_multiply.7 = (bf16[512,256]{1,0:T(8,128)(2,1)S(1)}, bf16[512,256]{1,0:T(8,128)(2,1)S(1)}, bf16[512,256]{1,0:T(8,128)(2,1)S(1)}, bf16[512,256]{1,0:T(8,128)(2,1)S(1)}) custom-call(f32[8,256]{1,0:T(8,128)S(1)} %coefficients.3.refs_0_, bf16[512,256]{1,0:T(8,128)(2,1)S(1)} %get-tuple-element.40.refs_1_, bf16[512,256]{1,0:T(8,128)(2,1)S(1)} %get-tuple-element.65.refs_2_, ...), custom_call_target="tpu_custom_call" | custom-call | tf_op jit(solution)/shard_map/mix_multiply/pallas_call | solution.py:44
  42.9 1.6 %collective-permute-start.38 = (bf16[512,256]{1,0:T(8,128)(2,1)S(1)}, bf16[512,256]{1,0:T(8,128)(2,1)S(1)}, u32[]{:S(2)}, u32[]{:S(2)}) collective-permute-start(bf16[512,256]{1,0:T(8,128)(2,1)S(1)} %get-tuple-element.69), channel_id=1, source_target_pairs={{0,2},{1,3},{2,0},{3,1},{4,6},{5,7},{6,4},{7,5},{8,10},{9,11},{10,... | collective-permute-start | bytes 786440 | tf_op jit(solution)/shard_map/ppermute | solution.py:228
  44.9 2.3 %collective-permute-start.26 = (bf16[1,512,128]{2,1,0:T(8,128)(2,1)S(1)}, bf16[1,512,128]{2,1,0:T(8,128)(2,1)S(1)}, u32[]{:S(2)}, u32[]{:S(2)}) collective-permute-start(bf16[1,512,128]{2,1,0:T(8,128)(2,1)S(1)} %mix.12), channel_id=1, source_target_pairs={{0,8},{4,12},{8,0},{12,4},{16,24},{20,28},{24,16},{28,20},{1,9},{5... | collective-permute-start | bytes 393224 | tf_op jit(solution)/shard_map/ppermute | solution.py:228
  47.5 3.8 %collective-permute-done.26.refs_5_ = bf16[1,512,128]{2,1,0:T(8,128)(2,1)S(1)} collective-permute-done((bf16[1,512,128]{2,1,0:T(8,128)(2,1)S(1)}, bf16[1,512,128]{2,1,0:T(8,128)(2,1)S(1)}, u32[]{:S(2)}, u32[]{:S(2)}) %collective-permute-start.26) | collective-permute-done | bytes 131104 | tf_op jit(solution)/shard_map/ppermute | solution.py:228
  51.2 1.7 %collective-permute-start.16 = (bf16[1,512,128]{2,1,0:T(8,128)(2,1)S(1)}, bf16[1,512,128]{2,1,0:T(8,128)(2,1)S(1)}, u32[]{:S(2)}, u32[]{:S(2)}) collective-permute-start(bf16[1,512,128]{2,1,0:T(8,128)(2,1)S(1)} %mix.10), channel_id=1, source_target_pairs={{0,8},{4,12},{8,0},{12,4},{16,24},{20,28},{24,16},{28,20},{1,9},{5... | collective-permute-start | bytes 393224 | tf_op jit(solution)/shard_map/ppermute | solution.py:228
  53.0 1.8 %mix_multiply.6 = (bf16[512,128]{1,0:T(8,128)(2,1)S(1)}, bf16[512,128]{1,0:T(8,128)(2,1)S(1)}, bf16[512,128]{1,0:T(8,128)(2,1)S(1)}, bf16[512,128]{1,0:T(8,128)(2,1)S(1)}) custom-call(f32[8,256]{1,0:T(8,128)S(1)} %coefficients.3.refs_0_, bf16[512,128]{1,0:T(8,128)(2,1)S(1)} %mask_chunk.3.refs_1_, bf16[512,128]{1,0:T(8,128)(2,1)S(1)} %get-tuple-element.57.refs_2_, ...), custom_call_target="tpu_custom_call" | custom-call | tf_op jit(solution)/shard_map/mix_multiply/pallas_call | solution.py:44
  55.1 0.4 collective-permute-start.6
  55.5 1.3 %collective-permute-done.39.refs_3_ = bf16[512,256]{1,0:T(8,128)(2,1)S(1)} collective-permute-done((bf16[512,256]{1,0:T(8,128)(2,1)S(1)}, bf16[512,256]{1,0:T(8,128)(2,1)S(1)}, u32[]{:S(2)}, u32[]{:S(2)}) %collective-permute-start.39) | collective-permute-done | bytes 262176 | tf_op jit(solution)/shard_map/ppermute | solution.py:228
  56.9 0.9 collective-permute-start.40
  57.8 0.8 collective-permute-start.41
  58.6 1.5 %collective-permute-start.28 = (bf16[512,128]{1,0:T(8,128)(2,1)S(1)}, bf16[512,128]{1,0:T(8,128)(2,1)S(1)}, u32[]{:S(2)}, u32[]{:S(2)}) collective-permute-start(bf16[512,128]{1,0:T(8,128)(2,1)S(1)} %get-tuple-element.61), channel_id=1, source_target_pairs={{0,2},{1,3},{2,0},{3,1},{4,6},{5,7},{6,4},{7,5},{8,10},{9,11},{10,... | collective-permute-start | bytes 393224 | tf_op jit(solution)/shard_map/ppermute | solution.py:228
  60.2 1.9 %mix_multiply.5 = (bf16[512,128]{1,0:T(8,128)(2,1)S(1)}, bf16[512,128]{1,0:T(8,128)(2,1)S(1)}, bf16[512,128]{1,0:T(8,128)(2,1)S(1)}, bf16[512,128]{1,0:T(8,128)(2,1)S(1)}) custom-call(f32[8,256]{1,0:T(8,128)S(1)} %coefficients.3.refs_0_, bf16[512,128]{1,0:T(8,128)(2,1)S(1)} %mask_chunk.4.refs_1_, bf16[512,128]{1,0:T(8,128)(2,1)S(1)} %get-tuple-element.49.refs_2_, ...), custom_call_target="tpu_custom_call" | custom-call | tf_op jit(solution)/shard_map/mix_multiply/pallas_call | solution.py:44
  62.2 0.9 collective-permute-done.6.refs_5_
  63.1 1.9 %mix_multiply.4 = (bf16[512,128]{1,0:T(8,128)(2,1)S(1)}, bf16[512,128]{1,0:T(8,128)(2,1)S(1)}, bf16[512,128]{1,0:T(8,128)(2,1)S(1)}, bf16[512,128]{1,0:T(8,128)(2,1)S(1)}) custom-call(f32[8,256]{1,0:T(8,128)S(1)} %coefficients.3.refs_0_, bf16[512,128]{1,0:T(8,128)(2,1)S(1)} %mask_chunk.5.refs_1_, bf16[512,128]{1,0:T(8,128)(2,1)S(1)} %get-tuple-element.41.refs_2_, ...), custom_call_target="tpu_custom_call" | custom-call | tf_op jit(solution)/shard_map/mix_multiply/pallas_call | solution.py:44
  65.0 1.6 %collective-permute-start.18 = (bf16[512,128]{1,0:T(8,128)(2,1)S(1)}, bf16[512,128]{1,0:T(8,128)(2,1)S(1)}, u32[]{:S(2)}, u32[]{:S(2)}) collective-permute-start(bf16[512,128]{1,0:T(8,128)(2,1)S(1)} %get-tuple-element.53), channel_id=1, source_target_pairs={{0,2},{1,3},{2,0},{3,1},{4,6},{5,7},{6,4},{7,5},{8,10},{9,11},{10,... | collective-permute-start | bytes 393224 | tf_op jit(solution)/shard_map/ppermute | solution.py:228
  66.6 1.1 %collective-permute-done.29.refs_3_ = bf16[512,128]{1,0:T(8,128)(2,1)S(1)} collective-permute-done((bf16[512,128]{1,0:T(8,128)(2,1)S(1)}, bf16[512,128]{1,0:T(8,128)(2,1)S(1)}, u32[]{:S(2)}, u32[]{:S(2)}) %collective-permute-start.29) | collective-permute-done | bytes 131104 | tf_op jit(solution)/shard_map/ppermute | solution.py:228
  67.7 0.4 collective-permute-start.19
  68.5 3.6 %collective-permute-done.40.refs_0_ = bf16[512,256]{1,0:T(8,128)(2,1)S(1)} collective-permute-done((bf16[512,256]{1,0:T(8,128)(2,1)S(1)}, bf16[512,256]{1,0:T(8,128)(2,1)S(1)}, u32[]{:S(2)}, u32[]{:S(2)}) %collective-permute-start.40) | collective-permute-done | bytes 262176 | tf_op jit(solution)/shard_map/ppermute | solution.py:228
  72.1 1.5 %collective-permute-start.8 = (bf16[512,128]{1,0:T(8,128)(2,1)S(1)}, bf16[512,128]{1,0:T(8,128)(2,1)S(1)}, u32[]{:S(2)}, u32[]{:S(2)}) collective-permute-start(bf16[512,128]{1,0:T(8,128)(2,1)S(1)} %get-tuple-element.45), channel_id=1, source_target_pairs={{0,2},{1,3},{2,0},{3,1},{4,6},{5,7},{6,4},{7,5},{8,10},{9,11},{10,... | collective-permute-start | bytes 393224 | tf_op jit(solution)/shard_map/ppermute | solution.py:228
  73.7 1.4 %collective-permute-start.42 = (bf16[512,256]{1,0:T(8,128)(2,1)S(1)}, bf16[512,256]{1,0:T(8,128)(2,1)S(1)}, u32[]{:S(2)}, u32[]{:S(2)}) collective-permute-start(bf16[512,256]{1,0:T(8,128)(2,1)S(1)} %get-tuple-element.71.refs_2_.refs_3_), channel_id=1, source_target_pairs={{0,4},{4,0},{8,12},{12,8},{16,20},{20,16},{24,28},{28,24},{1,5},{5... | collective-permute-start | bytes 786440 | tf_op jit(solution)/shard_map/ppermute | solution.py:228
  75.1 0.9 collective-permute-start.30
  76.0 0.6 collective-permute-start.31
  76.8 0.7 collective-permute-done.8.refs_2_
  77.5 1.4 %collective-permute-start.20 = (bf16[512,128]{1,0:T(8,128)(2,1)S(1)}, bf16[512,128]{1,0:T(8,128)(2,1)S(1)}, u32[]{:S(2)}, u32[]{:S(2)}) collective-permute-start(bf16[512,128]{1,0:T(8,128)(2,1)S(1)} %add_up.5.refs_1_.refs_2_), channel_id=1, source_target_pairs={{0,16},{4,20},{8,24},{12,28},{16,0},{20,4},{24,8},{28,12},{1,17},{... | collective-permute-start | bytes 393224 | tf_op jit(solution)/shard_map/ppermute | solution.py:228
  78.9 0.4 collective-permute-done.9.refs_3_
  79.4 1.4 %collective-permute-start.21 = (bf16[512,128]{1,0:T(8,128)(2,1)S(1)}, bf16[512,128]{1,0:T(8,128)(2,1)S(1)}, u32[]{:S(2)}, u32[]{:S(2)}) collective-permute-start(bf16[512,128]{1,0:T(8,128)(2,1)S(1)} %add_up.5.refs_1_.refs_2_), channel_id=1, source_target_pairs={{0,4},{4,0},{8,12},{12,8},{16,20},{20,16},{24,28},{28,24},{1,5},{5... | collective-permute-start | bytes 393224 | tf_op jit(solution)/shard_map/ppermute | solution.py:228
  80.8 7.1 %collective-permute-done.30.refs_0_ = bf16[512,128]{1,0:T(8,128)(2,1)S(1)} collective-permute-done((bf16[512,128]{1,0:T(8,128)(2,1)S(1)}, bf16[512,128]{1,0:T(8,128)(2,1)S(1)}, u32[]{:S(2)}, u32[]{:S(2)}) %collective-permute-start.30) | collective-permute-done | bytes 131104 | tf_op jit(solution)/shard_map/ppermute | solution.py:228
  88.0 0.7 collective-permute-start.11
  88.7 0.6 coefficients.2.refs_0_
  89.4 3.9 %collective-permute-done.20.refs_0_ = bf16[512,128]{1,0:T(8,128)(2,1)S(1)} collective-permute-done((bf16[512,128]{1,0:T(8,128)(2,1)S(1)}, bf16[512,128]{1,0:T(8,128)(2,1)S(1)}, u32[]{:S(2)}, u32[]{:S(2)}) %collective-permute-start.20) | collective-permute-done | bytes 131104 | tf_op jit(solution)/shard_map/ppermute | solution.py:228
  93.2 0.7 collective-permute-start.32
  93.9 1.3 %collective-permute-start.22 = (bf16[512,128]{1,0:T(8,128)(2,1)S(1)}, bf16[512,128]{1,0:T(8,128)(2,1)S(1)}, u32[]{:S(2)}, u32[]{:S(2)}) collective-permute-start(bf16[512,128]{1,0:T(8,128)(2,1)S(1)} %get-tuple-element.55.refs_2_.refs_3_), channel_id=1, source_target_pairs={{0,4},{4,0},{8,12},{12,8},{16,20},{20,16},{24,28},{28,24},{1,5},{5... | collective-permute-start | bytes 393224 | tf_op jit(solution)/shard_map/ppermute | solution.py:228
  95.6 0.3 collective-permute-done.10.refs_0_
  95.9 0.7 collective-permute-start.12
  96.6 1.6 %collective-permute-done.32.refs_4_.refs_5_ = bf16[512,128]{1,0:T(8,128)(2,1)S(1)} collective-permute-done((bf16[512,128]{1,0:T(8,128)(2,1)S(1)}, bf16[512,128]{1,0:T(8,128)(2,1)S(1)}, u32[]{:S(2)}, u32[]{:S(2)}) %collective-permute-start.32) | collective-permute-done | bytes 131104 | tf_op jit(solution)/shard_map/ppermute | solution.py:228
  98.4 0.6 collective-permute-start.33
  98.9 1.9 %collective-permute-done.22.refs_4_.refs_5_ = bf16[512,128]{1,0:T(8,128)(2,1)S(1)} collective-permute-done((bf16[512,128]{1,0:T(8,128)(2,1)S(1)}, bf16[512,128]{1,0:T(8,128)(2,1)S(1)}, u32[]{:S(2)}, u32[]{:S(2)}) %collective-permute-start.22) | collective-permute-done | bytes 131104 | tf_op jit(solution)/shard_map/ppermute | solution.py:228
  101.0 0.7 collective-permute-start.23
  101.7 0.7 collective-permute-done.12.refs_4_.refs_5_
  102.6 0.7 collective-permute-start.13
  103.3 1.4 %collective-permute-done.43.refs_6_ = bf16[1,512,256]{2,1,0:T(8,128)(2,1)S(1)} collective-permute-done((bf16[1,512,256]{2,1,0:T(8,128)(2,1)S(1)}, bf16[1,512,256]{2,1,0:T(8,128)(2,1)S(1)}, u32[]{:S(2)}, u32[]{:S(2)}) %collective-permute-start.43) | collective-permute-done | bytes 262176 | tf_op jit(solution)/shard_map/ppermute | solution.py:228
  104.8 1.0 finish.4.refs_7_
  105.8 1.5 %collective-permute-done.33.refs_6_ = bf16[1,512,128]{2,1,0:T(8,128)(2,1)S(1)} collective-permute-done((bf16[1,512,128]{2,1,0:T(8,128)(2,1)S(1)}, bf16[1,512,128]{2,1,0:T(8,128)(2,1)S(1)}, u32[]{:S(2)}, u32[]{:S(2)}) %collective-permute-start.33) | collective-permute-done | bytes 131104 | tf_op jit(solution)/shard_map/ppermute | solution.py:228
  107.3 0.9 finish.5.refs_7_
  108.2 0.5 collective-permute-done.23.refs_6_
  108.7 0.9 finish.6.refs_7_
  109.6 0.5 collective-permute-done.13.refs_6_
  110.2 0.9 finish.7
  (68 shorter events, 3.3 us)
Async XLA Ops:
  0.0 19.6 %copy-start.3 = (bf16[8,8]{1,0:T(8,128)(2,1)S(1)}, bf16[8,8]{1,0:T(8,128)(2,1)}, u32[]{:S(2)}) copy-start(bf16[8,8]{1,0:T(8,128)(2,1)} %param.6) | copy-start | bytes 388
  0.7 1.1 copy-start.1
  1.8 27.1 %copy-start.2 = (bf16[512,1,640]{2,0,1:T(8,128)(2,1)S(1)}, bf16[512,1,640]{2,0,1:T(8,128)(2,1)}, u32[]{:S(2)}) copy-start(bf16[512,1,640]{2,0,1:T(8,128)(2,1)} %param.4) | copy-start | bytes 1966084
  1.9 16.0 %collective-permute-start = (bf16[512,256]{1,0:T(8,128)(2,1)S(1)}, bf16[512,256]{1,0:T(8,128)(2,1)S(1)}, u32[]{:S(2)}, u32[]{:S(2)}) collective-permute-start(bf16[512,256]{1,0:T(8,128)(2,1)S(1)} %get-tuple-element.40.refs_1_), channel_id=1, source_target_pairs={{0,16},{4,20},{8,24},{12,28},{16,0},{20,4},{24,8},{28,12},{1,17},{... | collective-permute-start | bytes 786440 | tf_op jit(solution)/shard_map/ppermute | solution.py:228
  6.0 12.0 %collective-permute-start.34 = (bf16[512,256]{1,0:T(8,128)(2,1)S(1)}, bf16[512,256]{1,0:T(8,128)(2,1)S(1)}, u32[]{:S(2)}, u32[]{:S(2)}) collective-permute-start(bf16[512,256]{1,0:T(8,128)(2,1)S(1)} %get-tuple-element.40.refs_1_), channel_id=1, source_target_pairs={{0,4},{4,0},{8,12},{12,8},{16,20},{20,16},{24,28},{28,24},{1,5},{5... | collective-permute-start | bytes 786440 | tf_op jit(solution)/shard_map/ppermute | solution.py:228
  18.0 22.7 %copy-start = (bf16[2048,1,512]{2,0,1:T(8,128)(2,1)S(1)}, bf16[2048,1,512]{2,0,1:T(8,128)(2,1)}, u32[]{:S(2)}) copy-start(bf16[2048,1,512]{2,0,1:T(8,128)(2,1)} %param.7) | copy-start | bytes 6291460
  18.0 7.6 %collective-permute-start.35 = (bf16[512,256]{1,0:T(8,128)(2,1)S(1)}, bf16[512,256]{1,0:T(8,128)(2,1)S(1)}, u32[]{:S(2)}, u32[]{:S(2)}) collective-permute-start(bf16[512,256]{1,0:T(8,128)(2,1)S(1)} %get-tuple-element.65.refs_2_), channel_id=1, source_target_pairs={{0,4},{4,0},{8,12},{12,8},{16,20},{20,16},{24,28},{28,24},{1,5},{5... | collective-permute-start | bytes 786440 | tf_op jit(solution)/shard_map/ppermute | solution.py:228
  19.6 9.2 %collective-permute-start.1 = (bf16[512,128]{1,0:T(8,128)(2,1)S(1)}, bf16[512,128]{1,0:T(8,128)(2,1)S(1)}, u32[]{:S(2)}, u32[]{:S(2)}) collective-permute-start(bf16[512,128]{1,0:T(8,128)(2,1)S(1)} %mask_chunk.3.refs_1_), channel_id=1, source_target_pairs={{0,16},{4,20},{8,24},{12,28},{16,0},{20,4},{24,8},{28,12},{1,17},{... | collective-permute-start | bytes 393224 | tf_op jit(solution)/shard_map/ppermute | solution.py:228
  25.8 14.9 %collective-permute-start.36 = (bf16[1,512,256]{2,1,0:T(8,128)(2,1)S(1)}, bf16[1,512,256]{2,1,0:T(8,128)(2,1)S(1)}, u32[]{:S(2)}, u32[]{:S(2)}) collective-permute-start(bf16[1,512,256]{2,1,0:T(8,128)(2,1)S(1)} %mix.14), channel_id=1, source_target_pairs={{0,8},{4,12},{8,0},{12,4},{16,24},{20,28},{24,16},{28,20},{1,9},{5... | collective-permute-start | bytes 786440 | tf_op jit(solution)/shard_map/ppermute | solution.py:228
  27.3 5.6 %collective-permute-start.24 = (bf16[512,128]{1,0:T(8,128)(2,1)S(1)}, bf16[512,128]{1,0:T(8,128)(2,1)S(1)}, u32[]{:S(2)}, u32[]{:S(2)}) collective-permute-start(bf16[512,128]{1,0:T(8,128)(2,1)S(1)} %mask_chunk.3.refs_1_), channel_id=1, source_target_pairs={{0,4},{4,0},{8,12},{12,8},{16,20},{20,16},{24,28},{28,24},{1,5},{5... | collective-permute-start | bytes 393224 | tf_op jit(solution)/shard_map/ppermute | solution.py:228
  28.9 7.5 %collective-permute-start.2 = (bf16[512,128]{1,0:T(8,128)(2,1)S(1)}, bf16[512,128]{1,0:T(8,128)(2,1)S(1)}, u32[]{:S(2)}, u32[]{:S(2)}) collective-permute-start(bf16[512,128]{1,0:T(8,128)(2,1)S(1)} %mask_chunk.4.refs_1_), channel_id=1, source_target_pairs={{0,16},{4,20},{8,24},{12,28},{16,0},{20,4},{24,8},{28,12},{1,17},{... | collective-permute-start | bytes 393224 | tf_op jit(solution)/shard_map/ppermute | solution.py:228
  32.4 7.7 %collective-permute-start.14 = (bf16[512,128]{1,0:T(8,128)(2,1)S(1)}, bf16[512,128]{1,0:T(8,128)(2,1)S(1)}, u32[]{:S(2)}, u32[]{:S(2)}) collective-permute-start(bf16[512,128]{1,0:T(8,128)(2,1)S(1)} %mask_chunk.4.refs_1_), channel_id=1, source_target_pairs={{0,4},{4,0},{8,12},{12,8},{16,20},{20,16},{24,28},{28,24},{1,5},{5... | collective-permute-start | bytes 393224 | tf_op jit(solution)/shard_map/ppermute | solution.py:228
  32.9 10.0 %collective-permute-start.25 = (bf16[512,128]{1,0:T(8,128)(2,1)S(1)}, bf16[512,128]{1,0:T(8,128)(2,1)S(1)}, u32[]{:S(2)}, u32[]{:S(2)}) collective-permute-start(bf16[512,128]{1,0:T(8,128)(2,1)S(1)} %get-tuple-element.57.refs_2_), channel_id=1, source_target_pairs={{0,4},{4,0},{8,12},{12,8},{16,20},{20,16},{24,28},{28,24},{1,5},{5... | collective-permute-start | bytes 393224 | tf_op jit(solution)/shard_map/ppermute | solution.py:228
  36.5 8.0 %collective-permute-start.3 = (bf16[512,128]{1,0:T(8,128)(2,1)S(1)}, bf16[512,128]{1,0:T(8,128)(2,1)S(1)}, u32[]{:S(2)}, u32[]{:S(2)}) collective-permute-start(bf16[512,128]{1,0:T(8,128)(2,1)S(1)} %mask_chunk.5.refs_1_), channel_id=1, source_target_pairs={{0,16},{4,20},{8,24},{12,28},{16,0},{20,4},{24,8},{28,12},{1,17},{... | collective-permute-start | bytes 393224 | tf_op jit(solution)/shard_map/ppermute | solution.py:228
  38.7 6.2 %collective-permute-start.4 = (bf16[512,128]{1,0:T(8,128)(2,1)S(1)}, bf16[512,128]{1,0:T(8,128)(2,1)S(1)}, u32[]{:S(2)}, u32[]{:S(2)}) collective-permute-start(bf16[512,128]{1,0:T(8,128)(2,1)S(1)} %mask_chunk.5.refs_1_), channel_id=1, source_target_pairs={{0,4},{4,0},{8,12},{12,8},{16,20},{20,16},{24,28},{28,24},{1,5},{5... | collective-permute-start | bytes 393224 | tf_op jit(solution)/shard_map/ppermute | solution.py:228
  40.1 7.2 %collective-permute-start.15 = (bf16[512,128]{1,0:T(8,128)(2,1)S(1)}, bf16[512,128]{1,0:T(8,128)(2,1)S(1)}, u32[]{:S(2)}, u32[]{:S(2)}) collective-permute-start(bf16[512,128]{1,0:T(8,128)(2,1)S(1)} %get-tuple-element.49.refs_2_), channel_id=1, source_target_pairs={{0,4},{4,0},{8,12},{12,8},{16,20},{20,16},{24,28},{28,24},{1,5},{5... | collective-permute-start | bytes 393224 | tf_op jit(solution)/shard_map/ppermute | solution.py:228
  42.8 12.3 %collective-permute-start.37 = (bf16[512,256]{1,0:T(8,128)(2,1)S(1)}, bf16[512,256]{1,0:T(8,128)(2,1)S(1)}, u32[]{:S(2)}, u32[]{:S(2)}) collective-permute-start(bf16[512,256]{1,0:T(8,128)(2,1)S(1)} %get-tuple-element.68), channel_id=1, source_target_pairs={{0,1},{1,0},{2,3},{3,2},{4,5},{5,4},{6,7},{7,6},{8,9},{9,8},{10,11... | collective-permute-start | bytes 786440 | tf_op jit(solution)/shard_map/ppermute | solution.py:228
  42.9 12.6 %collective-permute-start.38 = (bf16[512,256]{1,0:T(8,128)(2,1)S(1)}, bf16[512,256]{1,0:T(8,128)(2,1)S(1)}, u32[]{:S(2)}, u32[]{:S(2)}) collective-permute-start(bf16[512,256]{1,0:T(8,128)(2,1)S(1)} %get-tuple-element.69), channel_id=1, source_target_pairs={{0,2},{1,3},{2,0},{3,1},{4,6},{5,7},{6,4},{7,5},{8,10},{9,11},{10,... | collective-permute-start | bytes 786440 | tf_op jit(solution)/shard_map/ppermute | solution.py:228
  44.5 12.3 %collective-permute-start.39 = (bf16[512,256]{1,0:T(8,128)(2,1)S(1)}, bf16[512,256]{1,0:T(8,128)(2,1)S(1)}, u32[]{:S(2)}, u32[]{:S(2)}) collective-permute-start(bf16[512,256]{1,0:T(8,128)(2,1)S(1)} %get-tuple-element.70), channel_id=1, source_target_pairs={{0,3},{1,2},{2,1},{3,0},{4,7},{5,6},{6,5},{7,4},{8,11},{9,10},{10,... | collective-permute-start | bytes 786440 | tf_op jit(solution)/shard_map/ppermute | solution.py:228
  44.9 6.3 %collective-permute-start.26 = (bf16[1,512,128]{2,1,0:T(8,128)(2,1)S(1)}, bf16[1,512,128]{2,1,0:T(8,128)(2,1)S(1)}, u32[]{:S(2)}, u32[]{:S(2)}) collective-permute-start(bf16[1,512,128]{2,1,0:T(8,128)(2,1)S(1)} %mix.12), channel_id=1, source_target_pairs={{0,8},{4,12},{8,0},{12,4},{16,24},{20,28},{24,16},{28,20},{1,9},{5... | collective-permute-start | bytes 393224 | tf_op jit(solution)/shard_map/ppermute | solution.py:228
  47.2 7.6 %collective-permute-start.5 = (bf16[512,128]{1,0:T(8,128)(2,1)S(1)}, bf16[512,128]{1,0:T(8,128)(2,1)S(1)}, u32[]{:S(2)}, u32[]{:S(2)}) collective-permute-start(bf16[512,128]{1,0:T(8,128)(2,1)S(1)} %get-tuple-element.41.refs_2_), channel_id=1, source_target_pairs={{0,4},{4,0},{8,12},{12,8},{16,20},{20,16},{24,28},{28,24},{1,5},{5... | collective-permute-start | bytes 393224 | tf_op jit(solution)/shard_map/ppermute | solution.py:228
  51.2 7.4 %collective-permute-start.16 = (bf16[1,512,128]{2,1,0:T(8,128)(2,1)S(1)}, bf16[1,512,128]{2,1,0:T(8,128)(2,1)S(1)}, u32[]{:S(2)}, u32[]{:S(2)}) collective-permute-start(bf16[1,512,128]{2,1,0:T(8,128)(2,1)S(1)} %mix.10), channel_id=1, source_target_pairs={{0,8},{4,12},{8,0},{12,4},{16,24},{20,28},{24,16},{28,20},{1,9},{5... | collective-permute-start | bytes 393224 | tf_op jit(solution)/shard_map/ppermute | solution.py:228
  54.8 7.2 %collective-permute-start.27 = (bf16[512,128]{1,0:T(8,128)(2,1)S(1)}, bf16[512,128]{1,0:T(8,128)(2,1)S(1)}, u32[]{:S(2)}, u32[]{:S(2)}) collective-permute-start(bf16[512,128]{1,0:T(8,128)(2,1)S(1)} %get-tuple-element.60), channel_id=1, source_target_pairs={{0,1},{1,0},{2,3},{3,2},{4,5},{5,4},{6,7},{7,6},{8,9},{9,8},{10,11... | collective-permute-start | bytes 393224 | tf_op jit(solution)/shard_map/ppermute | solution.py:228
  55.1 8.0 %collective-permute-start.6 = (bf16[1,512,128]{2,1,0:T(8,128)(2,1)S(1)}, bf16[1,512,128]{2,1,0:T(8,128)(2,1)S(1)}, u32[]{:S(2)}, u32[]{:S(2)}) collective-permute-start(bf16[1,512,128]{2,1,0:T(8,128)(2,1)S(1)} %mix.8), channel_id=1, source_target_pairs={{0,8},{4,12},{8,0},{12,4},{16,24},{20,28},{24,16},{28,20},{1,9},{5... | collective-permute-start | bytes 393224 | tf_op jit(solution)/shard_map/ppermute | solution.py:228
  56.9 15.1 %collective-permute-start.40 = (bf16[512,256]{1,0:T(8,128)(2,1)S(1)}, bf16[512,256]{1,0:T(8,128)(2,1)S(1)}, u32[]{:S(2)}, u32[]{:S(2)}) collective-permute-start(bf16[512,256]{1,0:T(8,128)(2,1)S(1)} %add_up.7.refs_1_.refs_2_), channel_id=1, source_target_pairs={{0,16},{4,20},{8,24},{12,28},{16,0},{20,4},{24,8},{28,12},{1,17},{... | collective-permute-start | bytes 786440 | tf_op jit(solution)/shard_map/ppermute | solution.py:228
  57.8 15.8 %collective-permute-start.41 = (bf16[512,256]{1,0:T(8,128)(2,1)S(1)}, bf16[512,256]{1,0:T(8,128)(2,1)S(1)}, u32[]{:S(2)}, u32[]{:S(2)}) collective-permute-start(bf16[512,256]{1,0:T(8,128)(2,1)S(1)} %add_up.7.refs_1_.refs_2_), channel_id=1, source_target_pairs={{0,4},{4,0},{8,12},{12,8},{16,20},{20,16},{24,28},{28,24},{1,5},{5... | collective-permute-start | bytes 786440 | tf_op jit(solution)/shard_map/ppermute | solution.py:228
  58.6 6.3 %collective-permute-start.28 = (bf16[512,128]{1,0:T(8,128)(2,1)S(1)}, bf16[512,128]{1,0:T(8,128)(2,1)S(1)}, u32[]{:S(2)}, u32[]{:S(2)}) collective-permute-start(bf16[512,128]{1,0:T(8,128)(2,1)S(1)} %get-tuple-element.61), channel_id=1, source_target_pairs={{0,2},{1,3},{2,0},{3,1},{4,6},{5,7},{6,4},{7,5},{8,10},{9,11},{10,... | collective-permute-start | bytes 393224 | tf_op jit(solution)/shard_map/ppermute | solution.py:228
  62.1 5.6 %collective-permute-start.29 = (bf16[512,128]{1,0:T(8,128)(2,1)S(1)}, bf16[512,128]{1,0:T(8,128)(2,1)S(1)}, u32[]{:S(2)}, u32[]{:S(2)}) collective-permute-start(bf16[512,128]{1,0:T(8,128)(2,1)S(1)} %get-tuple-element.62), channel_id=1, source_target_pairs={{0,3},{1,2},{2,1},{3,0},{4,7},{5,6},{6,5},{7,4},{8,11},{9,10},{10,... | collective-permute-start | bytes 393224 | tf_op jit(solution)/shard_map/ppermute | solution.py:228
  63.1 5.1 %collective-permute-start.17 = (bf16[512,128]{1,0:T(8,128)(2,1)S(1)}, bf16[512,128]{1,0:T(8,128)(2,1)S(1)}, u32[]{:S(2)}, u32[]{:S(2)}) collective-permute-start(bf16[512,128]{1,0:T(8,128)(2,1)S(1)} %get-tuple-element.52), channel_id=1, source_target_pairs={{0,1},{1,0},{2,3},{3,2},{4,5},{5,4},{6,7},{7,6},{8,9},{9,8},{10,11... | collective-permute-start | bytes 393224 | tf_op jit(solution)/shard_map/ppermute | solution.py:228
  65.0 8.7 %collective-permute-start.18 = (bf16[512,128]{1,0:T(8,128)(2,1)S(1)}, bf16[512,128]{1,0:T(8,128)(2,1)S(1)}, u32[]{:S(2)}, u32[]{:S(2)}) collective-permute-start(bf16[512,128]{1,0:T(8,128)(2,1)S(1)} %get-tuple-element.53), channel_id=1, source_target_pairs={{0,2},{1,3},{2,0},{3,1},{4,6},{5,7},{6,4},{7,5},{8,10},{9,11},{10,... | collective-permute-start | bytes 393224 | tf_op jit(solution)/shard_map/ppermute | solution.py:228
  67.7 7.4 %collective-permute-start.19 = (bf16[512,128]{1,0:T(8,128)(2,1)S(1)}, bf16[512,128]{1,0:T(8,128)(2,1)S(1)}, u32[]{:S(2)}, u32[]{:S(2)}) collective-permute-start(bf16[512,128]{1,0:T(8,128)(2,1)S(1)} %get-tuple-element.54), channel_id=1, source_target_pairs={{0,3},{1,2},{2,1},{3,0},{4,7},{5,6},{6,5},{7,4},{8,11},{9,10},{10,... | collective-permute-start | bytes 393224 | tf_op jit(solution)/shard_map/ppermute | solution.py:228
  68.2 7.9 %collective-permute-start.7 = (bf16[512,128]{1,0:T(8,128)(2,1)S(1)}, bf16[512,128]{1,0:T(8,128)(2,1)S(1)}, u32[]{:S(2)}, u32[]{:S(2)}) collective-permute-start(bf16[512,128]{1,0:T(8,128)(2,1)S(1)} %get-tuple-element.44), channel_id=1, source_target_pairs={{0,1},{1,0},{2,3},{3,2},{4,5},{5,4},{6,7},{7,6},{8,9},{9,8},{10,11... | collective-permute-start | bytes 393224 | tf_op jit(solution)/shard_map/ppermute | solution.py:228
  72.1 5.4 %collective-permute-start.8 = (bf16[512,128]{1,0:T(8,128)(2,1)S(1)}, bf16[512,128]{1,0:T(8,128)(2,1)S(1)}, u32[]{:S(2)}, u32[]{:S(2)}) collective-permute-start(bf16[512,128]{1,0:T(8,128)(2,1)S(1)} %get-tuple-element.45), channel_id=1, source_target_pairs={{0,2},{1,3},{2,0},{3,1},{4,6},{5,7},{6,4},{7,5},{8,10},{9,11},{10,... | collective-permute-start | bytes 393224 | tf_op jit(solution)/shard_map/ppermute | solution.py:228
  73.6 5.8 %collective-permute-start.9 = (bf16[512,128]{1,0:T(8,128)(2,1)S(1)}, bf16[512,128]{1,0:T(8,128)(2,1)S(1)}, u32[]{:S(2)}, u32[]{:S(2)}) collective-permute-start(bf16[512,128]{1,0:T(8,128)(2,1)S(1)} %get-tuple-element.46), channel_id=1, source_target_pairs={{0,3},{1,2},{2,1},{3,0},{4,7},{5,6},{6,5},{7,4},{8,11},{9,10},{10,... | collective-permute-start | bytes 393224 | tf_op jit(solution)/shard_map/ppermute | solution.py:228
  73.7 21.6 %collective-permute-start.42 = (bf16[512,256]{1,0:T(8,128)(2,1)S(1)}, bf16[512,256]{1,0:T(8,128)(2,1)S(1)}, u32[]{:S(2)}, u32[]{:S(2)}) collective-permute-start(bf16[512,256]{1,0:T(8,128)(2,1)S(1)} %get-tuple-element.71.refs_2_.refs_3_), channel_id=1, source_target_pairs={{0,4},{4,0},{8,12},{12,8},{16,20},{20,16},{24,28},{28,24},{1,5},{5... | collective-permute-start | bytes 786440 | tf_op jit(solution)/shard_map/ppermute | solution.py:228
  75.1 12.8 %collective-permute-start.30 = (bf16[512,128]{1,0:T(8,128)(2,1)S(1)}, bf16[512,128]{1,0:T(8,128)(2,1)S(1)}, u32[]{:S(2)}, u32[]{:S(2)}) collective-permute-start(bf16[512,128]{1,0:T(8,128)(2,1)S(1)} %add_up.6.refs_1_.refs_2_), channel_id=1, source_target_pairs={{0,16},{4,20},{8,24},{12,28},{16,0},{20,4},{24,8},{28,12},{1,17},{... | collective-permute-start | bytes 393224 | tf_op jit(solution)/shard_map/ppermute | solution.py:228
  76.0 11.9 %collective-permute-start.31 = (bf16[512,128]{1,0:T(8,128)(2,1)S(1)}, bf16[512,128]{1,0:T(8,128)(2,1)S(1)}, u32[]{:S(2)}, u32[]{:S(2)}) collective-permute-start(bf16[512,128]{1,0:T(8,128)(2,1)S(1)} %add_up.6.refs_1_.refs_2_), channel_id=1, source_target_pairs={{0,4},{4,0},{8,12},{12,8},{16,20},{20,16},{24,28},{28,24},{1,5},{5... | collective-permute-start | bytes 393224 | tf_op jit(solution)/shard_map/ppermute | solution.py:228
  77.5 15.7 %collective-permute-start.20 = (bf16[512,128]{1,0:T(8,128)(2,1)S(1)}, bf16[512,128]{1,0:T(8,128)(2,1)S(1)}, u32[]{:S(2)}, u32[]{:S(2)}) collective-permute-start(bf16[512,128]{1,0:T(8,128)(2,1)S(1)} %add_up.5.refs_1_.refs_2_), channel_id=1, source_target_pairs={{0,16},{4,20},{8,24},{12,28},{16,0},{20,4},{24,8},{28,12},{1,17},{... | collective-permute-start | bytes 393224 | tf_op jit(solution)/shard_map/ppermute | solution.py:228
  79.4 14.6 %collective-permute-start.21 = (bf16[512,128]{1,0:T(8,128)(2,1)S(1)}, bf16[512,128]{1,0:T(8,128)(2,1)S(1)}, u32[]{:S(2)}, u32[]{:S(2)}) collective-permute-start(bf16[512,128]{1,0:T(8,128)(2,1)S(1)} %add_up.5.refs_1_.refs_2_), channel_id=1, source_target_pairs={{0,4},{4,0},{8,12},{12,8},{16,20},{20,16},{24,28},{28,24},{1,5},{5... | collective-permute-start | bytes 393224 | tf_op jit(solution)/shard_map/ppermute | solution.py:228
  88.0 7.9 %collective-permute-start.10 = (bf16[512,128]{1,0:T(8,128)(2,1)S(1)}, bf16[512,128]{1,0:T(8,128)(2,1)S(1)}, u32[]{:S(2)}, u32[]{:S(2)}) collective-permute-start(bf16[512,128]{1,0:T(8,128)(2,1)S(1)} %add_up.4.refs_1_.refs_2_), channel_id=1, source_target_pairs={{0,16},{4,20},{8,24},{12,28},{16,0},{20,4},{24,8},{28,12},{1,17},{... | collective-permute-start | bytes 393224 | tf_op jit(solution)/shard_map/ppermute | solution.py:228
  88.0 7.9 %collective-permute-start.11 = (bf16[512,128]{1,0:T(8,128)(2,1)S(1)}, bf16[512,128]{1,0:T(8,128)(2,1)S(1)}, u32[]{:S(2)}, u32[]{:S(2)}) collective-permute-start(bf16[512,128]{1,0:T(8,128)(2,1)S(1)} %add_up.4.refs_1_.refs_2_), channel_id=1, source_target_pairs={{0,4},{4,0},{8,12},{12,8},{16,20},{20,16},{24,28},{28,24},{1,5},{5... | collective-permute-start | bytes 393224 | tf_op jit(solution)/shard_map/ppermute | solution.py:228
  93.2 5.0 %collective-permute-start.32 = (bf16[512,128]{1,0:T(8,128)(2,1)S(1)}, bf16[512,128]{1,0:T(8,128)(2,1)S(1)}, u32[]{:S(2)}, u32[]{:S(2)}) collective-permute-start(bf16[512,128]{1,0:T(8,128)(2,1)S(1)} %get-tuple-element.63.refs_2_.refs_3_), channel_id=1, source_target_pairs={{0,4},{4,0},{8,12},{12,8},{16,20},{20,16},{24,28},{28,24},{1,5},{5... | collective-permute-start | bytes 393224 | tf_op jit(solution)/shard_map/ppermute | solution.py:228
  93.9 6.9 %collective-permute-start.22 = (bf16[512,128]{1,0:T(8,128)(2,1)S(1)}, bf16[512,128]{1,0:T(8,128)(2,1)S(1)}, u32[]{:S(2)}, u32[]{:S(2)}) collective-permute-start(bf16[512,128]{1,0:T(8,128)(2,1)S(1)} %get-tuple-element.55.refs_2_.refs_3_), channel_id=1, source_target_pairs={{0,4},{4,0},{8,12},{12,8},{16,20},{20,16},{24,28},{28,24},{1,5},{5... | collective-permute-start | bytes 393224 | tf_op jit(solution)/shard_map/ppermute | solution.py:228
  95.5 9.2 %collective-permute-start.43 = (bf16[1,512,256]{2,1,0:T(8,128)(2,1)S(1)}, bf16[1,512,256]{2,1,0:T(8,128)(2,1)S(1)}, u32[]{:S(2)}, u32[]{:S(2)}) collective-permute-start(bf16[1,512,256]{2,1,0:T(8,128)(2,1)S(1)} %mix.15), channel_id=1, source_target_pairs={{0,8},{4,12},{8,0},{12,4},{16,24},{20,28},{24,16},{28,20},{1,9},{5... | collective-permute-start | bytes 786440 | tf_op jit(solution)/shard_map/ppermute | solution.py:228
  95.9 6.5 %collective-permute-start.12 = (bf16[512,128]{1,0:T(8,128)(2,1)S(1)}, bf16[512,128]{1,0:T(8,128)(2,1)S(1)}, u32[]{:S(2)}, u32[]{:S(2)}) collective-permute-start(bf16[512,128]{1,0:T(8,128)(2,1)S(1)} %get-tuple-element.47.refs_2_.refs_3_), channel_id=1, source_target_pairs={{0,4},{4,0},{8,12},{12,8},{16,20},{20,16},{24,28},{28,24},{1,5},{5... | collective-permute-start | bytes 393224 | tf_op jit(solution)/shard_map/ppermute | solution.py:228
  98.4 9.0 %collective-permute-start.33 = (bf16[1,512,128]{2,1,0:T(8,128)(2,1)S(1)}, bf16[1,512,128]{2,1,0:T(8,128)(2,1)S(1)}, u32[]{:S(2)}, u32[]{:S(2)}) collective-permute-start(bf16[1,512,128]{2,1,0:T(8,128)(2,1)S(1)} %mix.13), channel_id=1, source_target_pairs={{0,8},{4,12},{8,0},{12,4},{16,24},{20,28},{24,16},{28,20},{1,9},{5... | collective-permute-start | bytes 393224 | tf_op jit(solution)/shard_map/ppermute | solution.py:228
  101.0 7.7 %collective-permute-start.23 = (bf16[1,512,128]{2,1,0:T(8,128)(2,1)S(1)}, bf16[1,512,128]{2,1,0:T(8,128)(2,1)S(1)}, u32[]{:S(2)}, u32[]{:S(2)}) collective-permute-start(bf16[1,512,128]{2,1,0:T(8,128)(2,1)S(1)} %mix.11), channel_id=1, source_target_pairs={{0,8},{4,12},{8,0},{12,4},{16,24},{20,28},{24,16},{28,20},{1,9},{5... | collective-permute-start | bytes 393224 | tf_op jit(solution)/shard_map/ppermute | solution.py:228
  102.6 7.6 %collective-permute-start.13 = (bf16[1,512,128]{2,1,0:T(8,128)(2,1)S(1)}, bf16[1,512,128]{2,1,0:T(8,128)(2,1)S(1)}, u32[]{:S(2)}, u32[]{:S(2)}) collective-permute-start(bf16[1,512,128]{2,1,0:T(8,128)(2,1)S(1)} %mix.9), channel_id=1, source_target_pairs={{0,8},{4,12},{8,0},{12,4},{16,24},{20,28},{24,16},{28,20},{1,9},{5... | collective-permute-start | bytes 393224 | tf_op jit(solution)/shard_map/ppermute | solution.py:228

commit v6 on v5

--- a/solution.py
+++ b/solution.py
@@ -11,9 +11,9 @@
 F32 = jnp.float32
 BF16 = jnp.bfloat16
 SLAB = 64
-MATMUL_ROWS = 256
+MATMUL_ROWS = 512
 VMEM_LIMIT = 16 * 1024 * 1024
-LINK_SHARE = {'far': 0.0312, 'near': 0.0282, 'partial': 0.0371, 'core': 0.0223, 'row': 0.0375}
+LINK_SHARE = {'far': 0.0311, 'near': 0.0421, 'partial': 0.0537, 'row': 0.0541}
 LATENCY = 1.156
 
 smem = pl.BlockSpec(memory_space=pltpu.SMEM)
@@ -48,13 +48,8 @@
             scratch_shapes=list(scratch),
             input_output_aliases=aliases or {},
             compiler_params=pltpu.CompilerParams(vmem_limit_bytes=VMEM_LIMIT),
-            cost_estimate=pl.CostEstimate(flops=0, transcendentals=0, bytes_accessed=0),
+            cost_estimate=pl.CostEstimate(flops=0, transcendentals=0, bytes_accessed=sum(a.size * 2 for a in [*arrays, *out_shape])),
         )(*scalars, *arrays, *whole, *after)
-
-    def pin(self, *arrays):
-        return self.call(
-            lambda *refs: None, "pin", [like(a) for a in arrays], [], out_specs=[unread] * len(arrays), whole=arrays,
-            aliases={i: i for i in range(len(arrays))})
 
 
 def like(array):
@@ -81,16 +76,18 @@
 def mask_first(chain, block_rows, own, lo, width):
     rows = own.shape[0]
 
-    def kernel(length_ref, own_ref, out_ref, left_ref):
+    def kernel(length_ref, own_ref, out_ref, left_ref, whole_ref):
         left = length_ref[0] - lax.axis_index("row") * rows
         left_ref[...] = jnp.full(left_ref.shape, left, jnp.int32)
 
         def body(at):
-            out_ref[at, :] = masked(own_ref[at, lo:lo + width].astype(F32), at, left)
-
-        slabs(rows, body)
-
-    outs = [jax.ShapeDtypeStruct((rows, width), BF16), jax.ShapeDtypeStruct((8, 256), jnp.int32)]
+            kept = masked(own_ref[at, :].astype(F32), at, left)
+            whole_ref[at, :] = kept
+            out_ref[at, :] = kept[:, lo:lo + width]
+
+        slabs(rows, body)
+
+    outs = [jax.ShapeDtypeStruct((rows, width), BF16), jax.ShapeDtypeStruct((8, 256), jnp.int32), like(own)]
     return chain.call(kernel, "mask_first", outs, [own], [block_rows])
 
 
@@ -109,19 +106,21 @@
 def coefficients(chain, matrix, n_chan, entries, width):
     count = -(-len(entries) // 8) * 8
 
-    def kernel(matrix_ref, table_ref):
+    def kernel(matrix_ref, in_ref, out_ref):
         c = lax.axis_index("chan")
         for i, (t, m) in enumerate(entries):
-            table_ref[i:i + 1, :] = jnp.full((1, width), matrix_ref[c ^ t, c ^ m], F32)
-
-    return chain.call(kernel, "coefficients", [jax.ShapeDtypeStruct((count, width), F32)], [], [matrix])[0]
+            in_ref[i:i + 1, :] = jnp.full((1, width), matrix_ref[c ^ t, c ^ m], F32)
+            out_ref[i:i + 1, :] = jnp.full((1, width), matrix_ref[c ^ m, c ^ t], F32)
+
+    return chain.call(kernel, "coefficients", [jax.ShapeDtypeStruct((count, width), F32)] * 2, [], [matrix])
 
 
 def mixed(table_ref, entries, held, at, target):
     total = None
     for source, ref in held:
         entry = entries.index((target, source))
-        term = ref[at, :].astype(F32) * table_ref[entry:entry + 1, :ref.shape[1]]
+        term = ref[at, :] if not isinstance(ref, tuple) else ref[0][at, ref[1]:ref[1] + ref[2]]
+        term = term.astype(F32) * table_ref[entry:entry + 1, :term.shape[1]]
         total = term if total is None else total + term
     return total
 
@@ -130,7 +129,7 @@
     rows, width = held[0][1].shape
 
     def kernel(table_ref, *refs):
-        held_refs = [(m, ref) for (m, _), ref in zip(held, refs)]
+        held_refs = [(m, (ref, b[1], width) if isinstance(b, tuple) else ref) for (m, b), ref in zip(held, refs)]
         received_refs = refs[len(held):-1]
         out_ref = refs[-1]
 
@@ -144,7 +143,7 @@
 
         slabs(rows, body)
 
-    arrays = [table] + [b for _, b in held] + [r for r, _ in received]
+    arrays = [table] + [b[0] if isinstance(b, tuple) else b for _, b in held] + [r for r, _ in received]
     return chain.call(kernel, "mix", [stacked(len(targets), rows, width)], arrays)[0]
 
 
@@ -153,7 +152,7 @@
     group = weights.shape[0] // n_row
 
     def kernel(table_ref, *refs):
-        held_refs = [(m, ref) for (m, _), ref in zip(held, refs)]
+        held_refs = [(m, (ref, b[1], width) if isinstance(b, tuple) else ref) for (m, b), ref in zip(held, refs)]
         received_refs = refs[len(held):len(held) + len(received)]
         weights_ref, *out_refs, cross_ref = refs[len(held) + len(received):]
         g = lax.axis_index("row")
@@ -174,7 +173,7 @@
 
             slabs(group, rows_of, MATMUL_ROWS)
 
-    arrays = [table] + [b for _, b in held] + received + [weights]
+    arrays = [table] + [b[0] if isinstance(b, tuple) else b for _, b in held] + received + [weights]
     outs = [jax.ShapeDtypeStruct((group, width), BF16)] * n_row
     return chain.call(kernel, "mix_multiply", outs, arrays, scratch=[pltpu.VMEM((rows, width), BF16)])
 
@@ -194,7 +193,7 @@
     rows, width = held[0][1].shape
 
     def kernel(table_ref, left_ref, *refs):
-        held_refs = [(m, ref) for (m, _), ref in zip(held, refs)]
+        held_refs = [(m, (ref, b[1], width) if isinstance(b, tuple) else ref) for (m, b), ref in zip(held, refs)]
         received_refs = refs[len(held):len(held) + len(received)]
         out_ref, chunk_ref, done = refs[-3:]
 
@@ -209,7 +208,7 @@
         copy.start()
         copy.wait()
 
-    arrays = [table, left] + [b for _, b in held] + received
+    arrays = [table, left] + [b[0] if isinstance(b, tuple) else b for _, b in held] + received
     whole = [] if result is None else [result]
     return chain.call(
         kernel, "finish", [jax.ShapeDtypeStruct((rows, columns), BF16)], arrays,
@@ -245,20 +244,21 @@
         entries = [(t, m) for t in span(reduce_bits) for m in (0, far, near, far ^ near)]
         matrix = recoupling.astype(F32)
         chain = Chain()
-        tables, result, left, last_far = {}, None, None, None
+        tables, result, left, last_far, whole_beside = [], None, None, None, None
 
         def table(transposed):
-            if transposed not in tables:
-                tables[transposed] = coefficients(chain, matrix.T if transposed else matrix, n_chan, entries, lanes)
+            if not tables:
+                tables.extend(coefficients(chain, matrix, n_chan, entries, lanes))
             return tables[transposed]
 
-        def mixing(block, transposed, note_far=None):
+        def mixing(block, transposed, beside=None):
+            nonlocal last_far
             other = swap(block, "chan", n_chan, far)
-            beside = swap(block, "chan", n_chan, near)
-            if note_far:
-                note_far(other)
+            if transposed:
+                beside = swap(block, "chan", n_chan, near)
+            else:
+                last_far = other
             yield "far"
-            other, beside = chain.pin(other, beside)
             corner = swap(other, "chan", n_chan, near)
             held = [(0, block), (far, other), (near, beside), (far ^ near, corner)]
             targets, received = span(reduce_bits), []
@@ -271,17 +271,13 @@
             return held, [r for r, _ in received]
 
         def one_chunk(lo, width):
-            nonlocal result, left, last_far
-
-            def note_far(array):
-                nonlocal last_far
-                last_far = array
-
+            nonlocal result, left, whole_beside
             if left is None:
-                block, left = mask_first(chain, block_rows, own, lo, width)
+                block, left, whole_block = mask_first(chain, block_rows, own, lo, width)
+                whole_beside = swap(whole_block, "chan", n_chan, near)
             else:
                 block = mask_chunk(chain, left, own, lo, width, [last_far])
-            held, received = yield from mixing(block, False, note_far)
+            held, received = yield from mixing(block, False, (whole_beside, lo))
             parts = mix_multiply(chain, table(False), entries, held, received, weights, n_row)
             got = [swap(parts[d], "row", n_row, d) for d in range(1, n_row)]
             yield "row"

time: 111 us -> 109 us (0.982)
  starting transfers between devices: 44.8 us -> 52.2 us
  waiting for transfers between devices: 49.3 us -> 43.8 us
  Pallas kernels: 14.7 us -> 10 us
    ppermute x44 -> x41, starting transfers between devices: 44.8 us -> 52.2 us  [swap(): return lax.ppermute(x, axis, [(i, i ^ bit) for i in range(size)])]
    ppermute x44 -> x41, waiting for transfers between devices: 49.3 us -> 43.8 us  [swap(): return lax.ppermute(x, axis, [(i, i ^ bit) for i in range(size)])]
    pallas_call x34 -> x25, Pallas kernels: 14.7 us -> 10 us  [call(): pl.pallas_call(body, name=name, out_shape=list(out_shape), in_specs=[smem...]
  transfers between devices with their start and end apart: 44 -> 41, of which waited for: 20 -> 18; matrix products, arithmetic and copies ran while one was open for 0% -> 1% of each run, Pallas kernels for 12% -> 8%
where the time goes in v6:
time: 109 us
  starting transfers between devices  52.2 us (48%)
  waiting for transfers between devices  43.8 us (40%)
  Pallas kernels  10 us (9%)
  local copies, waits for them, and re-layouts  1.09 us (1%)
    ppermute x41, starting transfers between devices, swap(): return lax.ppermute(x, axis, [(i, i ^ bit) for i in range(size)])  52.2 us
    ppermute x41, waiting for transfers between devices, swap(): return lax.ppermute(x, axis, [(i, i ^ bit) for i in range(size)])  43.8 us
    pallas_call x25, Pallas kernels, call(): pl.pallas_call(body, name=name, out_shape=list(out_shape), in_specs=[smem...  10 us
  transfers between devices with their start and end apart: 41, of which 18 were waited for; matrix products, arithmetic and copies ran while one was open for 1% of the time, Pallas kernels for 8%

profile of v6, /device:TPU:0, one launch (start us, length us, event | category | flops | bytes accessed | tf_op | source)
XLA Modules:
  0.0 108.9 jit_solution(9580403174295784429)
XLA Ops:
  0.7 1.1 copy-done.1
  1.9 3.0 %collective-permute-start.4 = (bf16[512,640]{1,0:T(8,128)(2,1)S(1)}, bf16[512,640]{1,0:T(8,128)(2,1)S(1)}, u32[]{:S(2)}, u32[]{:S(2)}) collective-permute-start(bf16[512,640]{1,0:T(8,128)(2,1)S(1)} %get-tuple-element.30), channel_id=1, source_target_pairs={{0,4},{4,0},{8,12},{12,8},{16,20},{20,16},{24,28},{28,24},{1,5},{5... | collective-permute-start | bytes 1966088 | tf_op jit(solution)/shard_map/ppermute | solution.py:227
  4.9 2.6 %collective-permute-start = (bf16[512,256]{1,0:T(8,128)(2,1)S(1)}, bf16[512,256]{1,0:T(8,128)(2,1)S(1)}, u32[]{:S(2)}, u32[]{:S(2)}) collective-permute-start(bf16[512,256]{1,0:T(8,128)(2,1)S(1)} %get-tuple-element.29.refs_1_), channel_id=1, source_target_pairs={{0,16},{4,20},{8,24},{12,28},{16,0},{20,4},{24,8},{28,12},{1,17},{... | collective-permute-start | bytes 786440 | tf_op jit(solution)/shard_map/ppermute | solution.py:227
  7.5 11.7 %collective-permute-done.refs_2_ = bf16[512,256]{1,0:T(8,128)(2,1)S(1)} collective-permute-done((bf16[512,256]{1,0:T(8,128)(2,1)S(1)}, bf16[512,256]{1,0:T(8,128)(2,1)S(1)}, u32[]{:S(2)}, u32[]{:S(2)}) %collective-permute-start) | collective-permute-done | bytes 262176 | tf_op jit(solution)/shard_map/ppermute | solution.py:227
  19.2 0.5 collective-permute-start.32
  19.9 0.8 convert_element_type.3.refs_0_
  20.7 0.6 coefficients.1
  21.3 5.1 %collective-permute-done.32.refs_4_ = bf16[512,256]{1,0:T(8,128)(2,1)S(1)} collective-permute-done((bf16[512,256]{1,0:T(8,128)(2,1)S(1)}, bf16[512,256]{1,0:T(8,128)(2,1)S(1)}, u32[]{:S(2)}, u32[]{:S(2)}) %collective-permute-start.32) | collective-permute-done | bytes 262176 | tf_op jit(solution)/shard_map/ppermute | solution.py:227
  26.4 0.2 mix.14
  26.6 1.8 %collective-permute-start.33 = (bf16[1,512,256]{2,1,0:T(8,128)(2,1)S(1)}, bf16[1,512,256]{2,1,0:T(8,128)(2,1)S(1)}, u32[]{:S(2)}, u32[]{:S(2)}) collective-permute-start(bf16[1,512,256]{2,1,0:T(8,128)(2,1)S(1)} %mix.14), channel_id=1, source_target_pairs={{0,8},{4,12},{8,0},{12,4},{16,24},{20,28},{24,16},{28,20},{1,9},{5... | collective-permute-start | bytes 786440 | tf_op jit(solution)/shard_map/ppermute | solution.py:227
  28.5 3.4 %collective-permute-start.2 = (bf16[512,128]{1,0:T(8,128)(2,1)S(1)}, bf16[512,128]{1,0:T(8,128)(2,1)S(1)}, u32[]{:S(2)}, u32[]{:S(2)}) collective-permute-start(bf16[512,128]{1,0:T(8,128)(2,1)S(1)} %mask_chunk.4.refs_1_), channel_id=1, source_target_pairs={{0,16},{4,20},{8,24},{12,28},{16,0},{20,4},{24,8},{28,12},{1,17},{... | collective-permute-start | bytes 393224 | tf_op jit(solution)/shard_map/ppermute | solution.py:227
  32.0 0.5 collective-permute-start.23
  32.5 3.6 %collective-permute-done.2.refs_2_ = bf16[512,128]{1,0:T(8,128)(2,1)S(1)} collective-permute-done((bf16[512,128]{1,0:T(8,128)(2,1)S(1)}, bf16[512,128]{1,0:T(8,128)(2,1)S(1)}, u32[]{:S(2)}, u32[]{:S(2)}) %collective-permute-start.2) | collective-permute-done | bytes 131104 | tf_op jit(solution)/shard_map/ppermute | solution.py:227
  36.1 0.5 collective-permute-start.14
  36.7 3.4 %collective-permute-start.3 = (bf16[512,128]{1,0:T(8,128)(2,1)S(1)}, bf16[512,128]{1,0:T(8,128)(2,1)S(1)}, u32[]{:S(2)}, u32[]{:S(2)}) collective-permute-start(bf16[512,128]{1,0:T(8,128)(2,1)S(1)} %mask_chunk.5.refs_1_), channel_id=1, source_target_pairs={{0,16},{4,20},{8,24},{12,28},{16,0},{20,4},{24,8},{28,12},{1,17},{... | collective-permute-start | bytes 393224 | tf_op jit(solution)/shard_map/ppermute | solution.py:227
  40.2 1.0 mix_multiply.7
  41.3 1.6 %collective-permute-start.35 = (bf16[512,256]{1,0:T(8,128)(2,1)S(1)}, bf16[512,256]{1,0:T(8,128)(2,1)S(1)}, u32[]{:S(2)}, u32[]{:S(2)}) collective-permute-start(bf16[512,256]{1,0:T(8,128)(2,1)S(1)} %get-tuple-element.45), channel_id=1, source_target_pairs={{0,2},{1,3},{2,0},{3,1},{4,6},{5,7},{6,4},{7,5},{8,10},{9,11},{10,... | collective-permute-start | bytes 786440 | tf_op jit(solution)/shard_map/ppermute | solution.py:227
  43.0 0.3 collective-permute-start.36
  43.3 2.0 %collective-permute-start.24 = (bf16[1,512,128]{2,1,0:T(8,128)(2,1)S(1)}, bf16[1,512,128]{2,1,0:T(8,128)(2,1)S(1)}, u32[]{:S(2)}, u32[]{:S(2)}) collective-permute-start(bf16[1,512,128]{2,1,0:T(8,128)(2,1)S(1)} %mix.12), channel_id=1, source_target_pairs={{0,8},{4,12},{8,0},{12,4},{16,24},{20,28},{24,16},{28,20},{1,9},{5... | collective-permute-start | bytes 393224 | tf_op jit(solution)/shard_map/ppermute | solution.py:227
  45.3 0.7 collective-permute-start.5
  46.2 2.9 %collective-permute-done.24.refs_5_ = bf16[1,512,128]{2,1,0:T(8,128)(2,1)S(1)} collective-permute-done((bf16[1,512,128]{2,1,0:T(8,128)(2,1)S(1)}, bf16[1,512,128]{2,1,0:T(8,128)(2,1)S(1)}, u32[]{:S(2)}, u32[]{:S(2)}) %collective-permute-start.24) | collective-permute-done | bytes 131104 | tf_op jit(solution)/shard_map/ppermute | solution.py:227
  49.1 1.2 %collective-permute-start.15 = (bf16[1,512,128]{2,1,0:T(8,128)(2,1)S(1)}, bf16[1,512,128]{2,1,0:T(8,128)(2,1)S(1)}, u32[]{:S(2)}, u32[]{:S(2)}) collective-permute-start(bf16[1,512,128]{2,1,0:T(8,128)(2,1)S(1)} %mix.10), channel_id=1, source_target_pairs={{0,8},{4,12},{8,0},{12,4},{16,24},{20,28},{24,16},{28,20},{1,9},{5... | collective-permute-start | bytes 393224 | tf_op jit(solution)/shard_map/ppermute | solution.py:227
  50.3 0.9 mix_multiply.6
  51.4 1.6 %collective-permute-start.26 = (bf16[512,128]{1,0:T(8,128)(2,1)S(1)}, bf16[512,128]{1,0:T(8,128)(2,1)S(1)}, u32[]{:S(2)}, u32[]{:S(2)}) collective-permute-start(bf16[512,128]{1,0:T(8,128)(2,1)S(1)} %get-tuple-element.41), channel_id=1, source_target_pairs={{0,2},{1,3},{2,0},{3,1},{4,6},{5,7},{6,4},{7,5},{8,10},{9,11},{10,... | collective-permute-start | bytes 393224 | tf_op jit(solution)/shard_map/ppermute | solution.py:227
  53.0 0.3 collective-permute-start.27
  53.3 1.8 %collective-permute-done.36.refs_3_ = bf16[512,256]{1,0:T(8,128)(2,1)S(1)} collective-permute-done((bf16[512,256]{1,0:T(8,128)(2,1)S(1)}, bf16[512,256]{1,0:T(8,128)(2,1)S(1)}, u32[]{:S(2)}, u32[]{:S(2)}) %collective-permute-start.36) | collective-permute-done | bytes 262176 | tf_op jit(solution)/shard_map/ppermute | solution.py:227
  55.3 0.7 collective-permute-start.37
  56.0 3.0 %collective-permute-start.6 = (bf16[1,512,128]{2,1,0:T(8,128)(2,1)S(1)}, bf16[1,512,128]{2,1,0:T(8,128)(2,1)S(1)}, u32[]{:S(2)}, u32[]{:S(2)}) collective-permute-start(bf16[1,512,128]{2,1,0:T(8,128)(2,1)S(1)} %mix.8), channel_id=1, source_target_pairs={{0,8},{4,12},{8,0},{12,4},{16,24},{20,28},{24,16},{28,20},{1,9},{5... | collective-permute-start | bytes 393224 | tf_op jit(solution)/shard_map/ppermute | solution.py:227
  59.1 0.9 mix_multiply.5
  60.2 1.5 %collective-permute-start.17 = (bf16[512,128]{1,0:T(8,128)(2,1)S(1)}, bf16[512,128]{1,0:T(8,128)(2,1)S(1)}, u32[]{:S(2)}, u32[]{:S(2)}) collective-permute-start(bf16[512,128]{1,0:T(8,128)(2,1)S(1)} %get-tuple-element.37), channel_id=1, source_target_pairs={{0,2},{1,3},{2,0},{3,1},{4,6},{5,7},{6,4},{7,5},{8,10},{9,11},{10,... | collective-permute-start | bytes 393224 | tf_op jit(solution)/shard_map/ppermute | solution.py:227
  61.7 0.8 collective-permute-start.18
  62.6 2.4 %collective-permute-done.6.refs_5_ = bf16[1,512,128]{2,1,0:T(8,128)(2,1)S(1)} collective-permute-done((bf16[1,512,128]{2,1,0:T(8,128)(2,1)S(1)}, bf16[1,512,128]{2,1,0:T(8,128)(2,1)S(1)}, u32[]{:S(2)}, u32[]{:S(2)}) %collective-permute-start.6) | collective-permute-done | bytes 131104 | tf_op jit(solution)/shard_map/ppermute | solution.py:227
  65.0 4.1 %collective-permute-start.28 = (bf16[512,128]{1,0:T(8,128)(2,1)S(1)}, bf16[512,128]{1,0:T(8,128)(2,1)S(1)}, u32[]{:S(2)}, u32[]{:S(2)}) collective-permute-start(bf16[512,128]{1,0:T(8,128)(2,1)S(1)} %add_up.6.refs_1_.refs_2_), channel_id=1, source_target_pairs={{0,16},{4,20},{8,24},{12,28},{16,0},{20,4},{24,8},{28,12},{1,17},{... | collective-permute-start | bytes 393224 | tf_op jit(solution)/shard_map/ppermute | solution.py:227
  69.1 0.9 mix_multiply.4
  70.1 1.6 %collective-permute-start.8 = (bf16[512,128]{1,0:T(8,128)(2,1)S(1)}, bf16[512,128]{1,0:T(8,128)(2,1)S(1)}, u32[]{:S(2)}, u32[]{:S(2)}) collective-permute-start(bf16[512,128]{1,0:T(8,128)(2,1)S(1)} %get-tuple-element.33), channel_id=1, source_target_pairs={{0,2},{1,3},{2,0},{3,1},{4,6},{5,7},{6,4},{7,5},{8,10},{9,11},{10,... | collective-permute-start | bytes 393224 | tf_op jit(solution)/shard_map/ppermute | solution.py:227
  71.7 1.6 %collective-permute-start.38 = (bf16[512,256]{1,0:T(8,128)(2,1)S(1)}, bf16[512,256]{1,0:T(8,128)(2,1)S(1)}, u32[]{:S(2)}, u32[]{:S(2)}) collective-permute-start(bf16[512,256]{1,0:T(8,128)(2,1)S(1)} %add_up.7.refs_1_.refs_2_), channel_id=1, source_target_pairs={{0,4},{4,0},{8,12},{12,8},{16,20},{20,16},{24,28},{28,24},{1,5},{5... | collective-permute-start | bytes 786440 | tf_op jit(solution)/shard_map/ppermute | solution.py:227
  73.2 0.6 collective-permute-done.37.refs_2_.refs_3_
  73.9 1.5 %collective-permute-start.39 = (bf16[512,256]{1,0:T(8,128)(2,1)S(1)}, bf16[512,256]{1,0:T(8,128)(2,1)S(1)}, u32[]{:S(2)}, u32[]{:S(2)}) collective-permute-start(bf16[512,256]{1,0:T(8,128)(2,1)S(1)} %collective-permute-done.37.refs_2_.refs_3_), channel_id=1, source_target_pairs={{0,4},{4,0},{8,12},{12,8},{16,20},{20,16},{24,28},{28,24},{1,5},{5... | collective-permute-start | bytes 786440 | tf_op jit(solution)/shard_map/ppermute | solution.py:227
  75.4 1.1 collective-permute-done.28.refs_2_.refs_3_
  76.5 1.0 collective-permute-start.9
  77.7 1.6 %collective-permute-start.29 = (bf16[512,128]{1,0:T(8,128)(2,1)S(1)}, bf16[512,128]{1,0:T(8,128)(2,1)S(1)}, u32[]{:S(2)}, u32[]{:S(2)}) collective-permute-start(bf16[512,128]{1,0:T(8,128)(2,1)S(1)} %add_up.6.refs_1_.refs_2_), channel_id=1, source_target_pairs={{0,4},{4,0},{8,12},{12,8},{16,20},{20,16},{24,28},{28,24},{1,5},{5... | collective-permute-start | bytes 393224 | tf_op jit(solution)/shard_map/ppermute | solution.py:227
  79.2 3.0 %collective-permute-done.9.refs_3_ = bf16[512,128]{1,0:T(8,128)(2,1)S(1)} collective-permute-done((bf16[512,128]{1,0:T(8,128)(2,1)S(1)}, bf16[512,128]{1,0:T(8,128)(2,1)S(1)}, u32[]{:S(2)}, u32[]{:S(2)}) %collective-permute-start.9) | collective-permute-done | bytes 131104 | tf_op jit(solution)/shard_map/ppermute | solution.py:227
  82.2 1.5 %collective-permute-start.30 = (bf16[512,128]{1,0:T(8,128)(2,1)S(1)}, bf16[512,128]{1,0:T(8,128)(2,1)S(1)}, u32[]{:S(2)}, u32[]{:S(2)}) collective-permute-start(bf16[512,128]{1,0:T(8,128)(2,1)S(1)} %collective-permute-done.28.refs_2_.refs_3_), channel_id=1, source_target_pairs={{0,4},{4,0},{8,12},{12,8},{16,20},{20,16},{24,28},{28,24},{1,5},{5... | collective-permute-start | bytes 393224 | tf_op jit(solution)/shard_map/ppermute | solution.py:227
  83.8 1.9 %collective-permute-done.19.refs_2_.refs_3_ = bf16[512,128]{1,0:T(8,128)(2,1)S(1)} collective-permute-done((bf16[512,128]{1,0:T(8,128)(2,1)S(1)}, bf16[512,128]{1,0:T(8,128)(2,1)S(1)}, u32[]{:S(2)}, u32[]{:S(2)}) %collective-permute-start.19) | collective-permute-done | bytes 131104 | tf_op jit(solution)/shard_map/ppermute | solution.py:227
  85.7 1.5 %collective-permute-start.20 = (bf16[512,128]{1,0:T(8,128)(2,1)S(1)}, bf16[512,128]{1,0:T(8,128)(2,1)S(1)}, u32[]{:S(2)}, u32[]{:S(2)}) collective-permute-start(bf16[512,128]{1,0:T(8,128)(2,1)S(1)} %add_up.5.refs_1_.refs_2_), channel_id=1, source_target_pairs={{0,4},{4,0},{8,12},{12,8},{16,20},{20,16},{24,28},{28,24},{1,5},{5... | collective-permute-start | bytes 393224 | tf_op jit(solution)/shard_map/ppermute | solution.py:227
  87.2 0.9 collective-permute-start.21
  88.0 0.2 mix.15
  88.3 1.0 collective-permute-done.29.refs_3_.refs_4_
  89.2 2.2 %collective-permute-start.40 = (bf16[1,512,256]{2,1,0:T(8,128)(2,1)S(1)}, bf16[1,512,256]{2,1,0:T(8,128)(2,1)S(1)}, u32[]{:S(2)}, u32[]{:S(2)}) collective-permute-start(bf16[1,512,256]{2,1,0:T(8,128)(2,1)S(1)} %mix.15), channel_id=1, source_target_pairs={{0,8},{4,12},{8,0},{12,4},{16,24},{20,28},{24,16},{28,20},{1,9},{5... | collective-permute-start | bytes 786440 | tf_op jit(solution)/shard_map/ppermute | solution.py:227
  91.5 0.6 collective-permute-done.30.refs_4_.refs_5_
  92.0 1.6 %collective-permute-start.11 = (bf16[512,128]{1,0:T(8,128)(2,1)S(1)}, bf16[512,128]{1,0:T(8,128)(2,1)S(1)}, u32[]{:S(2)}, u32[]{:S(2)}) collective-permute-start(bf16[512,128]{1,0:T(8,128)(2,1)S(1)} %add_up.4.refs_1_.refs_2_), channel_id=1, source_target_pairs={{0,4},{4,0},{8,12},{12,8},{16,20},{20,16},{24,28},{28,24},{1,5},{5... | collective-permute-start | bytes 393224 | tf_op jit(solution)/shard_map/ppermute | solution.py:227
  93.6 1.3 %collective-permute-done.10.refs_2_.refs_3_ = bf16[512,128]{1,0:T(8,128)(2,1)S(1)} collective-permute-done((bf16[512,128]{1,0:T(8,128)(2,1)S(1)}, bf16[512,128]{1,0:T(8,128)(2,1)S(1)}, u32[]{:S(2)}, u32[]{:S(2)}) %collective-permute-start.10) | collective-permute-done | bytes 131104 | tf_op jit(solution)/shard_map/ppermute | solution.py:227
  95.0 1.5 %collective-permute-start.12 = (bf16[512,128]{1,0:T(8,128)(2,1)S(1)}, bf16[512,128]{1,0:T(8,128)(2,1)S(1)}, u32[]{:S(2)}, u32[]{:S(2)}) collective-permute-start(bf16[512,128]{1,0:T(8,128)(2,1)S(1)} %collective-permute-done.10.refs_2_.refs_3_), channel_id=1, source_target_pairs={{0,4},{4,0},{8,12},{12,8},{16,20},{20,16},{24,28},{28,24},{1,5},{5... | collective-permute-start | bytes 393224 | tf_op jit(solution)/shard_map/ppermute | solution.py:227
  96.7 1.0 collective-permute-done.21.refs_4_.refs_5_
  97.8 1.1 %collective-permute-start.22 = (bf16[1,512,128]{2,1,0:T(8,128)(2,1)S(1)}, bf16[1,512,128]{2,1,0:T(8,128)(2,1)S(1)}, u32[]{:S(2)}, u32[]{:S(2)}) collective-permute-start(bf16[1,512,128]{2,1,0:T(8,128)(2,1)S(1)} %mix.11), channel_id=1, source_target_pairs={{0,8},{4,12},{8,0},{12,4},{16,24},{20,28},{24,16},{28,20},{1,9},{5... | collective-permute-start | bytes 393224 | tf_op jit(solution)/shard_map/ppermute | solution.py:227
  98.9 1.6 %collective-permute-done.11.refs_3_.refs_4_ = bf16[512,128]{1,0:T(8,128)(2,1)S(1)} collective-permute-done((bf16[512,128]{1,0:T(8,128)(2,1)S(1)}, bf16[512,128]{1,0:T(8,128)(2,1)S(1)}, u32[]{:S(2)}, u32[]{:S(2)}) %collective-permute-start.11) | collective-permute-done | bytes 131104 | tf_op jit(solution)/shard_map/ppermute | solution.py:227
  100.5 2.0 %collective-permute-done.12.refs_4_.refs_5_ = bf16[512,128]{1,0:T(8,128)(2,1)S(1)} collective-permute-done((bf16[512,128]{1,0:T(8,128)(2,1)S(1)}, bf16[512,128]{1,0:T(8,128)(2,1)S(1)}, u32[]{:S(2)}, u32[]{:S(2)}) %collective-permute-start.12) | collective-permute-done | bytes 131104 | tf_op jit(solution)/shard_map/ppermute | solution.py:227
  102.6 0.4 collective-permute-start.13
  103.0 1.0 finish.4.refs_7_
  104.1 0.9 finish.5.refs_7_
  104.9 0.9 collective-permute-done.22.refs_6_
  105.8 0.9 finish.6.refs_7_
  106.7 1.4 %collective-permute-done.13.refs_6_ = bf16[1,512,128]{2,1,0:T(8,128)(2,1)S(1)} collective-permute-done((bf16[1,512,128]{2,1,0:T(8,128)(2,1)S(1)}, bf16[1,512,128]{2,1,0:T(8,128)(2,1)S(1)}, u32[]{:S(2)}, u32[]{:S(2)}) %collective-permute-start.13) | collective-permute-done | bytes 131104 | tf_op jit(solution)/shard_map/ppermute | solution.py:227
  108.1 0.9 finish.7
  (50 shorter events, 2.5 us)
Async XLA Ops:
  0.7 1.1 copy-start.1
  1.7 26.7 %copy-start.2 = (bf16[512,1,640]{2,0,1:T(8,128)(2,1)S(1)}, bf16[512,1,640]{2,0,1:T(8,128)(2,1)}, u32[]{:S(2)}) copy-start(bf16[512,1,640]{2,0,1:T(8,128)(2,1)} %param.4) | copy-start | bytes 1966084
  1.9 24.4 %collective-permute-start.4 = (bf16[512,640]{1,0:T(8,128)(2,1)S(1)}, bf16[512,640]{1,0:T(8,128)(2,1)S(1)}, u32[]{:S(2)}, u32[]{:S(2)}) collective-permute-start(bf16[512,640]{1,0:T(8,128)(2,1)S(1)} %get-tuple-element.30), channel_id=1, source_target_pairs={{0,4},{4,0},{8,12},{12,8},{16,20},{20,16},{24,28},{28,24},{1,5},{5... | collective-permute-start | bytes 1966088 | tf_op jit(solution)/shard_map/ppermute | solution.py:227
  4.9 14.3 %collective-permute-start = (bf16[512,256]{1,0:T(8,128)(2,1)S(1)}, bf16[512,256]{1,0:T(8,128)(2,1)S(1)}, u32[]{:S(2)}, u32[]{:S(2)}) collective-permute-start(bf16[512,256]{1,0:T(8,128)(2,1)S(1)} %get-tuple-element.29.refs_1_), channel_id=1, source_target_pairs={{0,16},{4,20},{8,24},{12,28},{16,0},{20,4},{24,8},{28,12},{1,17},{... | collective-permute-start | bytes 786440 | tf_op jit(solution)/shard_map/ppermute | solution.py:227
  19.2 7.2 %collective-permute-start.32 = (bf16[512,256]{1,0:T(8,128)(2,1)S(1)}, bf16[512,256]{1,0:T(8,128)(2,1)S(1)}, u32[]{:S(2)}, u32[]{:S(2)}) collective-permute-start(bf16[512,256]{1,0:T(8,128)(2,1)S(1)} %collective-permute-done.refs_2_), channel_id=1, source_target_pairs={{0,4},{4,0},{8,12},{12,8},{16,20},{20,16},{24,28},{28,24},{1,5},{5... | collective-permute-start | bytes 786440 | tf_op jit(solution)/shard_map/ppermute | solution.py:227
  19.7 20.5 %copy-start = (bf16[2048,1,512]{2,0,1:T(8,128)(2,1)S(1)}, bf16[2048,1,512]{2,0,1:T(8,128)(2,1)}, u32[]{:S(2)}) copy-start(bf16[2048,1,512]{2,0,1:T(8,128)(2,1)} %param.7) | copy-start | bytes 6291460
  19.8 8.6 %collective-permute-start.1 = (bf16[512,128]{1,0:T(8,128)(2,1)S(1)}, bf16[512,128]{1,0:T(8,128)(2,1)S(1)}, u32[]{:S(2)}, u32[]{:S(2)}) collective-permute-start(bf16[512,128]{1,0:T(8,128)(2,1)S(1)} %mask_chunk.3.refs_1_), channel_id=1, source_target_pairs={{0,16},{4,20},{8,24},{12,28},{16,0},{20,4},{24,8},{28,12},{1,17},{... | collective-permute-start | bytes 393224 | tf_op jit(solution)/shard_map/ppermute | solution.py:227
  26.6 13.6 %collective-permute-start.33 = (bf16[1,512,256]{2,1,0:T(8,128)(2,1)S(1)}, bf16[1,512,256]{2,1,0:T(8,128)(2,1)S(1)}, u32[]{:S(2)}, u32[]{:S(2)}) collective-permute-start(bf16[1,512,256]{2,1,0:T(8,128)(2,1)S(1)} %mix.14), channel_id=1, source_target_pairs={{0,8},{4,12},{8,0},{12,4},{16,24},{20,28},{24,16},{28,20},{1,9},{5... | collective-permute-start | bytes 786440 | tf_op jit(solution)/shard_map/ppermute | solution.py:227
  28.5 7.6 %collective-permute-start.2 = (bf16[512,128]{1,0:T(8,128)(2,1)S(1)}, bf16[512,128]{1,0:T(8,128)(2,1)S(1)}, u32[]{:S(2)}, u32[]{:S(2)}) collective-permute-start(bf16[512,128]{1,0:T(8,128)(2,1)S(1)} %mask_chunk.4.refs_1_), channel_id=1, source_target_pairs={{0,16},{4,20},{8,24},{12,28},{16,0},{20,4},{24,8},{28,12},{1,17},{... | collective-permute-start | bytes 393224 | tf_op jit(solution)/shard_map/ppermute | solution.py:227
  32.0 10.9 %collective-permute-start.23 = (bf16[512,128]{1,0:T(8,128)(2,1)S(1)}, bf16[512,128]{1,0:T(8,128)(2,1)S(1)}, u32[]{:S(2)}, u32[]{:S(2)}) collective-permute-start(bf16[512,128]{1,0:T(8,128)(2,1)S(1)} %collective-permute-done.1.refs_2_), channel_id=1, source_target_pairs={{0,4},{4,0},{8,12},{12,8},{16,20},{20,16},{24,28},{28,24},{1,5},{5... | collective-permute-start | bytes 393224 | tf_op jit(solution)/shard_map/ppermute | solution.py:227
  36.1 7.2 %collective-permute-start.14 = (bf16[512,128]{1,0:T(8,128)(2,1)S(1)}, bf16[512,128]{1,0:T(8,128)(2,1)S(1)}, u32[]{:S(2)}, u32[]{:S(2)}) collective-permute-start(bf16[512,128]{1,0:T(8,128)(2,1)S(1)} %collective-permute-done.2.refs_2_), channel_id=1, source_target_pairs={{0,4},{4,0},{8,12},{12,8},{16,20},{20,16},{24,28},{28,24},{1,5},{5... | collective-permute-start | bytes 393224 | tf_op jit(solution)/shard_map/ppermute | solution.py:227
  36.7 8.6 %collective-permute-start.3 = (bf16[512,128]{1,0:T(8,128)(2,1)S(1)}, bf16[512,128]{1,0:T(8,128)(2,1)S(1)}, u32[]{:S(2)}, u32[]{:S(2)}) collective-permute-start(bf16[512,128]{1,0:T(8,128)(2,1)S(1)} %mask_chunk.5.refs_1_), channel_id=1, source_target_pairs={{0,16},{4,20},{8,24},{12,28},{16,0},{20,4},{24,8},{28,12},{1,17},{... | collective-permute-start | bytes 393224 | tf_op jit(solution)/shard_map/ppermute | solution.py:227
  41.2 10.2 %collective-permute-start.34 = (bf16[512,256]{1,0:T(8,128)(2,1)S(1)}, bf16[512,256]{1,0:T(8,128)(2,1)S(1)}, u32[]{:S(2)}, u32[]{:S(2)}) collective-permute-start(bf16[512,256]{1,0:T(8,128)(2,1)S(1)} %get-tuple-element.44), channel_id=1, source_target_pairs={{0,1},{1,0},{2,3},{3,2},{4,5},{5,4},{6,7},{7,6},{8,9},{9,8},{10,11... | collective-permute-start | bytes 786440 | tf_op jit(solution)/shard_map/ppermute | solution.py:227
  41.3 11.7 %collective-permute-start.35 = (bf16[512,256]{1,0:T(8,128)(2,1)S(1)}, bf16[512,256]{1,0:T(8,128)(2,1)S(1)}, u32[]{:S(2)}, u32[]{:S(2)}) collective-permute-start(bf16[512,256]{1,0:T(8,128)(2,1)S(1)} %get-tuple-element.45), channel_id=1, source_target_pairs={{0,2},{1,3},{2,0},{3,1},{4,6},{5,7},{6,4},{7,5},{8,10},{9,11},{10,... | collective-permute-start | bytes 786440 | tf_op jit(solution)/shard_map/ppermute | solution.py:227
  43.0 12.1 %collective-permute-start.36 = (bf16[512,256]{1,0:T(8,128)(2,1)S(1)}, bf16[512,256]{1,0:T(8,128)(2,1)S(1)}, u32[]{:S(2)}, u32[]{:S(2)}) collective-permute-start(bf16[512,256]{1,0:T(8,128)(2,1)S(1)} %get-tuple-element.46), channel_id=1, source_target_pairs={{0,3},{1,2},{2,1},{3,0},{4,7},{5,6},{6,5},{7,4},{8,11},{9,10},{10,... | collective-permute-start | bytes 786440 | tf_op jit(solution)/shard_map/ppermute | solution.py:227
  43.3 5.7 %collective-permute-start.24 = (bf16[1,512,128]{2,1,0:T(8,128)(2,1)S(1)}, bf16[1,512,128]{2,1,0:T(8,128)(2,1)S(1)}, u32[]{:S(2)}, u32[]{:S(2)}) collective-permute-start(bf16[1,512,128]{2,1,0:T(8,128)(2,1)S(1)} %mix.12), channel_id=1, source_target_pairs={{0,8},{4,12},{8,0},{12,4},{16,24},{20,28},{24,16},{28,20},{1,9},{5... | collective-permute-start | bytes 393224 | tf_op jit(solution)/shard_map/ppermute | solution.py:227
  45.3 5.8 %collective-permute-start.5 = (bf16[512,128]{1,0:T(8,128)(2,1)S(1)}, bf16[512,128]{1,0:T(8,128)(2,1)S(1)}, u32[]{:S(2)}, u32[]{:S(2)}) collective-permute-start(bf16[512,128]{1,0:T(8,128)(2,1)S(1)} %collective-permute-done.3.refs_2_), channel_id=1, source_target_pairs={{0,4},{4,0},{8,12},{12,8},{16,20},{20,16},{24,28},{28,24},{1,5},{5... | collective-permute-start | bytes 393224 | tf_op jit(solution)/shard_map/ppermute | solution.py:227
  49.1 6.9 %collective-permute-start.15 = (bf16[1,512,128]{2,1,0:T(8,128)(2,1)S(1)}, bf16[1,512,128]{2,1,0:T(8,128)(2,1)S(1)}, u32[]{:S(2)}, u32[]{:S(2)}) collective-permute-start(bf16[1,512,128]{2,1,0:T(8,128)(2,1)S(1)} %mix.10), channel_id=1, source_target_pairs={{0,8},{4,12},{8,0},{12,4},{16,24},{20,28},{24,16},{28,20},{1,9},{5... | collective-permute-start | bytes 393224 | tf_op jit(solution)/shard_map/ppermute | solution.py:227
  51.2 8.8 %collective-permute-start.25 = (bf16[512,128]{1,0:T(8,128)(2,1)S(1)}, bf16[512,128]{1,0:T(8,128)(2,1)S(1)}, u32[]{:S(2)}, u32[]{:S(2)}) collective-permute-start(bf16[512,128]{1,0:T(8,128)(2,1)S(1)} %get-tuple-element.40), channel_id=1, source_target_pairs={{0,1},{1,0},{2,3},{3,2},{4,5},{5,4},{6,7},{7,6},{8,9},{9,8},{10,11... | collective-permute-start | bytes 393224 | tf_op jit(solution)/shard_map/ppermute | solution.py:227
  51.4 8.8 %collective-permute-start.26 = (bf16[512,128]{1,0:T(8,128)(2,1)S(1)}, bf16[512,128]{1,0:T(8,128)(2,1)S(1)}, u32[]{:S(2)}, u32[]{:S(2)}) collective-permute-start(bf16[512,128]{1,0:T(8,128)(2,1)S(1)} %get-tuple-element.41), channel_id=1, source_target_pairs={{0,2},{1,3},{2,0},{3,1},{4,6},{5,7},{6,4},{7,5},{8,10},{9,11},{10,... | collective-permute-start | bytes 393224 | tf_op jit(solution)/shard_map/ppermute | solution.py:227
  53.0 8.7 %collective-permute-start.27 = (bf16[512,128]{1,0:T(8,128)(2,1)S(1)}, bf16[512,128]{1,0:T(8,128)(2,1)S(1)}, u32[]{:S(2)}, u32[]{:S(2)}) collective-permute-start(bf16[512,128]{1,0:T(8,128)(2,1)S(1)} %get-tuple-element.42), channel_id=1, source_target_pairs={{0,3},{1,2},{2,1},{3,0},{4,7},{5,6},{6,5},{7,4},{8,11},{9,10},{10,... | collective-permute-start | bytes 393224 | tf_op jit(solution)/shard_map/ppermute | solution.py:227
  55.3 18.6 %collective-permute-start.37 = (bf16[512,256]{1,0:T(8,128)(2,1)S(1)}, bf16[512,256]{1,0:T(8,128)(2,1)S(1)}, u32[]{:S(2)}, u32[]{:S(2)}) collective-permute-start(bf16[512,256]{1,0:T(8,128)(2,1)S(1)} %add_up.7.refs_1_.refs_2_), channel_id=1, source_target_pairs={{0,16},{4,20},{8,24},{12,28},{16,0},{20,4},{24,8},{28,12},{1,17},{... | collective-permute-start | bytes 786440 | tf_op jit(solution)/shard_map/ppermute | solution.py:227
  56.0 8.9 %collective-permute-start.6 = (bf16[1,512,128]{2,1,0:T(8,128)(2,1)S(1)}, bf16[1,512,128]{2,1,0:T(8,128)(2,1)S(1)}, u32[]{:S(2)}, u32[]{:S(2)}) collective-permute-start(bf16[1,512,128]{2,1,0:T(8,128)(2,1)S(1)} %mix.8), channel_id=1, source_target_pairs={{0,8},{4,12},{8,0},{12,4},{16,24},{20,28},{24,16},{28,20},{1,9},{5... | collective-permute-start | bytes 393224 | tf_op jit(solution)/shard_map/ppermute | solution.py:227
  59.9 10.0 %collective-permute-start.16 = (bf16[512,128]{1,0:T(8,128)(2,1)S(1)}, bf16[512,128]{1,0:T(8,128)(2,1)S(1)}, u32[]{:S(2)}, u32[]{:S(2)}) collective-permute-start(bf16[512,128]{1,0:T(8,128)(2,1)S(1)} %get-tuple-element.36), channel_id=1, source_target_pairs={{0,1},{1,0},{2,3},{3,2},{4,5},{5,4},{6,7},{7,6},{8,9},{9,8},{10,11... | collective-permute-start | bytes 393224 | tf_op jit(solution)/shard_map/ppermute | solution.py:227
  60.2 9.9 %collective-permute-start.17 = (bf16[512,128]{1,0:T(8,128)(2,1)S(1)}, bf16[512,128]{1,0:T(8,128)(2,1)S(1)}, u32[]{:S(2)}, u32[]{:S(2)}) collective-permute-start(bf16[512,128]{1,0:T(8,128)(2,1)S(1)} %get-tuple-element.37), channel_id=1, source_target_pairs={{0,2},{1,3},{2,0},{3,1},{4,6},{5,7},{6,4},{7,5},{8,10},{9,11},{10,... | collective-permute-start | bytes 393224 | tf_op jit(solution)/shard_map/ppermute | solution.py:227
  61.7 10.0 %collective-permute-start.18 = (bf16[512,128]{1,0:T(8,128)(2,1)S(1)}, bf16[512,128]{1,0:T(8,128)(2,1)S(1)}, u32[]{:S(2)}, u32[]{:S(2)}) collective-permute-start(bf16[512,128]{1,0:T(8,128)(2,1)S(1)} %get-tuple-element.38), channel_id=1, source_target_pairs={{0,3},{1,2},{2,1},{3,0},{4,7},{5,6},{6,5},{7,4},{8,11},{9,10},{10,... | collective-permute-start | bytes 393224 | tf_op jit(solution)/shard_map/ppermute | solution.py:227
  65.0 11.5 %collective-permute-start.28 = (bf16[512,128]{1,0:T(8,128)(2,1)S(1)}, bf16[512,128]{1,0:T(8,128)(2,1)S(1)}, u32[]{:S(2)}, u32[]{:S(2)}) collective-permute-start(bf16[512,128]{1,0:T(8,128)(2,1)S(1)} %add_up.6.refs_1_.refs_2_), channel_id=1, source_target_pairs={{0,16},{4,20},{8,24},{12,28},{16,0},{20,4},{24,8},{28,12},{1,17},{... | collective-permute-start | bytes 393224 | tf_op jit(solution)/shard_map/ppermute | solution.py:227
  70.0 7.6 %collective-permute-start.7 = (bf16[512,128]{1,0:T(8,128)(2,1)S(1)}, bf16[512,128]{1,0:T(8,128)(2,1)S(1)}, u32[]{:S(2)}, u32[]{:S(2)}) collective-permute-start(bf16[512,128]{1,0:T(8,128)(2,1)S(1)} %get-tuple-element.32), channel_id=1, source_target_pairs={{0,1},{1,0},{2,3},{3,2},{4,5},{5,4},{6,7},{7,6},{8,9},{9,8},{10,11... | collective-permute-start | bytes 393224 | tf_op jit(solution)/shard_map/ppermute | solution.py:227
  70.1 7.6 %collective-permute-start.8 = (bf16[512,128]{1,0:T(8,128)(2,1)S(1)}, bf16[512,128]{1,0:T(8,128)(2,1)S(1)}, u32[]{:S(2)}, u32[]{:S(2)}) collective-permute-start(bf16[512,128]{1,0:T(8,128)(2,1)S(1)} %get-tuple-element.33), channel_id=1, source_target_pairs={{0,2},{1,3},{2,0},{3,1},{4,6},{5,7},{6,4},{7,5},{8,10},{9,11},{10,... | collective-permute-start | bytes 393224 | tf_op jit(solution)/shard_map/ppermute | solution.py:227
  71.7 14.0 %collective-permute-start.38 = (bf16[512,256]{1,0:T(8,128)(2,1)S(1)}, bf16[512,256]{1,0:T(8,128)(2,1)S(1)}, u32[]{:S(2)}, u32[]{:S(2)}) collective-permute-start(bf16[512,256]{1,0:T(8,128)(2,1)S(1)} %add_up.7.refs_1_.refs_2_), channel_id=1, source_target_pairs={{0,4},{4,0},{8,12},{12,8},{16,20},{20,16},{24,28},{28,24},{1,5},{5... | collective-permute-start | bytes 786440 | tf_op jit(solution)/shard_map/ppermute | solution.py:227
  73.9 13.3 %collective-permute-start.39 = (bf16[512,256]{1,0:T(8,128)(2,1)S(1)}, bf16[512,256]{1,0:T(8,128)(2,1)S(1)}, u32[]{:S(2)}, u32[]{:S(2)}) collective-permute-start(bf16[512,256]{1,0:T(8,128)(2,1)S(1)} %collective-permute-done.37.refs_2_.refs_3_), channel_id=1, source_target_pairs={{0,4},{4,0},{8,12},{12,8},{16,20},{20,16},{24,28},{28,24},{1,5},{5... | collective-permute-start | bytes 786440 | tf_op jit(solution)/shard_map/ppermute | solution.py:227
  76.5 5.7 %collective-permute-start.9 = (bf16[512,128]{1,0:T(8,128)(2,1)S(1)}, bf16[512,128]{1,0:T(8,128)(2,1)S(1)}, u32[]{:S(2)}, u32[]{:S(2)}) collective-permute-start(bf16[512,128]{1,0:T(8,128)(2,1)S(1)} %get-tuple-element.34), channel_id=1, source_target_pairs={{0,3},{1,2},{2,1},{3,0},{4,7},{5,6},{6,5},{7,4},{8,11},{9,10},{10,... | collective-permute-start | bytes 393224 | tf_op jit(solution)/shard_map/ppermute | solution.py:227
  77.6 8.1 %collective-permute-start.19 = (bf16[512,128]{1,0:T(8,128)(2,1)S(1)}, bf16[512,128]{1,0:T(8,128)(2,1)S(1)}, u32[]{:S(2)}, u32[]{:S(2)}) collective-permute-start(bf16[512,128]{1,0:T(8,128)(2,1)S(1)} %add_up.5.refs_1_.refs_2_), channel_id=1, source_target_pairs={{0,16},{4,20},{8,24},{12,28},{16,0},{20,4},{24,8},{28,12},{1,17},{... | collective-permute-start | bytes 393224 | tf_op jit(solution)/shard_map/ppermute | solution.py:227
  77.7 11.6 %collective-permute-start.29 = (bf16[512,128]{1,0:T(8,128)(2,1)S(1)}, bf16[512,128]{1,0:T(8,128)(2,1)S(1)}, u32[]{:S(2)}, u32[]{:S(2)}) collective-permute-start(bf16[512,128]{1,0:T(8,128)(2,1)S(1)} %add_up.6.refs_1_.refs_2_), channel_id=1, source_target_pairs={{0,4},{4,0},{8,12},{12,8},{16,20},{20,16},{24,28},{28,24},{1,5},{5... | collective-permute-start | bytes 393224 | tf_op jit(solution)/shard_map/ppermute | solution.py:227
  82.2 9.9 %collective-permute-start.30 = (bf16[512,128]{1,0:T(8,128)(2,1)S(1)}, bf16[512,128]{1,0:T(8,128)(2,1)S(1)}, u32[]{:S(2)}, u32[]{:S(2)}) collective-permute-start(bf16[512,128]{1,0:T(8,128)(2,1)S(1)} %collective-permute-done.28.refs_2_.refs_3_), channel_id=1, source_target_pairs={{0,4},{4,0},{8,12},{12,8},{16,20},{20,16},{24,28},{28,24},{1,5},{5... | collective-permute-start | bytes 393224 | tf_op jit(solution)/shard_map/ppermute | solution.py:227
  85.6 9.3 %collective-permute-start.10 = (bf16[512,128]{1,0:T(8,128)(2,1)S(1)}, bf16[512,128]{1,0:T(8,128)(2,1)S(1)}, u32[]{:S(2)}, u32[]{:S(2)}) collective-permute-start(bf16[512,128]{1,0:T(8,128)(2,1)S(1)} %add_up.4.refs_1_.refs_2_), channel_id=1, source_target_pairs={{0,16},{4,20},{8,24},{12,28},{16,0},{20,4},{24,8},{28,12},{1,17},{... | collective-permute-start | bytes 393224 | tf_op jit(solution)/shard_map/ppermute | solution.py:227
  85.7 10.9 %collective-permute-start.20 = (bf16[512,128]{1,0:T(8,128)(2,1)S(1)}, bf16[512,128]{1,0:T(8,128)(2,1)S(1)}, u32[]{:S(2)}, u32[]{:S(2)}) collective-permute-start(bf16[512,128]{1,0:T(8,128)(2,1)S(1)} %add_up.5.refs_1_.refs_2_), channel_id=1, source_target_pairs={{0,4},{4,0},{8,12},{12,8},{16,20},{20,16},{24,28},{28,24},{1,5},{5... | collective-permute-start | bytes 393224 | tf_op jit(solution)/shard_map/ppermute | solution.py:227
  87.2 10.5 %collective-permute-start.21 = (bf16[512,128]{1,0:T(8,128)(2,1)S(1)}, bf16[512,128]{1,0:T(8,128)(2,1)S(1)}, u32[]{:S(2)}, u32[]{:S(2)}) collective-permute-start(bf16[512,128]{1,0:T(8,128)(2,1)S(1)} %collective-permute-done.19.refs_2_.refs_3_), channel_id=1, source_target_pairs={{0,4},{4,0},{8,12},{12,8},{16,20},{20,16},{24,28},{28,24},{1,5},{5... | collective-permute-start | bytes 393224 | tf_op jit(solution)/shard_map/ppermute | solution.py:227
  89.2 13.8 %collective-permute-start.40 = (bf16[1,512,256]{2,1,0:T(8,128)(2,1)S(1)}, bf16[1,512,256]{2,1,0:T(8,128)(2,1)S(1)}, u32[]{:S(2)}, u32[]{:S(2)}) collective-permute-start(bf16[1,512,256]{2,1,0:T(8,128)(2,1)S(1)} %mix.15), channel_id=1, source_target_pairs={{0,8},{4,12},{8,0},{12,4},{16,24},{20,28},{24,16},{28,20},{1,9},{5... | collective-permute-start | bytes 786440 | tf_op jit(solution)/shard_map/ppermute | solution.py:227
  92.0 8.4 %collective-permute-start.11 = (bf16[512,128]{1,0:T(8,128)(2,1)S(1)}, bf16[512,128]{1,0:T(8,128)(2,1)S(1)}, u32[]{:S(2)}, u32[]{:S(2)}) collective-permute-start(bf16[512,128]{1,0:T(8,128)(2,1)S(1)} %add_up.4.refs_1_.refs_2_), channel_id=1, source_target_pairs={{0,4},{4,0},{8,12},{12,8},{16,20},{20,16},{24,28},{28,24},{1,5},{5... | collective-permute-start | bytes 393224 | tf_op jit(solution)/shard_map/ppermute | solution.py:227
  95.0 7.5 %collective-permute-start.12 = (bf16[512,128]{1,0:T(8,128)(2,1)S(1)}, bf16[512,128]{1,0:T(8,128)(2,1)S(1)}, u32[]{:S(2)}, u32[]{:S(2)}) collective-permute-start(bf16[512,128]{1,0:T(8,128)(2,1)S(1)} %collective-permute-done.10.refs_2_.refs_3_), channel_id=1, source_target_pairs={{0,4},{4,0},{8,12},{12,8},{16,20},{20,16},{24,28},{28,24},{1,5},{5... | collective-permute-start | bytes 393224 | tf_op jit(solution)/shard_map/ppermute | solution.py:227
  96.6 7.4 %collective-permute-start.31 = (bf16[1,512,128]{2,1,0:T(8,128)(2,1)S(1)}, bf16[1,512,128]{2,1,0:T(8,128)(2,1)S(1)}, u32[]{:S(2)}, u32[]{:S(2)}) collective-permute-start(bf16[1,512,128]{2,1,0:T(8,128)(2,1)S(1)} %mix.13), channel_id=1, source_target_pairs={{0,8},{4,12},{8,0},{12,4},{16,24},{20,28},{24,16},{28,20},{1,9},{5... | collective-permute-start | bytes 393224 | tf_op jit(solution)/shard_map/ppermute | solution.py:227
  97.8 8.0 %collective-permute-start.22 = (bf16[1,512,128]{2,1,0:T(8,128)(2,1)S(1)}, bf16[1,512,128]{2,1,0:T(8,128)(2,1)S(1)}, u32[]{:S(2)}, u32[]{:S(2)}) collective-permute-start(bf16[1,512,128]{2,1,0:T(8,128)(2,1)S(1)} %mix.11), channel_id=1, source_target_pairs={{0,8},{4,12},{8,0},{12,4},{16,24},{20,28},{24,16},{28,20},{1,9},{5... | collective-permute-start | bytes 393224 | tf_op jit(solution)/shard_map/ppermute | solution.py:227
  102.6 5.4 %collective-permute-start.13 = (bf16[1,512,128]{2,1,0:T(8,128)(2,1)S(1)}, bf16[1,512,128]{2,1,0:T(8,128)(2,1)S(1)}, u32[]{:S(2)}, u32[]{:S(2)}) collective-permute-start(bf16[1,512,128]{2,1,0:T(8,128)(2,1)S(1)} %mix.9), channel_id=1, source_target_pairs={{0,8},{4,12},{8,0},{12,4},{16,24},{20,28},{24,16},{28,20},{1,9},{5... | collective-permute-start | bytes 393224 | tf_op jit(solution)/shard_map/ppermute | solution.py:227
